TPU v7x, 32 devices: a whole 2x2x4 slice. The times are simulated.
32 devices in a mesh: section: 2 (over x), dp: 4 (over z), tensor: 4 (over y, core).
Axes of the slice: x: 2, y: 2, z: 4, core: 2. Of those that a mesh axis runs over, the one named last changes fastest.
Arguments:
- section_input: bfloat16 [2, 8192, 640], P(None, ('dp', 'tensor')), may hold values from -6 to 6
- cotangent: bfloat16 [2, 8192, 640], P(None, ('dp', 'tensor')), may hold values from -6 to 6
- segments: int32 [2, 8192], P(None, 'dp'), may hold values from 0 to 23, as said below
- query_weight: bfloat16 [2, 640, 1024], P('section', 'dp', 'tensor'), may hold values from -0.25 to 0.25
- key_weight: bfloat16 [2, 640, 256], P('section', 'dp'), may hold values from -0.25 to 0.25
- value_weight: bfloat16 [2, 640, 256], P('section', 'dp'), may hold values from -0.25 to 0.25
- output_weight: bfloat16 [2, 640, 1024], P('section', 'dp', 'tensor'), may hold values from -0.1875 to 0.1875
- gate_weight: bfloat16 [2, 640, 2048], P('section', 'dp', 'tensor'), may hold values from -0.25 to 0.25
- up_weight: bfloat16 [2, 640, 2048], P('section', 'dp', 'tensor'), may hold values from -0.25 to 0.25
- down_weight: bfloat16 [2, 640, 2048], P('section', 'dp', 'tensor'), may hold values from -0.125 to 0.125
- norm_gains: bfloat16 [2, 640, 4], P('section', 'dp'), may hold values from 0.5 to 1.5
- head_gains: bfloat16 [2, 256, 2], P('section', 'dp'), may hold values from 0.5 to 1.5
Outputs:
- section_output: float32 [2, 2, 8192, 640], P('section', None, ('dp', 'tensor'))
- input_grads: float32 [2, 2, 8192, 640], P('section', None, ('dp', 'tensor'))
- query_grad: float32 [2, 640, 1024], P('section', 'dp', 'tensor')
- key_grad: float32 [2, 640, 256], P('section', 'dp')
- value_grad: float32 [2, 640, 256], P('section', 'dp')
- output_grad: float32 [2, 640, 1024], P('section', 'dp', 'tensor')
- gate_grad: float32 [2, 640, 2048], P('section', 'dp', 'tensor')
- up_grad: float32 [2, 640, 2048], P('section', 'dp', 'tensor')
- down_grad: float32 [2, 640, 2048], P('section', 'dp', 'tensor')
- norm_gains_grad: float32 [2, 640, 4], P('section', 'dp')
- head_gains_grad: float32 [2, 256, 2], P('section', 'dp')
Inputs may be any that keep to these rules, and one draw needn't show every extreme that they name: `segments`: segment numbers never fall along a micro-batch's tokens, every sequence of 2048 tokens begins with a new one, and no segment crosses from one sequence to the next.
All inputs are finite; a program needn't handle non-finite values.
Results may differ from a plain program's by a relative error of at most 0.029.
Values may be sent and summed in bfloat16 or wider, within the bound.
No kernel may reach another device: no remote copies, remote signals or barrier semaphores. Data moves between devices by JAX's collectives and lax.ppermute only.
A program may use at most 256 MiB of HBM per device.

v0:
```python
import functools

import jax
import jax.numpy as jnp
from jax import lax
from jax.experimental import pallas as pl
from jax.experimental.pallas import tpu as pltpu
from jax.sharding import PartitionSpec as P

HD = 256
HALF = HD // 2
WIN = 512
BLK = 256
EPS = 1e-06
F32 = jnp.float32
BF16 = jnp.bfloat16
LIMIT = 50 * 1024 * 1024


def nn(a, b):
    return lax.dot_general(a, b, (((1,), (0,)), ((), ())), preferred_element_type=F32)


def nt(a, b):
    return lax.dot_general(a, b, (((1,), (1,)), ((), ())), preferred_element_type=F32)


def tn(a, b):
    return lax.dot_general(a, b, (((0,), (0,)), ((), ())), preferred_element_type=F32)


def rms(values, gain):
    return values * lax.rsqrt(jnp.mean(values * values, axis=-1, keepdims=True) + EPS) * gain


def rms_back(grad, values, gain):
    scale = lax.rsqrt(jnp.mean(values * values, axis=-1, keepdims=True) + EPS)
    unit = values * scale
    scaled = grad * gain
    inner = jnp.mean(scaled * unit, axis=-1, keepdims=True)
    return scale * (scaled - unit * inner), jnp.sum(grad * unit, axis=0, keepdims=True)


def rot(values, cosine, sine):
    a, b = values[:, :HALF], values[:, HALF:]
    return jnp.concatenate([a * cosine - b * sine, b * cosine + a * sine], axis=-1)


def rot_back(grad, cosine, sine):
    a, b = grad[:, :HALF], grad[:, HALF:]
    return jnp.concatenate([a * cosine + b * sine, b * cosine - a * sine], axis=-1)


GELU_A = 0.7978845608028654
GELU_B = 0.044715


def triangle():
    row = lax.broadcasted_iota(jnp.int32, (BLK, BLK), 0)
    column = lax.broadcasted_iota(jnp.int32, (BLK, BLK), 1)
    return column <= row


def tiles(block):
    rows = slice(block * BLK, (block + 1) * BLK)
    other = slice((1 - block) * BLK, (2 - block) * BLK)
    return rows, other, block == 1


def masks(block, lower, seg_col, seg_own, seg_prev):
    rows, other, own = tiles(block)
    mine = seg_col[rows, :]
    diagonal = mine == jnp.where(lower, seg_own[:, rows], seg_prev[:, rows])
    rest = mine == (seg_own if own else seg_prev)[:, other]
    return diagonal, rest


def stream(step, choice, own, other, held, arrived):
    def spot(index, part):
        if len(held.shape) == 4:
            return held.at[index, part]
        columns = held.shape[4] // 2
        return held.at[index, 0, :, :, pl.ds(part * columns, columns)]

    def fetch(index):
        for wanted, slots in ((1, own), (0, other)):

            @pl.when(choice[0] == wanted)
            def _(slots=slots):
                for part, ref in enumerate(slots[index]):
                    pltpu.make_async_copy(
                        ref, spot(index % 2, part), arrived.at[index % 2, part]
                    ).start()

    @pl.when(step == 0)
    def _():
        fetch(0)

    for index in range(1, len(own)):

        @pl.when(step == index - 1)
        def _(index=index):
            fetch(index)

    now = lax.rem(step, 2)
    for part, ref in enumerate(own[0]):
        pltpu.make_async_copy(ref, spot(now, part), arrived.at[now, part]).wait()
    return now


def assemble_kernel(cuts, place, *refs):
    count = (len(refs) - len(cuts) - 1)
    pieces, outs, done = refs[:count], refs[count:-1], refs[-1]
    copies = []
    for shift, piece in enumerate(pieces):
        owner = lax.rem(place[0] + count - shift, count)
        for cut, (start, rows) in enumerate(cuts):
            at = pl.ds(pl.multiple_of(owner * rows, rows), rows)
            lead = (slice(None),) * (len(piece.shape) - 2)
            copies.append(
                pltpu.make_async_copy(
                    piece.at[lead + (pl.ds(start, rows),)],
                    outs[cut].at[lead + (at,)],
                    done.at[shift, cut],
                )
            )
    for copy in copies:
        copy.start()
    for copy in copies:
        copy.wait()


def prep_kernel(x, gains, heads, kvw, cosine, sine, normed, kraw, kv):
    rows = rms(x[...].astype(F32), gains[0:1, :]).astype(BF16)
    normed[...] = rows
    raw = nn(rows, kvw[:, :HD])
    kraw[...] = raw
    kv[:, :HD] = rot(rms(raw, heads[1:2, :]), cosine[...], sine[...]).astype(BF16)
    kv[:, HD:] = nn(rows, kvw[:, HD : 2 * HD]).astype(BF16)


def flat(tile):
    return tile.reshape(-1, tile.shape[-1])


def tall(tile):
    return tile.reshape(2, -1, tile.shape[-1])


def attend_kernel(
    choice, x, normed, gains, heads, own, prev, cosine, sine, seg_col, seg_own, seg_prev,
    qo_a, qo_b, qo_c, qo_d, qraw, q, mixed, lse, branch, middle, normed_two, held, arrived,
):
    step = pl.program_id(0)
    slots = [[qo_a, qo_b], [qo_c, qo_d]]
    now = stream(step, choice, slots, slots, held, arrived)
    for head in range(2):
        raw = nn(normed[...], held[now, head, :, :HD])
        qraw[head] = raw
        turned = rot(rms(raw, heads[0:1, :]), cosine[...], sine[...]).astype(BF16)
        q[head] = turned * jnp.asarray(0.0625, BF16)
    lower = triangle()
    for block in range(2):
        rows, other, is_own = tiles(block)
        diagonal, rest = masks(block, lower, seg_col[...], seg_own[...], seg_prev[...])
        query = flat(q[:, rows, :])
        far = own if is_own else prev
        near_scores = jnp.where(
            lower, tall(nt(query, own[rows, :HD])), tall(nt(query, prev[rows, :HD]))
        )
        near_scores = jnp.where(diagonal, near_scores, -1e30)
        far_scores = jnp.where(rest, tall(nt(query, far[other, :HD])), -1e30)
        largest = jnp.maximum(
            jnp.max(near_scores, axis=-1, keepdims=True),
            jnp.max(far_scores, axis=-1, keepdims=True),
        )
        near = jnp.exp(near_scores - largest)
        rest_p = jnp.exp(far_scores - largest)
        total = jnp.sum(near, axis=-1, keepdims=True) + jnp.sum(rest_p, axis=-1, keepdims=True)
        inverse = 1.0 / total
        near = near * inverse
        rest_p = (rest_p * inverse).astype(BF16)
        near_own = jnp.where(lower, near, 0.0).astype(BF16)
        near_prev = jnp.where(lower, 0.0, near).astype(BF16)
        mixed[:, rows, :] = tall(
            nn(flat(near_own), own[rows, HD:])
            + nn(flat(near_prev), prev[rows, HD:])
            + nn(flat(rest_p), far[other, HD:])
        ).astype(BF16)
        lse[:, rows, :] = largest + jnp.log(total)
    part = nt(mixed[0], held[now, 0, :, HD:]) + nt(mixed[1], held[now, 1, :, HD:])

    @pl.when(step == 0)
    def _():
        branch[...] = part

    @pl.when(step > 0)
    def _():
        branch[...] += part

    @pl.when(step == pl.num_programs(0) - 1)
    def _():
        mid = x[...].astype(F32) + rms(branch[...], gains[1:2, :])
        middle[...] = mid
        normed_two[...] = rms(mid, gains[2:3, :]).astype(BF16)


def slots_of(refs):
    halves = [[refs[at], refs[at + 1]] for at in range(0, len(refs), 2)]
    return halves[: len(halves) // 2], halves[len(halves) // 2 :]


def feed_kernel(choice, normed_two, middle, gains, *refs):
    own, other = slots_of(refs[:16])
    gate_out, up_out, branch_two, out, out_low, held, arrived = refs[16:]
    step = pl.program_id(0)
    now = stream(step, choice, own, other, held, arrived)
    rows = normed_two[...]
    gate = nn(rows, held[now, 0, 0])
    upward = nn(rows, held[now, 0, 1])
    gate_out[0] = gate.astype(BF16)
    up_out[0] = upward.astype(BF16)
    wave = jnp.tanh(GELU_A * gate * (1.0 + GELU_B * gate * gate))
    hidden = (0.5 * gate * (1.0 + wave) * upward).astype(BF16)
    part = nt(hidden, held[now, 0, 2])

    @pl.when(step == 0)
    def _():
        branch_two[...] = part

    @pl.when(step > 0)
    def _():
        branch_two[...] += part

    @pl.when(step == pl.num_programs(0) - 1)
    def _():
        total = middle[...] + rms(branch_two[...], gains[3:4, :])
        out[...] = total
        out_low[...] = total.astype(BF16)


def feed_back_kernel(
    choice, grad, branch_two, middle, branch, normed_two, gains, gate_in, up_in, *refs
):
    own, other = slots_of(refs[:16])
    send, keep, grad_middle, grad_branch, gain_grads = refs[16:21]
    incoming, incoming_t, rows_t, total, held, arrived = refs[21:]
    step = pl.program_id(0)
    now = stream(step, choice, own, other, held, arrived)

    @pl.when(step == 0)
    def _():
        values, gain = rms_back(grad[...].astype(F32), branch_two[...], gains[3:4, :])
        incoming[...] = values.astype(BF16)
        incoming_t[...] = values.T.astype(BF16)
        rows_t[...] = normed_two[...].T
        gain_grads[2:3, :] = gain
        gain_grads[3:4, :] = jnp.zeros_like(gain)

    gate = gate_in[0].astype(F32)
    upward = up_in[0].astype(F32)
    square = gate * gate
    wave = jnp.tanh(GELU_A * gate * (1.0 + GELU_B * square))
    bell = 0.5 * (1.0 + wave)
    active = gate * bell
    slope = bell + gate * (1.0 - wave * wave) * (0.5 * GELU_A * (1.0 + 3.0 * GELU_B * square))
    grad_hidden = nn(incoming[...], held[now, 0, 2])
    grad_up = (grad_hidden * active).astype(BF16)
    grad_gate = (grad_hidden * upward * slope).astype(BF16)
    hidden = (active * upward).astype(BF16)
    columns = hidden.shape[1] // 2

    def store(place):
        for number, (left, right) in enumerate(
            ((rows_t, grad_gate), (rows_t, grad_up), (incoming_t, hidden))
        ):
            value = nn(left[...], right).astype(BF16)
            place[0, 0, number] = value[:, :columns]
            place[0, 1, number] = value[:, columns:]

    @pl.when(step < 2)
    def _():
        store(send)

    @pl.when(step >= 2)
    def _():
        store(keep)

    part = nt(grad_gate, held[now, 0, 0]) + nt(grad_up, held[now, 0, 1])

    @pl.when(step == 0)
    def _():
        total[...] = part

    @pl.when(step > 0)
    def _():
        total[...] += part

    @pl.when(step == pl.num_programs(0) - 1)
    def _():
        from_norm, gain = rms_back(total[...], middle[...], gains[2:3, :])
        gain_grads[1:2, :] = gain
        mid = grad[...].astype(F32) + from_norm
        grad_middle[...] = mid
        values, gain = rms_back(mid, branch[...], gains[1:2, :])
        gain_grads[0:1, :] = gain
        grad_branch[...] = values.astype(BF16)


def attend_back_kernel(
    choice, grad_branch, normed, heads, q, qraw, mixed, lse, own, prev, cosine, sine,
    seg_col, seg_own, seg_prev, qo_a, qo_b, qo_c, qo_d,
    send, keep, kv_own, kv_prev, grad_normed, head_grad, grad_t, rows_t, prev_sum, grad_q,
    held, arrived, mixed_g, raw_g,
):
    step = pl.program_id(0)
    slots = [[qo_a, qo_b], [qo_c, qo_d]]
    now = stream(step, choice, slots, slots, held, arrived)

    @pl.when(step == 0)
    def _():
        grad_t[...] = grad_branch[...].T
        rows_t[...] = normed[...].T
        kv_own[...] = jnp.zeros_like(kv_own)
        prev_sum[...] = jnp.zeros_like(prev_sum)
        grad_normed[...] = jnp.zeros_like(grad_normed)
        head_grad[...] = jnp.zeros_like(head_grad)

    for head in range(2):
        mixed_g[head] = nn(grad_branch[...], held[now, head, :, HD:]).astype(BF16)
    lower = triangle()
    for block in range(2):
        rows, other, is_own = tiles(block)
        diagonal, rest = masks(block, lower, seg_col[...], seg_own[...], seg_prev[...])
        query = flat(q[:, rows, :])
        incoming = flat(mixed_g[:, rows, :])
        far = own if is_own else prev
        far_sum = kv_own if is_own else prev_sum
        log_total = lse[:, rows, :]
        near_scores = jnp.where(
            lower, tall(nt(query, own[rows, :HD])), tall(nt(query, prev[rows, :HD]))
        )
        near = jnp.exp(jnp.where(diagonal, near_scores, -1e30) - log_total)
        rest_p = jnp.exp(jnp.where(rest, tall(nt(query, far[other, :HD])), -1e30) - log_total)
        near_grad = jnp.where(
            lower, tall(nt(incoming, own[rows, HD:])), tall(nt(incoming, prev[rows, HD:]))
        )
        rest_grad = tall(nt(incoming, far[other, HD:]))
        inner = jnp.sum(near * near_grad, axis=-1, keepdims=True) + jnp.sum(
            rest_p * rest_grad, axis=-1, keepdims=True
        )
        near_score = near * (near_grad - inner)
        rest_score = flat(rest_p * (rest_grad - inner)).astype(BF16)
        score_own = flat(jnp.where(lower, near_score, 0.0)).astype(BF16)
        score_prev = flat(jnp.where(lower, 0.0, near_score)).astype(BF16)
        near_own = flat(jnp.where(lower, near, 0.0)).astype(BF16)
        near_prev = flat(jnp.where(lower, 0.0, near)).astype(BF16)
        rest_p = flat(rest_p).astype(BF16)
        grad_q[:, rows, :] = tall(
            0.0625
            * (
                nn(score_own, own[rows, :HD])
                + nn(score_prev, prev[rows, :HD])
                + nn(rest_score, far[other, :HD])
            )
        )
        kv_own[rows, :HD] += tn(score_own, query)
        prev_sum[rows, :HD] += tn(score_prev, query)
        far_sum[other, :HD] += tn(rest_score, query)
        kv_own[rows, HD:] += tn(near_own, incoming)
        prev_sum[rows, HD:] += tn(near_prev, incoming)
        far_sum[other, HD:] += tn(rest_p, incoming)
    for head in range(2):
        values, gain = rms_back(
            rot_back(grad_q[head], cosine[...], sine[...]), qraw[head], heads[0:1, :]
        )
        head_grad[0:1, :] += gain
        raw_g[head] = values.astype(BF16)
        grad_normed[...] += nt(raw_g[head], held[now, head, :, :HD])

    def store(place):
        for head in range(2):
            place[head, :, :HD] = nn(rows_t[...], raw_g[head]).astype(BF16)
            place[head, :, HD:] = nn(grad_t[...], mixed[head]).astype(BF16)

    @pl.when(step == 0)
    def _():
        store(send)

    @pl.when(step == 1)
    def _():
        store(keep)

    @pl.when(step == pl.num_programs(0) - 1)
    def _():
        kv_prev[...] = prev_sum[...].astype(BF16)


def finish_kernel(
    kv_own, kv_next, kraw, normed, kvw, heads, gains, x, grad_normed, grad_middle, cosine, sine,
    kv_grad, grad_x, grad_low, gain_grad, head_grad,
):
    summed = kv_own[...] + kv_next[...].astype(F32)
    values, gain = rms_back(
        rot_back(summed[:, :HD], cosine[...], sine[...]), kraw[...], heads[1:2, :]
    )
    head_grad[...] = gain
    grad_key = values.astype(BF16)
    grad_value = summed[:, HD:].astype(BF16)
    rows = normed[...]
    kv_grad[:, :HD] = tn(rows, grad_key).astype(BF16)
    kv_grad[:, HD:] = tn(rows, grad_value).astype(BF16)
    from_all = grad_normed[...] + nt(grad_key, kvw[:, :HD]) + nt(grad_value, kvw[:, HD : 2 * HD])
    from_norm, gain = rms_back(from_all, x[...].astype(F32), gains[0:1, :])
    gain_grad[...] = gain
    total = grad_middle[...] + from_norm
    grad_x[...] = total
    grad_low[...] = total.astype(BF16)


def whole(shape):
    zeros = (0,) * len(shape)
    return pl.BlockSpec(shape, lambda *at: zeros)


def anywhere(shape):
    return pl.BlockSpec(memory_space=pl.ANY)


def fetched(shape):
    return pl.BlockSpec(memory_space=pltpu.HBM)


def scalars(shape):
    return pl.BlockSpec(memory_space=pltpu.SMEM)


def slot(shape):
    zeros = (0,) * (len(shape) - 1)
    return pl.BlockSpec((1,) + tuple(shape[1:]), lambda at: (at,) + zeros)


def pair(shape):
    zeros = (0,) * (len(shape) - 1)
    return pl.BlockSpec((2,) + tuple(shape[1:]), lambda at: (at,) + zeros)


def early(shape):
    zeros = (0,) * (len(shape) - 1)
    return pl.BlockSpec((1,) + tuple(shape[1:]), lambda at: (jnp.minimum(at, 1),) + zeros)


def late(shape):
    zeros = (0,) * (len(shape) - 1)
    return pl.BlockSpec((1,) + tuple(shape[1:]), lambda at: (jnp.maximum(at - 2, 0),) + zeros)


def run(kernel, grid, ins, outs, scratch=(), micros=2):
    arrays = [a for a, _ in ins]
    return pl.pallas_call(
        kernel,
        grid=grid,
        in_specs=[spec(a.shape) for a, spec in ins],
        out_specs=[spec(shape) for shape, _, spec in outs],
        out_shape=[jax.ShapeDtypeStruct(shape, kind) for shape, kind, _ in outs],
        scratch_shapes=list(scratch),
        compiler_params=pltpu.CompilerParams(vmem_limit_bytes=LIMIT),
        cost_estimate=pl.CostEstimate(
            flops=micros * 1153000000, bytes_accessed=1, transcendentals=0
        ),
    )(*arrays)


def qo_scratch(width):
    return [pltpu.VMEM((2, 2, width, 2 * HD), BF16), pltpu.SemaphoreType.DMA((2, 2))]


def ff_scratch(width, units):
    return [pltpu.VMEM((2, 1, 3, width, 2 * units), BF16), pltpu.SemaphoreType.DMA((2, 2))]


def forward_keys(x, small, common):
    cosine, sine = common[:2]
    kvw, gains, heads = small
    rows, width = x.shape
    normed, kraw, kv = run(
        prep_kernel, (1,),
        [(x, whole), (gains, whole), (heads, whole), (kvw, whole), (cosine, whole), (sine, whole)],
        [((rows, width), BF16, whole), ((rows, HD), F32, whole), ((rows, 2 * HD), BF16, whole)],
        micros=2,
    )
    return normed, kraw, kv


def halo_on(kv):
    return lax.ppermute(kv, "tensor", [(i, i + 1) for i in range(lax.axis_size("tensor") - 1)])


def forward_attend(x, keys, small, choice, qo, common):
    cosine, sine, seg_col, seg_own, seg_prev = common
    kvw, gains, heads = small
    normed, kraw, kv, prev = keys
    rows, width = x.shape
    slots = len(qo)
    return run(
        attend_kernel, (slots // 2,),
        [(choice, scalars), (x, whole), (normed, whole), (gains, whole), (heads, whole),
         (kv, whole), (prev, whole), (cosine, whole), (sine, whole), (seg_col, whole),
         (seg_own, whole), (seg_prev, whole)] + [(part, fetched) for part in qo],
        [((slots, rows, HD), F32, pair), ((slots, rows, HD), BF16, pair),
         ((slots, rows, HD), BF16, pair), ((slots, rows, 1), F32, pair),
         ((rows, width), F32, whole), ((rows, width), F32, whole), ((rows, width), BF16, whole)],
        qo_scratch(width),
        micros=14,
    )


def forward_feed(attended, small, choice, ff):
    gains = small[1]
    middle, normed_two = attended[5:]
    rows, width = middle.shape
    slots, units = len(ff) // 4, ff[0].shape[2]
    return run(
        feed_kernel, (slots,),
        [(choice, scalars), (normed_two, whole), (middle, whole), (gains, whole)]
        + [(part, fetched) for part in ff],
        [((slots, rows, 2 * units), BF16, slot), ((slots, rows, 2 * units), BF16, slot),
         ((rows, width), F32, whole), ((rows, width), F32, whole), ((rows, width), BF16, whole)],
        ff_scratch(width, units),
        micros=12,
    )


def backward_feed(grad, branch, middle, normed_two, fed, small, choice, ff):
    gains = small[1]
    gate, upward, branch_two = fed[:3]
    rows, width = middle.shape
    slots, units = len(ff) // 4, ff[0].shape[2]
    half = slots // 2
    return run(
        feed_back_kernel, (slots,),
        [(choice, scalars), (grad, whole), (branch_two, whole), (middle, whole), (branch, whole),
         (normed_two, whole), (gains, whole), (gate, slot), (upward, slot)]
        + [(part, fetched) for part in ff],
        [((half, 2, 3, width, units), BF16, early), ((half, 2, 3, width, units), BF16, late),
         ((rows, width), F32, whole), ((rows, width), BF16, whole), ((4, width), F32, whole)],
        [pltpu.VMEM((rows, width), BF16), pltpu.VMEM((width, rows), BF16),
         pltpu.VMEM((width, rows), BF16), pltpu.VMEM((rows, width), F32)]
        + ff_scratch(width, units),
        micros=25,
    )


def backward_attend(grad_branch, keys, attended, small, choice, qo, common):
    cosine, sine, seg_col, seg_own, seg_prev = common
    heads = small[2]
    normed, kraw, kv, prev = keys
    qraw, q, mixed, lse = attended[:4]
    rows, width = normed.shape
    slots = len(qo)
    half = slots // 2
    return run(
        attend_back_kernel, (slots // 2,),
        [(choice, scalars), (grad_branch, whole), (normed, whole), (heads, whole), (q, pair),
         (qraw, pair), (mixed, pair), (lse, pair), (kv, whole), (prev, whole), (cosine, whole),
         (sine, whole), (seg_col, whole), (seg_own, whole), (seg_prev, whole)]
        + [(part, fetched) for part in qo],
        [((half, width, 2 * HD), BF16, whole), ((half, width, 2 * HD), BF16, whole),
         ((rows, 2 * HD), F32, whole), ((rows, 2 * HD), BF16, whole), ((rows, width), F32, whole),
         ((1, HD), F32, whole)],
        [pltpu.VMEM((width, rows), BF16), pltpu.VMEM((width, rows), BF16),
         pltpu.VMEM((rows, 2 * HD), F32), pltpu.VMEM((2, rows, HD), F32)] + qo_scratch(width)
        + [pltpu.VMEM((2, rows, HD), BF16)] * 2,
        micros=17,
    )


def backward_keys(x, kv_own, kv_next, keys, small, grad_normed, grad_middle, common):
    cosine, sine = common[:2]
    kvw, gains, heads = small
    normed, kraw = keys[:2]
    rows, width = x.shape
    return run(
        finish_kernel, (1,),
        [(kv_own, whole), (kv_next, whole), (kraw, whole), (normed, whole), (kvw, whole),
         (heads, whole), (gains, whole), (x, whole), (grad_normed, whole), (grad_middle, whole),
         (cosine, whole), (sine, whole)],
        [((width, 2 * HD), BF16, whole), ((rows, width), F32, whole), ((rows, width), BF16, whole),
         ((1, width), F32, whole),
         ((1, HD), F32, whole)],
        micros=5,
    )


def halo_back(kv_prev):
    return lax.ppermute(
        kv_prev, "tensor", [(i + 1, i) for i in range(lax.axis_size("tensor") - 1)]
    )


def tensor_pairs(bit):
    return [(i, i ^ bit) for i in range(lax.axis_size("tensor"))]


def rows_over_dp(part, cuts):
    count = lax.axis_size("dp")
    lead, columns = part.shape[:-2], part.shape[-1]
    if count > 4:
        full = jnp.moveaxis(lax.all_gather(part, "dp", axis=0), 0, -3)
        return [
            full[..., start : start + rows, :].reshape(lead + (count * rows, columns))
            for start, rows in cuts
        ]
    pieces = [part] + [
        lax.ppermute(part, "dp", [(i, (i + shift) % count) for i in range(count)])
        for shift in range(1, count)
    ]
    place = lax.axis_index("dp").astype(jnp.int32).reshape(1)
    return run(
        functools.partial(assemble_kernel, cuts), (),
        [(place, scalars)] + [(piece, anywhere) for piece in pieces],
        [(lead + (count * rows, columns), part.dtype, anywhere) for _, rows in cuts],
        [pltpu.SemaphoreType.DMA((count, len(cuts)))],
    )


def across_tensor(part):
    return lax.ppermute(part, "tensor", tensor_pairs(2))


def beside_tensor(part):
    return lax.ppermute(part, "tensor", tensor_pairs(1))


def across_section(part):
    return lax.ppermute(part, "section", [(0, 1), (1, 0)])


def after(values, *others):
    return lax.optimization_barrier((values, others))[0]


def add(left, right):
    return (left.astype(F32) + right.astype(F32)).astype(BF16)


def summed_over_dp(parts):
    count = lax.axis_size("dp")
    if count > 4:
        return [
            lax.psum_scatter(part, "dp", scatter_dimension=1, tiled=True) for part in parts
        ]
    me = lax.axis_index("dp")
    shapes = [(part.shape[0], part.shape[1] // count, part.shape[2]) for part in parts]

    def share(owner):
        blocks = [
            lax.dynamic_slice_in_dim(part, owner % count * shape[1], shape[1], 1)
            for part, shape in zip(parts, shapes)
        ]
        return jnp.concatenate([block.reshape(-1, block.shape[2]) for block in blocks])

    total = share(me).astype(F32)
    pieces = [
        lax.ppermute(share(me + shift), "dp", [(i, (i + shift) % count) for i in range(count)])
        for shift in range(1, count)
    ]
    for piece in pieces:
        total += piece.astype(F32)
    total, sums, start = total.astype(BF16), [], 0
    for shape in shapes:
        size = shape[0] * shape[1]
        sums.append(total[start : start + size].reshape(shape))
        start += size
    return sums


def side_by_side(part):
    return jnp.concatenate([part[..., :HD], part[..., HD:]])


def joined(part):
    half = part.shape[0] // 2
    return jnp.concatenate([part[:half], part[half:]], axis=-1)


def kept_sums(arrived, keep, half=None):
    if half is not None:
        arrived, keep = arrived[:, half], keep[:, half]
    return add(keep[1], arrived[1]), add(keep[0], arrived[0])


def pack_shared(kv_grad, gain_rows, head_rows):
    count = lax.axis_size("dp")
    width, columns = kv_grad.shape

    def shares(rows):
        parts = jnp.swapaxes(rows.reshape(rows.shape[0], count, -1), 0, 1)
        return jnp.pad(parts, ((0, 0), (0, 0), (0, columns - parts.shape[2])))

    small = jnp.concatenate([shares(gain_rows), shares(head_rows)], axis=1).astype(BF16)
    small = jnp.pad(small, ((0, 0), (0, 10), (0, 0)))
    return jnp.concatenate([kv_grad.reshape(count, -1, columns), small], axis=1).reshape(
        1, -1, columns
    )


def core_half(packed):
    count = lax.axis_size("dp")
    columns = packed.shape[-1]
    halves = packed.reshape(count, 2, -1, columns)
    mine = lax.axis_index("tensor") % 2

    def half(at):
        return lax.dynamic_index_in_dim(halves, at, 1, keepdims=False).reshape(1, -1, columns)

    return add(half(mine), beside_tensor(half(1 - mine)))


def body(
    section_input, cotangent, segments, query_weight, key_weight, value_weight, output_weight,
    gate_weight, up_weight, down_weight, norm_gains, head_gains,
):
    section = lax.axis_index("section")
    place = lax.axis_index("tensor")
    first = section == 0
    rows = section_input.shape[1]
    per_head = head_gains.shape[1]
    local = norm_gains.shape[1]

    gain_rows = norm_gains[0].T
    head_rows = jnp.pad(head_gains[0].T, ((0, 0), (0, local - per_head)))
    small = jnp.pad(jnp.concatenate([gain_rows, head_rows]), ((0, 10), (0, 2 * HD - local)))
    shared = jnp.concatenate(
        [
            jnp.concatenate([query_weight[0], output_weight[0]], axis=1),
            lax.dynamic_slice_in_dim(
                jnp.concatenate([key_weight[0], value_weight[0]], axis=1),
                place % 2 * (local // 2), local // 2, 0,
            ),
            small,
        ]
    )
    cuts = ((0, local), (local, local // 2), (local + local // 2, 16))
    units = gate_weight.shape[2] // 2
    feeds = [
        jnp.stack([w[0, :, half * units : (half + 1) * units]
                   for w in (gate_weight, up_weight, down_weight)])
        for half in range(2)
    ]
    other = across_section(shared)
    own_segments = lax.dynamic_index_in_dim(segments, section, 0, keepdims=False)
    length = own_segments.shape[0]
    places = jnp.arange(length, dtype=jnp.int32)
    before = jnp.concatenate([own_segments[:1] - 1, own_segments[:-1]])
    starts = lax.cummax(jnp.where(own_segments != before, places, 0), axis=0)
    positions = lax.dynamic_slice_in_dim(places - starts, place * rows, rows, 0)
    inverse = jnp.exp(-jnp.log(10000.0) * jnp.arange(HALF, dtype=F32) / HALF)
    angle = positions.astype(F32)[:, None] * inverse[None, :]
    here = lax.dynamic_slice_in_dim(own_segments, place * rows, rows, 0)
    padded = jnp.concatenate([jnp.full((rows,), -1, jnp.int32), own_segments])
    prior = lax.dynamic_slice_in_dim(padded, place * rows, rows, 0)
    common = (jnp.cos(angle), jnp.sin(angle), here[:, None], here[None, :], prior[None, :])

    x0 = lax.dynamic_index_in_dim(section_input, section, 0, keepdims=False)
    grad = lax.dynamic_index_in_dim(cotangent, section, 0, keepdims=False)
    count = lax.axis_size("dp")

    def small_of(gathered):
        rows = gathered[2].reshape(count, 16, 2 * HD).astype(F32)
        gains = jnp.swapaxes(rows[:, :4, :local], 0, 1).reshape(4, count * local)
        heads = jnp.swapaxes(rows[:, 4:6, :per_head], 0, 1).reshape(2, HD)
        mine, other = gathered[1], beside_tensor(gathered[1])
        halves = [jnp.where(place % 2 == at, mine, other) for at in range(2)]
        halves = [half.reshape(count, 1, -1, 2 * HD) for half in halves]
        return jnp.concatenate(halves, axis=1).reshape(-1, 2 * HD), gains, heads

    choices = [(section == layer).astype(jnp.int32).reshape(1) for layer in range(2)]
    shared_l = [jnp.where(first, shared, other), jnp.where(first, other, shared)]

    whole_cut = ((0, local),)
    gathered0 = rows_over_dp(shared_l[0], cuts)
    feed_in, qo_mine, kvw0, rows0, x0 = after((feeds[0], *gathered0, x0))
    qo_across = across_tensor(qo_mine)
    feed_a = rows_over_dp(feed_in, whole_cut)[0]
    small0 = small_of((qo_mine, kvw0, rows0))
    feed_a, feed_in, qo_across, small0 = after((feed_a, feeds[1], qo_across, small0))
    keys0 = forward_keys(x0, small0, common)
    other_a, mine_a = across_section(feed_a), across_tensor(feed_a)
    feed_b = rows_over_dp(feed_in, whole_cut)[0]
    prev0 = halo_on(keys0[2])
    other_a, mine_a, feed_b = after((other_a, mine_a, feed_b))
    qo0 = [beside_tensor(qo_mine), beside_tensor(qo_across), qo_mine, qo_across]
    other_b, mine_b = across_section(feed_b), across_tensor(feed_b)
    keys0 = (*keys0, prev0)
    qo0, keys0 = after((qo0, keys0))
    beside_a = [beside_tensor(part) for part in (feed_a, mine_a, other_a)]
    attended0 = forward_attend(x0, keys0, small0, choices[0], qo0, common)
    other_a, other_b, mine_b, beside_a, attended0, shared1 = after(
        (other_a, other_b, mine_b, beside_a, attended0, shared_l[1])
    )
    far_a, far_b = across_tensor(other_a), across_section(mine_b)
    gathered1 = rows_over_dp(shared1, cuts)
    far_a, far_b, mine_b, other_b, gathered1 = after((far_a, far_b, mine_b, other_b, gathered1))
    beside_b = [beside_tensor(part) for part in (feed_b, mine_b, other_b)]
    beside_far = [beside_tensor(far_a), beside_tensor(far_b)]
    small1 = small_of(gathered1)
    qo_mine1, beside_b, beside_far = after((gathered1[0], beside_b, beside_far))
    ff = [beside_a[0], beside_b[0], beside_a[1], beside_b[1], feed_a, feed_b, mine_a, mine_b,
          beside_a[2], beside_b[2], *beside_far, other_a, other_b, far_a, far_b]
    qo_across1 = across_tensor(qo_mine1)
    fed0 = forward_feed(attended0, small0, choices[0], ff)
    out0, x1 = fed0[3:]
    keys1 = forward_keys(x1, small1, common)
    keys1, qo_across1 = after((keys1, qo_across1))
    prev1 = halo_on(keys1[2])
    qo1 = [beside_tensor(qo_mine1), beside_tensor(qo_across1), qo_mine1, qo_across1]
    x1, prev1, qo1 = after((x1, prev1, qo1))
    keys1 = (*keys1, prev1)
    attended1 = forward_attend(x1, keys1, small1, choices[1], qo1, common)
    fed1 = forward_feed(attended1, small1, choices[1], ff)
    out1, out1_low = fed1[3:]

    def packed(kv, gain, key, fed, at):
        return pack_shared(
            kv, jnp.concatenate([gain, fed[4][:3]]), jnp.concatenate([at[5], key])
        )

    out_got = across_section(jnp.where(first, out1_low, x1))
    ff1 = backward_feed(grad, *attended1[4:], fed1, small1, choices[1], ff)
    ff1, out_got = after((ff1, out_got))
    ff1_core = beside_tensor(ff1[0])
    at1 = backward_attend(ff1[3], keys1, attended1, small1, choices[1], qo1, common)
    at1, ff1_core = after((at1, ff1_core))
    next1 = halo_back(at1[3])
    qo1_core = beside_tensor(at1[0])
    sums1 = [kept_sums(ff1_core, ff1[1], half) for half in range(2)]
    next1, qo1_core, sums1 = after((next1, qo1_core, sums1))
    across1a = across_tensor(sums1[0][0])
    kv1, grad1, grad1_low, gain1, key1 = backward_keys(
        x1, at1[2], next1, keys1, small1, at1[4], ff1[2], common
    )
    ff0 = backward_feed(grad1_low, *attended0[4:], fed0, small0, choices[0], ff)
    across1a, ff0, sums1, qo1_core = after((across1a, ff0, sums1, qo1_core))
    ff0_core = beside_tensor(ff0[0])
    across1b = across_tensor(sums1[1][0])
    at0 = backward_attend(ff0[3], keys0, attended0, small0, choices[0], qo0, common)
    pair1 = kept_sums(qo1_core, at1[1])
    at0, ff0_core, across1b, pair1, kv1 = after((at0, ff0_core, across1b, pair1, kv1))
    pair1_across = across_tensor(pair1[0])
    rest1 = core_half(packed(kv1, gain1, key1, ff1, at1))[0]
    next0 = halo_back(at0[3])
    qo0_core = beside_tensor(at0[0])
    sums0 = [kept_sums(ff0_core, ff0[1], half) for half in range(2)]
    across0a = across_tensor(sums0[0][0])
    kv0, grad0, grad0_low, gain0, key0 = backward_keys(
        x0, at0[2], next0, keys0, small0, at0[4], ff0[2], common
    )
    grad_got = across_section(jnp.where(first, grad1_low, grad0_low))
    pair0 = kept_sums(qo0_core, at0[1])
    rest0 = core_half(packed(kv0, gain0, key0, ff0, at0))[0]
    full1 = [add(sums1[0][1], across1a), add(sums1[1][1], across1b)]
    pair1 = add(pair1[1], pair1_across)
    across0a, rest0, rest1, pair0, pair1, sums0, full1, grad_got = after(
        (across0a, rest0, rest1, pair0, pair1, sums0, full1, grad_got)
    )

    def swapped(zero, one):
        return add(jnp.where(first, zero, one), across_section(jnp.where(first, one, zero)))

    across0b = across_tensor(sums0[1][0])
    feed_a = swapped(add(sums0[0][1], across0a), full1[0])
    low0 = jnp.concatenate([pair0[0], rest0, rest1])
    across0b, feed_a, low0, sums0 = after((across0b, feed_a, low0, sums0))
    low0_across = across_tensor(low0)
    feed_b = swapped(add(sums0[1][1], across0b), full1[1])
    feed_a = summed_over_dp([feed_a])[0]
    low0_across, feed_a, feed_b = after((low0_across, feed_a, feed_b))
    size = low0.shape[0] - rest1.shape[0]
    low = swapped(
        add(jnp.concatenate([pair0[1], rest0]), low0_across[:size]),
        jnp.concatenate([pair1, add(rest1, low0_across[size:])]),
    )
    feed_b = summed_over_dp([feed_b])[0]
    feed_b, low = after((feed_b, low))
    pair_rows = pair0[0].shape[0]
    pair, rest = summed_over_dp(
        [side_by_side(low[None, :pair_rows]), side_by_side(low[None, pair_rows:])]
    )
    pair, rest = joined(pair).astype(F32), joined(rest)[0]
    beside = beside_tensor(rest)
    even = place % 2 == 0
    rest = jnp.concatenate(
        [jnp.where(even, rest, beside), jnp.where(even, beside, rest)]
    ).astype(F32)
    feed = jnp.stack([feed_a, feed_b]).astype(F32)

    def placed(zero, one, got):
        got = got.astype(F32)
        return jnp.stack([jnp.where(first, zero, got), jnp.where(first, got, one)])[None]

    return (
        placed(out0, out1, out_got),
        placed(grad0, grad1, grad_got),
        pair[:, :, :HD],
        rest[None, :local, :HD],
        rest[None, :local, HD:],
        pair[:, :, HD:],
        *[jnp.concatenate([feed[0, n], feed[1, n]], axis=1)[None] for n in range(3)],
        rest[local : local + 4, :local].T[None],
        rest[local + 4 : local + 6, :per_head].T[None],
    )


def solution(mesh):
    return jax.shard_map(
        body,
        mesh=mesh,
        in_specs=(
            P(None, ("dp", "tensor"), None),
            P(None, ("dp", "tensor"), None),
            P(None, "dp"),
            P("section", "dp", "tensor"),
            P("section", "dp", None),
            P("section", "dp", None),
            P("section", "dp", "tensor"),
            P("section", "dp", "tensor"),
            P("section", "dp", "tensor"),
            P("section", "dp", "tensor"),
            P("section", "dp", None),
            P("section", "dp", None),
        ),
        out_specs=(
            P("section", None, ("dp", "tensor"), None),
            P("section", None, ("dp", "tensor"), None),
            P("section", "dp", "tensor"),
            P("section", "dp", None),
            P("section", "dp", None),
            P("section", "dp", "tensor"),
            P("section", "dp", "tensor"),
            P("section", "dp", "tensor"),
            P("section", "dp", "tensor"),
            P("section", "dp", None),
            P("section", "dp", None),
        ),
        check_vma=False,
    )
```

profile of v0, /device:TPU:27, one launch (start us, length us, event | category | flops | bytes accessed | tf_op | source)
XLA Modules:
  0.0 468.7 jit_solution(923468365433394226)
XLA Ops:
  6.2 1.6 fusion.56
  8.9 1.7 fusion.54
  12.6 4.6 collective-permute-done.1.refs_1_
  17.2 16.7 %collective-permute-done.2.refs_2_ = bf16[256,512]{1,0:T(8,128)(2,1)S(1)} collective-permute-done((bf16[256,512]{1,0:T(8,128)(2,1)S(1)}, bf16[256,512]{1,0:T(8,128)(2,1)S(1)}, u32[]{:S(2)}, u32[]{:S(2)}) %collective-permute-start.2) | collective-permute-done | bytes 262176 | tf_op jit(solution)/shard_map/ppermute | solution.py:615
  35.5 3.0 collective-permute-start.5
  43.8 16.2 %collective-permute-done.5.refs_2_ = bf16[3,160,256]{2,1,0:T(8,128)(2,1)S(1)} collective-permute-done((bf16[3,160,256]{2,1,0:T(8,128)(2,1)S(1)}, bf16[3,160,256]{2,1,0:T(8,128)(2,1)S(1)}, u32[]{:S(2)}, u32[]{:S(2)}) %collective-permute-start.5) | collective-permute-done | bytes 245792 | tf_op jit(solution)/shard_map/ppermute | solution.py:615
  63.6 1.6 collective-permute-start.9
  67.6 1.5 collective-permute-done.11.refs_1_
  69.1 2.8 collective-permute-start.19
  71.9 12.2 %collective-permute-done.12.refs_2_ = bf16[3,160,256]{2,1,0:T(8,128)(2,1)S(1)} collective-permute-done((bf16[3,160,256]{2,1,0:T(8,128)(2,1)S(1)}, bf16[3,160,256]{2,1,0:T(8,128)(2,1)S(1)}, u32[]{:S(2)}, u32[]{:S(2)}) %collective-permute-start.12) | collective-permute-done | bytes 245792 | tf_op jit(solution)/shard_map/ppermute | solution.py:615
  85.0 1.6 shard_map.206
  88.2 3.0 collective-permute-start.21
  94.4 3.3 collective-permute-done.21.prev
  97.7 1.7 collective-permute-start.14
  99.3 3.2 collective-permute-start.17
  102.5 12.2 %shard_map.207 = (f32[4,512,256]{2,1,0:T(8,128)}, bf16[4,512,256]{2,1,0:T(8,128)(2,1)}, bf16[4,512,256]{2,1,0:T(8,128)(2,1)}, f32[4,512,1]{2,1,0:T(8,128)}, f32[...) custom-call(s32[1]{0:T(128)} %bitcast.choice, ...), custom_call_target="tpu_custom_call" | custom-call | flops 16142000128 | bytes 1 | tf_op jit(solution)/shard_map/pallas_call | solution.py:460
  116.5 2.8 collective-permute-done.14.refs_13_
  119.4 2.4 collective-permute-done.15.refs_7_
  122.2 12.1 %collective-permute-start.26 = (bf16[256,512]{1,0:T(8,128)(2,1)S(1)}, bf16[256,512]{1,0:T(8,128)(2,1)S(1)}, u32[]{:S(2)}, u32[]{:S(2)}) collective-permute-start(bf16[256,512]{1,0:T(8,128)(2,1)S(1)} %get-tuple-element.239.refs_0_), channel_id=1, source_target_pairs={{0,12},{4,0},{8,4},{12,8},{1,13},{5,1},{9,5},{13,9},{2,14},{6,2},{... | collective-permute-start | bytes 786440 | tf_op jit(solution)/shard_map/ppermute | solution.py:615
  134.3 2.7 collective-permute-done.25.refs_2_
  137.0 3.2 collective-permute-done.26.refs_3_
  141.4 1.9 collective-permute-done.22.refs_14_
  143.3 3.5 collective-permute-start.32
  159.8 11.8 %shard_map.209 = (bf16[4,512,512]{2,1,0:T(8,128)(2,1)}, bf16[4,512,512]{2,1,0:T(8,128)(2,1)}, f32[512,640]{1,0:T(8,128)}, f32[512,640]{1,0:T(8,128)}, bf16[512,640]{1,0:T(8,128)(2,1)S(1)}) custom-call(s32[1]{0:T(128)} %bitcast.choice, bf16[512,640]{1,0:T(8,128)(2,1)S(1)} %copy-done.22, f32[512,640]{1,0:T(8,128)} %get-tuple-element.234.middle, ...), custom_call_target="tpu_custom_call" | custom-call | flops 13836000256 | bytes 1 | tf_op jit(solution)/shard_map/pallas_call | solution.py:460
  174.1 2.4 collective-permute-start.34
  177.6 4.9 %collective-permute-done.34.prev = bf16[512,512]{1,0:T(8,128)(2,1)S(1)} collective-permute-done((bf16[512,512]{1,0:T(8,128)(2,1)S(1)}, bf16[512,512]{1,0:T(8,128)(2,1)S(1)}, u32[]{:S(2)}, u32[]{:S(2)}) %collective-permute-start.34) | collective-permute-done | bytes 524320 | tf_op jit(solution)/shard_map/ppermute | solution.py:496
  183.7 11.0 %shard_map.211 = (f32[4,512,256]{2,1,0:T(8,128)}, bf16[4,512,256]{2,1,0:T(8,128)(2,1)}, bf16[4,512,256]{2,1,0:T(8,128)(2,1)}, f32[4,512,1]{2,1,0:T(8,128)}, f32[...) custom-call(s32[1]{0:T(128)} %bitcast.27.choice, bf16[512,640]{1,0:T(8,128)(2,1)S(1)} %get-tuple-element.265.x, ...), custom_call_target="tpu_custom_call" | custom-call | flops 16142000128 | bytes 1 | tf_op jit(solution)/shard_map/pallas_call | solution.py:460
  194.7 11.7 %shard_map.212 = (bf16[4,512,512]{2,1,0:T(8,128)(2,1)}, bf16[4,512,512]{2,1,0:T(8,128)(2,1)}, f32[512,640]{1,0:T(8,128)}, f32[512,640]{1,0:T(8,128)}, bf16[512,640]{1,0:T(8,128)(2,1)S(1)}) custom-call(s32[1]{0:T(128)} %bitcast.27.choice, bf16[512,640]{1,0:T(8,128)(2,1)S(1)} %get-tuple-element.272.normed_two, f32[512,640]{1,0:T(8,128)} %get-tuple-element.273.middle, ...), custom_call_target="tpu_custom_call" | custom-call | flops 13836000256 | bytes 1 | tf_op jit(solution)/shard_map/pallas_call | solution.py:460
  207.7 22.8 %shard_map.213 = (bf16[2,2,3,640,256]{4,3,2,1,0:T(8,128)(2,1)}, bf16[2,2,3,640,256]{4,3,2,1,0:T(8,128)(2,1)}, f32[512,640]{1,0:T(8,128)}, bf16[512,640]{1,0:T(8,128)(2,1)S(1)}, f32[4,640]{1,0:T(4,128)S(1)}) custom-call(s32[1]{0:T(128)} %bitcast.27.choice, bf16[512,640]{1,0:T(8,128)(2,1)S(1)} %dynamic-slice_bitcast_fusion.grad, ...), custom_call_target="tpu_custom_call" | custom-call | flops 28824999936 | bytes 1 | tf_op jit(solution)/shard_map/pallas_call | solution.py:460
  230.6 16.2 %shard_map.214 = (bf16[2,640,512]{2,1,0:T(8,128)(2,1)}, bf16[2,640,512]{2,1,0:T(8,128)(2,1)}, f32[512,512]{1,0:T(8,128)}, bf16[512,512]{1,0:T(8,128)(2,1)S(1)}, ...) custom-call(s32[1]{0:T(128)} %bitcast.27.choice, bf16[512,640]{1,0:T(8,128)(2,1)S(1)} %get-tuple-element.286.grad_branch, ...), custom_call_target="tpu_custom_call" | custom-call | flops 19601000448 | bytes 1 | tf_op jit(solution)/shard_map/pallas_call | solution.py:460
  247.1 2.3 collective-permute-start.39
  249.4 4.5 fusion.9
  253.9 4.8 %collective-permute-done.39.kv_next = bf16[512,512]{1,0:T(8,128)(2,1)S(1)} collective-permute-done((bf16[512,512]{1,0:T(8,128)(2,1)S(1)}, bf16[512,512]{1,0:T(8,128)(2,1)S(1)}, u32[]{:S(2)}, u32[]{:S(2)}) %collective-permute-start.39) | collective-permute-done | bytes 524320 | tf_op jit(solution)/shard_map/ppermute | solution.py:596
  259.9 5.1 %shard_map.215 = (bf16[640,512]{1,0:T(8,128)(2,1)S(1)}, f32[512,640]{1,0:T(8,128)}, bf16[512,640]{1,0:T(8,128)(2,1)S(1)}, f32[1,640]{1,0:T(1,128)S(1)}, f32[1,256]{1,0:T(1,128)S(1)}) custom-call(f32[512,512]{1,0:T(8,128)} %get-tuple-element.303.kv_own, bf16[512,512]{1,0:T(8,128)(2,1)S(1)} %collective-permute-done.39.kv_next, f32[512,256]{1,0:T(8,128)S(1)} %copy-done.20, ...), custom_call_target="tpu_custom_call" | custom-call | flops 5765000192 | bytes 1 | tf_op jit(solution)/shard_map/pallas_call | solution.py:460
  265.0 23.4 %shard_map.216 = (bf16[2,2,3,640,256]{4,3,2,1,0:T(8,128)(2,1)}, bf16[2,2,3,640,256]{4,3,2,1,0:T(8,128)(2,1)}, f32[512,640]{1,0:T(8,128)}, bf16[512,640]{1,0:T(8,128)(2,1)S(1)}, f32[4,640]{1,0:T(4,128)S(1)}) custom-call(s32[1]{0:T(128)} %bitcast.choice, bf16[512,640]{1,0:T(8,128)(2,1)S(1)} %get-tuple-element.308.grad, ...), custom_call_target="tpu_custom_call" | custom-call | flops 28824999936 | bytes 1 | tf_op jit(solution)/shard_map/pallas_call | solution.py:460
  292.0 16.7 %shard_map.217 = (bf16[2,640,512]{2,1,0:T(8,128)(2,1)}, bf16[2,640,512]{2,1,0:T(8,128)(2,1)}, f32[512,512]{1,0:T(8,128)}, bf16[512,512]{1,0:T(8,128)(2,1)S(1)}, ...) custom-call(s32[1]{0:T(128)} %bitcast.choice, bf16[512,640]{1,0:T(8,128)(2,1)S(1)} %copy-done.25, ...), custom_call_target="tpu_custom_call" | custom-call | flops 19601000448 | bytes 1 | tf_op jit(solution)/shard_map/pallas_call | solution.py:460
  308.8 1.5 fusion.19
  310.3 2.6 add_convert_fusion.7
  312.9 3.1 collective-permute-start.44
  318.1 4.7 %fusion.13 = (bf16[3,640,256]{2,1,0:T(8,128)(2,1)}, bf16[3,640,256]{2,1,0:T(8,128)(2,1)}, bf16[3,640,256]{2,1,0:T(8,128)(2,1)}, bf16[3,640,256]{2,1,0:T(8,128)(2,1)}) fusion(bf16[2,2,3,640,256]{4,3,2,1,0:T(8,128)(2,1)} %collective-permute-done.42, bf16[2,2,3,640,256]{4,3,2,1,0:T(8,128)(2,1)S(1)} %copy-done.34), kind=kLoop, calls=%fused_computation.44 | loop fusion | flops 7864320 | bytes 11796480 | tf_op jit(solution)/shard_map/convert_element_type | solution.py:644
  325.1 4.2 collective-permute-done.44.kv_next
  329.3 5.1 %shard_map.218 = (bf16[640,512]{1,0:T(8,128)(2,1)S(1)}, f32[512,640]{1,0:T(8,128)}, bf16[512,640]{1,0:T(8,128)(2,1)S(1)}, f32[1,640]{1,0:T(1,128)S(1)}, f32[1,256]{1,0:T(1,128)S(1)}) custom-call(f32[512,512]{1,0:T(8,128)} %get-tuple-element.338.kv_own, bf16[512,512]{1,0:T(8,128)(2,1)S(1)} %collective-permute-done.44.kv_next, f32[512,256]{1,0:T(8,128)S(1)} %copy-done.18, ...), custom_call_target="tpu_custom_call" | custom-call | flops 5765000192 | bytes 1 | tf_op jit(solution)/shard_map/pallas_call | solution.py:460
  337.2 1.8 fusion.21
  339.0 15.2 %collective-permute-done.45 = bf16[3,640,256]{2,1,0:T(8,128)(2,1)} collective-permute-done((bf16[3,640,256]{2,1,0:T(8,128)(2,1)}, bf16[3,640,256]{2,1,0:T(8,128)(2,1)}, u32[]{:S(2)}, u32[]{:S(2)}) %collective-permute-start.45) | collective-permute-done | bytes 983072 | tf_op jit(solution)/shard_map/ppermute | solution.py:628
  355.1 1.7 broadcast_select_fusion.2
  359.2 15.2 %collective-permute-done.52 = bf16[3,640,256]{2,1,0:T(8,128)(2,1)S(1)} collective-permute-done((bf16[3,640,256]{2,1,0:T(8,128)(2,1)S(1)}, bf16[3,640,256]{2,1,0:T(8,128)(2,1)S(1)}, u32[]{:S(2)}, u32[]{:S(2)}) %collective-permute-start.52) | collective-permute-done | bytes 983072 | tf_op jit(solution)/shard_map/ppermute | solution.py:636
  374.4 2.7 add_convert_fusion.4
  377.1 2.6 collective-permute-start.53
  381.3 1.5 constant_dynamic-slice_fusion.8
  382.9 4.0 collective-permute-start.54
  387.5 1.6 fusion.2
  390.1 15.2 %collective-permute-done.55 = bf16[480,256]{1,0:T(8,128)(2,1)S(1)} collective-permute-done((bf16[480,256]{1,0:T(8,128)(2,1)S(1)}, bf16[480,256]{1,0:T(8,128)(2,1)S(1)}, u32[]{:S(2)}, u32[]{:S(2)}) %collective-permute-start.55) | collective-permute-done | bytes 245792 | tf_op jit(solution)/shard_map/ppermute | solution.py:665
  405.5 1.8 add_convert_fusion.2
  408.4 1.6 broadcast_select_fusion
  411.3 1.7 maximum_bitcast_fusion
  413.0 1.9 collective-permute-start.58
  414.9 3.2 collective-permute-start.59
  419.6 1.7 maximum_bitcast_fusion.1
  421.3 16.6 %collective-permute-done.59 = bf16[480,256]{1,0:T(8,128)(2,1)S(1)} collective-permute-done((bf16[480,256]{1,0:T(8,128)(2,1)S(1)}, bf16[480,256]{1,0:T(8,128)(2,1)S(1)}, u32[]{:S(2)}, u32[]{:S(2)}) %collective-permute-start.59) | collective-permute-done | bytes 245792 | tf_op jit(solution)/shard_map/ppermute | solution.py:665
  438.1 1.8 add_convert_fusion
  440.3 1.8 collective-permute-start.63
  442.1 1.5 collective-permute-start.64
  446.0 17.8 %collective-permute-done.63 = bf16[496,256]{1,0:T(8,128)(2,1)S(1)} collective-permute-done((bf16[496,256]{1,0:T(8,128)(2,1)S(1)}, bf16[496,256]{1,0:T(8,128)(2,1)S(1)}, u32[]{:S(2)}, u32[]{:S(2)}) %collective-permute-start.63) | collective-permute-done | bytes 253984 | tf_op jit(solution)/shard_map/ppermute | solution.py:665
  464.1 1.5 collective-permute-start.65
  (318 shorter events, 78.4 us)
Async XLA Ops:
  3.3 7.4 %collective-permute-start = (bf16[256,512]{1,0:T(8,128)(2,1)S(1)}, bf16[256,512]{1,0:T(8,128)(2,1)S(1)}, u32[]{:S(2)}, u32[]{:S(2)}) collective-permute-start(bf16[256,512]{1,0:T(8,128)(2,1)S(1)} %fusion.31), channel_id=1, source_target_pairs={{0,16},{16,0},{1,17},{17,1},{2,18},{18,2},{3,19},{19,3},{4,20},{20... | collective-permute-start | bytes 786440 | tf_op jit(solution)/shard_map/ppermute | solution.py:636
  10.7 6.4 %collective-permute-start.1 = (bf16[256,512]{1,0:T(8,128)(2,1)S(1)}, bf16[256,512]{1,0:T(8,128)(2,1)S(1)}, u32[]{:S(2)}, u32[]{:S(2)}) collective-permute-start(bf16[256,512]{1,0:T(8,128)(2,1)S(1)} %get-tuple-element.432.refs_0_), channel_id=1, source_target_pairs={{0,4},{4,8},{8,12},{12,0},{1,5},{5,9},{9,13},{13,1},{2,6},{6,10},{... | collective-permute-start | bytes 786440 | tf_op jit(solution)/shard_map/ppermute | solution.py:615
  10.8 23.1 %collective-permute-start.2 = (bf16[256,512]{1,0:T(8,128)(2,1)S(1)}, bf16[256,512]{1,0:T(8,128)(2,1)S(1)}, u32[]{:S(2)}, u32[]{:S(2)}) collective-permute-start(bf16[256,512]{1,0:T(8,128)(2,1)S(1)} %get-tuple-element.432.refs_0_), channel_id=1, source_target_pairs={{0,8},{4,12},{8,0},{12,4},{1,9},{5,13},{9,1},{13,5},{2,10},{6,14},... | collective-permute-start | bytes 786440 | tf_op jit(solution)/shard_map/ppermute | solution.py:615
  12.1 21.8 %collective-permute-start.3 = (bf16[256,512]{1,0:T(8,128)(2,1)S(1)}, bf16[256,512]{1,0:T(8,128)(2,1)S(1)}, u32[]{:S(2)}, u32[]{:S(2)}) collective-permute-start(bf16[256,512]{1,0:T(8,128)(2,1)S(1)} %get-tuple-element.432.refs_0_), channel_id=1, source_target_pairs={{0,12},{4,0},{8,4},{12,8},{1,13},{5,1},{9,5},{13,9},{2,14},{6,2},{... | collective-permute-start | bytes 786440 | tf_op jit(solution)/shard_map/ppermute | solution.py:615
  35.4 8.4 %collective-permute-start.4 = (bf16[3,160,256]{2,1,0:T(8,128)(2,1)S(1)}, bf16[3,160,256]{2,1,0:T(8,128)(2,1)S(1)}, u32[]{:S(2)}, u32[]{:S(2)}) collective-permute-start(bf16[3,160,256]{2,1,0:T(8,128)(2,1)S(1)} %pad_maximum_fusion.7.refs_0_), channel_id=1, source_target_pairs={{0,4},{4,8},{8,12},{12,0},{1,5},{5,9},{9,13},{13,1},{2,6},{6,10},{... | collective-permute-start | bytes 737288 | tf_op jit(solution)/shard_map/ppermute | solution.py:615
  35.5 24.6 %collective-permute-start.5 = (bf16[3,160,256]{2,1,0:T(8,128)(2,1)S(1)}, bf16[3,160,256]{2,1,0:T(8,128)(2,1)S(1)}, u32[]{:S(2)}, u32[]{:S(2)}) collective-permute-start(bf16[3,160,256]{2,1,0:T(8,128)(2,1)S(1)} %pad_maximum_fusion.7.refs_0_), channel_id=1, source_target_pairs={{0,8},{4,12},{8,0},{12,4},{1,9},{5,13},{9,1},{13,5},{2,10},{6,14},... | collective-permute-start | bytes 737288 | tf_op jit(solution)/shard_map/ppermute | solution.py:615
  38.4 21.6 %collective-permute-start.6 = (bf16[3,160,256]{2,1,0:T(8,128)(2,1)S(1)}, bf16[3,160,256]{2,1,0:T(8,128)(2,1)S(1)}, u32[]{:S(2)}, u32[]{:S(2)}) collective-permute-start(bf16[3,160,256]{2,1,0:T(8,128)(2,1)S(1)} %pad_maximum_fusion.7.refs_0_), channel_id=1, source_target_pairs={{0,12},{4,0},{8,4},{12,8},{1,13},{5,1},{9,5},{13,9},{2,14},{6,2},{... | collective-permute-start | bytes 737288 | tf_op jit(solution)/shard_map/ppermute | solution.py:615
  40.9 20.2 %collective-permute-start.8 = (bf16[320,512]{1,0:T(8,128)(2,1)S(1)}, bf16[320,512]{1,0:T(8,128)(2,1)}, u32[]{:S(2)}, u32[]{:S(2)}) collective-permute-start(bf16[320,512]{1,0:T(8,128)(2,1)S(1)} %get-tuple-element.204), channel_id=1, source_target_pairs={{0,1},{1,0},{2,3},{3,2},{4,5},{5,4},{6,7},{7,6},{8,9},{9,8},{10,11... | collective-permute-start | bytes 983048 | tf_op jit(solution)/shard_map/ppermute | solution.py:632
  42.3 19.9 %collective-permute-start.7 = (bf16[640,512]{1,0:T(8,128)(2,1)S(1)}, bf16[640,512]{1,0:T(8,128)(2,1)}, u32[]{:S(2)}, u32[]{:S(2)}) collective-permute-start(bf16[640,512]{1,0:T(8,128)(2,1)S(1)} %get-tuple-element.224.qo_c), channel_id=1, source_target_pairs={{0,2},{1,3},{2,0},{3,1},{4,6},{5,7},{6,4},{7,5},{8,10},{9,11},{10,... | collective-permute-start | bytes 1966088 | tf_op jit(solution)/shard_map/ppermute | solution.py:628
  62.2 6.9 %collective-permute-start.11 = (bf16[3,160,256]{2,1,0:T(8,128)(2,1)S(1)}, bf16[3,160,256]{2,1,0:T(8,128)(2,1)S(1)}, u32[]{:S(2)}, u32[]{:S(2)}) collective-permute-start(bf16[3,160,256]{2,1,0:T(8,128)(2,1)S(1)} %pad_maximum_fusion.8.refs_0_), channel_id=1, source_target_pairs={{0,4},{4,8},{8,12},{12,0},{1,5},{5,9},{9,13},{13,1},{2,6},{6,10},{... | collective-permute-start | bytes 737288 | tf_op jit(solution)/shard_map/ppermute | solution.py:615
  62.2 21.9 %collective-permute-start.12 = (bf16[3,160,256]{2,1,0:T(8,128)(2,1)S(1)}, bf16[3,160,256]{2,1,0:T(8,128)(2,1)S(1)}, u32[]{:S(2)}, u32[]{:S(2)}) collective-permute-start(bf16[3,160,256]{2,1,0:T(8,128)(2,1)S(1)} %pad_maximum_fusion.8.refs_0_), channel_id=1, source_target_pairs={{0,8},{4,12},{8,0},{12,4},{1,9},{5,13},{9,1},{13,5},{2,10},{6,14},... | collective-permute-start | bytes 737288 | tf_op jit(solution)/shard_map/ppermute | solution.py:615
  62.4 35.3 %collective-permute-start.10 = (bf16[3,640,256]{2,1,0:T(8,128)(2,1)}, bf16[3,640,256]{2,1,0:T(8,128)(2,1)}, u32[]{:S(2)}, u32[]{:S(2)}) collective-permute-start(bf16[3,640,256]{2,1,0:T(8,128)(2,1)} %shard_map.204.refs_4_), channel_id=1, source_target_pairs={{0,2},{1,3},{2,0},{3,1},{4,6},{5,7},{6,4},{7,5},{8,10},{9,11},{10,... | collective-permute-start | bytes 2949128 | tf_op jit(solution)/shard_map/ppermute | solution.py:628
  63.6 34.0 %collective-permute-start.9 = (bf16[3,640,256]{2,1,0:T(8,128)(2,1)}, bf16[3,640,256]{2,1,0:T(8,128)(2,1)}, u32[]{:S(2)}, u32[]{:S(2)}) collective-permute-start(bf16[3,640,256]{2,1,0:T(8,128)(2,1)} %shard_map.204.refs_4_), channel_id=1, source_target_pairs={{0,16},{16,0},{1,17},{17,1},{2,18},{18,2},{3,19},{19,3},{4,20},{20... | collective-permute-start | bytes 2949128 | tf_op jit(solution)/shard_map/ppermute | solution.py:636
  65.2 23.0 %collective-permute-start.13 = (bf16[3,160,256]{2,1,0:T(8,128)(2,1)S(1)}, bf16[3,160,256]{2,1,0:T(8,128)(2,1)S(1)}, u32[]{:S(2)}, u32[]{:S(2)}) collective-permute-start(bf16[3,160,256]{2,1,0:T(8,128)(2,1)S(1)} %pad_maximum_fusion.8.refs_0_), channel_id=1, source_target_pairs={{0,12},{4,0},{8,4},{12,8},{1,13},{5,1},{9,5},{13,9},{2,14},{6,2},{... | collective-permute-start | bytes 737288 | tf_op jit(solution)/shard_map/ppermute | solution.py:615
  69.1 25.0 %collective-permute-start.19 = (bf16[640,512]{1,0:T(8,128)(2,1)S(1)}, bf16[640,512]{1,0:T(8,128)(2,1)}, u32[]{:S(2)}, u32[]{:S(2)}) collective-permute-start(bf16[640,512]{1,0:T(8,128)(2,1)S(1)} %get-tuple-element.224.qo_c), channel_id=1, source_target_pairs={{0,1},{1,0},{2,3},{3,2},{4,5},{5,4},{6,7},{7,6},{8,9},{9,8},{10,11... | collective-permute-start | bytes 1966088 | tf_op jit(solution)/shard_map/ppermute | solution.py:632
  84.1 13.6 %collective-permute-start.20 = (bf16[640,512]{1,0:T(8,128)(2,1)}, bf16[640,512]{1,0:T(8,128)(2,1)}, u32[]{:S(2)}, u32[]{:S(2)}) collective-permute-start(bf16[640,512]{1,0:T(8,128)(2,1)} %collective-permute-done.7.qo_d), channel_id=1, source_target_pairs={{0,1},{1,0},{2,3},{3,2},{4,5},{5,4},{6,7},{7,6},{8,9},{9,8},{10,11... | collective-permute-start | bytes 1966088 | tf_op jit(solution)/shard_map/ppermute | solution.py:632
  88.2 9.5 %collective-permute-start.21 = (bf16[512,512]{1,0:T(8,128)(2,1)}, bf16[512,512]{1,0:T(8,128)(2,1)}, u32[]{:S(2)}, u32[]{:S(2)}) collective-permute-start(bf16[512,512]{1,0:T(8,128)(2,1)} %get-tuple-element.220.own), channel_id=1, source_target_pairs={{0,1},{1,2},{2,3},{4,5},{5,6},{6,7},{8,9},{9,10},{10,11},{12,13},{... | collective-permute-start | bytes 1572872 | tf_op jit(solution)/shard_map/ppermute | solution.py:496
  94.1 21.4 %collective-permute-start.16 = (bf16[3,640,256]{2,1,0:T(8,128)(2,1)}, bf16[3,640,256]{2,1,0:T(8,128)(2,1)S(1)}, u32[]{:S(2)}, u32[]{:S(2)}) collective-permute-start(bf16[3,640,256]{2,1,0:T(8,128)(2,1)} %shard_map.204.refs_4_), channel_id=1, source_target_pairs={{0,1},{1,0},{2,3},{3,2},{4,5},{5,4},{6,7},{7,6},{8,9},{9,8},{10,11... | collective-permute-start | bytes 2949128 | tf_op jit(solution)/shard_map/ppermute | solution.py:632
  97.7 21.7 %collective-permute-start.14 = (bf16[3,640,256]{2,1,0:T(8,128)(2,1)}, bf16[3,640,256]{2,1,0:T(8,128)(2,1)}, u32[]{:S(2)}, u32[]{:S(2)}) collective-permute-start(bf16[3,640,256]{2,1,0:T(8,128)(2,1)} %shard_map.205.refs_5_), channel_id=1, source_target_pairs={{0,16},{16,0},{1,17},{17,1},{2,18},{18,2},{3,19},{19,3},{4,20},{20... | collective-permute-start | bytes 2949128 | tf_op jit(solution)/shard_map/ppermute | solution.py:636
  99.3 22.4 %collective-permute-start.15 = (bf16[3,640,256]{2,1,0:T(8,128)(2,1)}, bf16[3,640,256]{2,1,0:T(8,128)(2,1)}, u32[]{:S(2)}, u32[]{:S(2)}) collective-permute-start(bf16[3,640,256]{2,1,0:T(8,128)(2,1)} %shard_map.205.refs_5_), channel_id=1, source_target_pairs={{0,2},{1,3},{2,0},{3,1},{4,6},{5,7},{6,4},{7,5},{8,10},{9,11},{10,... | collective-permute-start | bytes 2949128 | tf_op jit(solution)/shard_map/ppermute | solution.py:628
  99.3 22.4 %collective-permute-start.17 = (bf16[3,640,256]{2,1,0:T(8,128)(2,1)}, bf16[3,640,256]{2,1,0:T(8,128)(2,1)S(1)}, u32[]{:S(2)}, u32[]{:S(2)}) collective-permute-start(bf16[3,640,256]{2,1,0:T(8,128)(2,1)} %collective-permute-done.10.refs_6_), channel_id=1, source_target_pairs={{0,1},{1,0},{2,3},{3,2},{4,5},{5,4},{6,7},{7,6},{8,9},{9,8},{10,11... | collective-permute-start | bytes 2949128 | tf_op jit(solution)/shard_map/ppermute | solution.py:632
  102.5 19.2 %collective-permute-start.18 = (bf16[3,640,256]{2,1,0:T(8,128)(2,1)}, bf16[3,640,256]{2,1,0:T(8,128)(2,1)S(1)}, u32[]{:S(2)}, u32[]{:S(2)}) collective-permute-start(bf16[3,640,256]{2,1,0:T(8,128)(2,1)} %collective-permute-done.9.refs_12_), channel_id=1, source_target_pairs={{0,1},{1,0},{2,3},{3,2},{4,5},{5,4},{6,7},{7,6},{8,9},{9,8},{10,11... | collective-permute-start | bytes 2949128 | tf_op jit(solution)/shard_map/ppermute | solution.py:632
  121.8 21.5 %collective-permute-start.22 = (bf16[3,640,256]{2,1,0:T(8,128)(2,1)}, bf16[3,640,256]{2,1,0:T(8,128)(2,1)}, u32[]{:S(2)}, u32[]{:S(2)}) collective-permute-start(bf16[3,640,256]{2,1,0:T(8,128)(2,1)} %collective-permute-done.9.refs_12_), channel_id=1, source_target_pairs={{0,2},{1,3},{2,0},{3,1},{4,6},{5,7},{6,4},{7,5},{8,10},{9,11},{10,... | collective-permute-start | bytes 2949128 | tf_op jit(solution)/shard_map/ppermute | solution.py:628
  121.8 21.5 %collective-permute-start.23 = (bf16[3,640,256]{2,1,0:T(8,128)(2,1)}, bf16[3,640,256]{2,1,0:T(8,128)(2,1)}, u32[]{:S(2)}, u32[]{:S(2)}) collective-permute-start(bf16[3,640,256]{2,1,0:T(8,128)(2,1)} %collective-permute-done.15.refs_7_), channel_id=1, source_target_pairs={{0,16},{16,0},{1,17},{17,1},{2,18},{18,2},{3,19},{19,3},{4,20},{20... | collective-permute-start | bytes 2949128 | tf_op jit(solution)/shard_map/ppermute | solution.py:636
  122.2 12.1 %collective-permute-start.24 = (bf16[256,512]{1,0:T(8,128)(2,1)S(1)}, bf16[256,512]{1,0:T(8,128)(2,1)S(1)}, u32[]{:S(2)}, u32[]{:S(2)}) collective-permute-start(bf16[256,512]{1,0:T(8,128)(2,1)S(1)} %get-tuple-element.239.refs_0_), channel_id=1, source_target_pairs={{0,4},{4,8},{8,12},{12,0},{1,5},{5,9},{9,13},{13,1},{2,6},{6,10},{... | collective-permute-start | bytes 786440 | tf_op jit(solution)/shard_map/ppermute | solution.py:615
  122.2 14.8 %collective-permute-start.25 = (bf16[256,512]{1,0:T(8,128)(2,1)S(1)}, bf16[256,512]{1,0:T(8,128)(2,1)S(1)}, u32[]{:S(2)}, u32[]{:S(2)}) collective-permute-start(bf16[256,512]{1,0:T(8,128)(2,1)S(1)} %get-tuple-element.239.refs_0_), channel_id=1, source_target_pairs={{0,8},{4,12},{8,0},{12,4},{1,9},{5,13},{9,1},{13,5},{2,10},{6,14},... | collective-permute-start | bytes 786440 | tf_op jit(solution)/shard_map/ppermute | solution.py:615
  122.2 18.1 %collective-permute-start.26 = (bf16[256,512]{1,0:T(8,128)(2,1)S(1)}, bf16[256,512]{1,0:T(8,128)(2,1)S(1)}, u32[]{:S(2)}, u32[]{:S(2)}) collective-permute-start(bf16[256,512]{1,0:T(8,128)(2,1)S(1)} %get-tuple-element.239.refs_0_), channel_id=1, source_target_pairs={{0,12},{4,0},{8,4},{12,8},{1,13},{5,1},{9,5},{13,9},{2,14},{6,2},{... | collective-permute-start | bytes 786440 | tf_op jit(solution)/shard_map/ppermute | solution.py:615
  143.3 4.8 %collective-permute-start.32 = (bf16[320,512]{1,0:T(8,128)(2,1)S(1)}, bf16[320,512]{1,0:T(8,128)(2,1)S(1)}, u32[]{:S(2)}, u32[]{:S(2)}) collective-permute-start(bf16[320,512]{1,0:T(8,128)(2,1)S(1)} %get-tuple-element.258), channel_id=1, source_target_pairs={{0,1},{1,0},{2,3},{3,2},{4,5},{5,4},{6,7},{7,6},{8,9},{9,8},{10,11... | collective-permute-start | bytes 983048 | tf_op jit(solution)/shard_map/ppermute | solution.py:632
  146.8 3.0 collective-permute-start.27
  146.9 4.3 collective-permute-start.28
  147.4 5.3 %collective-permute-start.29 = (bf16[3,640,256]{2,1,0:T(8,128)(2,1)}, bf16[3,640,256]{2,1,0:T(8,128)(2,1)}, u32[]{:S(2)}, u32[]{:S(2)}) collective-permute-start(bf16[3,640,256]{2,1,0:T(8,128)(2,1)} %collective-permute-done.14.refs_13_), channel_id=1, source_target_pairs={{0,1},{1,0},{2,3},{3,2},{4,5},{5,4},{6,7},{7,6},{8,9},{9,8},{10,11... | collective-permute-start | bytes 2949128 | tf_op jit(solution)/shard_map/ppermute | solution.py:632
  147.4 6.6 %collective-permute-start.30 = (bf16[3,640,256]{2,1,0:T(8,128)(2,1)}, bf16[3,640,256]{2,1,0:T(8,128)(2,1)}, u32[]{:S(2)}, u32[]{:S(2)}) collective-permute-start(bf16[3,640,256]{2,1,0:T(8,128)(2,1)} %collective-permute-done.22.refs_14_), channel_id=1, source_target_pairs={{0,1},{1,0},{2,3},{3,2},{4,5},{5,4},{6,7},{7,6},{8,9},{9,8},{10,11... | collective-permute-start | bytes 2949128 | tf_op jit(solution)/shard_map/ppermute | solution.py:632
  148.1 7.4 %collective-permute-start.31 = (bf16[3,640,256]{2,1,0:T(8,128)(2,1)}, bf16[3,640,256]{2,1,0:T(8,128)(2,1)}, u32[]{:S(2)}, u32[]{:S(2)}) collective-permute-start(bf16[3,640,256]{2,1,0:T(8,128)(2,1)} %collective-permute-done.23.refs_15_), channel_id=1, source_target_pairs={{0,1},{1,0},{2,3},{3,2},{4,5},{5,4},{6,7},{7,6},{8,9},{9,8},{10,11... | collective-permute-start | bytes 2949128 | tf_op jit(solution)/shard_map/ppermute | solution.py:632
  155.5 18.6 %collective-permute-start.33 = (bf16[640,512]{1,0:T(8,128)(2,1)}, bf16[640,512]{1,0:T(8,128)(2,1)}, u32[]{:S(2)}, u32[]{:S(2)}) collective-permute-start(bf16[640,512]{1,0:T(8,128)(2,1)} %get-tuple-element.270.qo_c), channel_id=1, source_target_pairs={{0,2},{1,3},{2,0},{3,1},{4,6},{5,7},{6,4},{7,5},{8,10},{9,11},{10,... | collective-permute-start | bytes 1966088 | tf_op jit(solution)/shard_map/ppermute | solution.py:628
  156.9 20.8 %collective-permute-start.35 = (bf16[640,512]{1,0:T(8,128)(2,1)}, bf16[640,512]{1,0:T(8,128)(2,1)}, u32[]{:S(2)}, u32[]{:S(2)}) collective-permute-start(bf16[640,512]{1,0:T(8,128)(2,1)} %get-tuple-element.270.qo_c), channel_id=1, source_target_pairs={{0,1},{1,0},{2,3},{3,2},{4,5},{5,4},{6,7},{7,6},{8,9},{9,8},{10,11... | collective-permute-start | bytes 1966088 | tf_op jit(solution)/shard_map/ppermute | solution.py:632
  174.1 8.5 %collective-permute-start.36 = (bf16[640,512]{1,0:T(8,128)(2,1)}, bf16[640,512]{1,0:T(8,128)(2,1)}, u32[]{:S(2)}, u32[]{:S(2)}) collective-permute-start(bf16[640,512]{1,0:T(8,128)(2,1)} %collective-permute-done.33.qo_d), channel_id=1, source_target_pairs={{0,1},{1,0},{2,3},{3,2},{4,5},{5,4},{6,7},{7,6},{8,9},{9,8},{10,11... | collective-permute-start | bytes 1966088 | tf_op jit(solution)/shard_map/ppermute | solution.py:632
  174.1 8.5 %collective-permute-start.34 = (bf16[512,512]{1,0:T(8,128)(2,1)S(1)}, bf16[512,512]{1,0:T(8,128)(2,1)S(1)}, u32[]{:S(2)}, u32[]{:S(2)}) collective-permute-start(bf16[512,512]{1,0:T(8,128)(2,1)S(1)} %get-tuple-element.263.own), channel_id=1, source_target_pairs={{0,1},{1,2},{2,3},{4,5},{5,6},{6,7},{8,9},{9,10},{10,11},{12,13},{... | collective-permute-start | bytes 1572872 | tf_op jit(solution)/shard_map/ppermute | solution.py:496
  206.4 24.0 %collective-permute-start.37 = (bf16[512,640]{1,0:T(8,128)(2,1)S(1)}, bf16[512,640]{1,0:T(8,128)(2,1)S(1)}, u32[]{:S(2)}, u32[]{:S(2)}) collective-permute-start(bf16[512,640]{1,0:T(8,128)(2,1)S(1)} %broadcast_select_fusion.4), channel_id=1, source_target_pairs={{0,16},{16,0},{1,17},{17,1},{2,18},{18,2},{3,19},{19,3},{4,20},{20... | collective-permute-start | bytes 1966088 | tf_op jit(solution)/shard_map/ppermute | solution.py:636
  230.5 16.3 %collective-permute-start.38 = (bf16[2,2,3,640,256]{4,3,2,1,0:T(8,128)(2,1)}, bf16[2,2,3,640,256]{4,3,2,1,0:T(8,128)(2,1)}, u32[]{:S(2)}, u32[]{:S(2)}) collective-permute-start(bf16[2,2,3,640,256]{4,3,2,1,0:T(8,128)(2,1)} %get-tuple-element.297), channel_id=1, source_target_pairs={{0,1},{1,0},{2,3},{3,2},{4,5},{5,4},{6,7},{7,6},{8,9},{9,8},{10,11... | collective-permute-start | bytes 11796488 | tf_op jit(solution)/shard_map/ppermute | solution.py:632
  246.8 12.0 %collective-permute-start.40 = (bf16[2,640,512]{2,1,0:T(8,128)(2,1)}, bf16[2,640,512]{2,1,0:T(8,128)(2,1)S(1)}, u32[]{:S(2)}, u32[]{:S(2)}) collective-permute-start(bf16[2,640,512]{2,1,0:T(8,128)(2,1)} %get-tuple-element.299), channel_id=1, source_target_pairs={{0,1},{1,0},{2,3},{3,2},{4,5},{5,4},{6,7},{7,6},{8,9},{9,8},{10,11... | collective-permute-start | bytes 3932168 | tf_op jit(solution)/shard_map/ppermute | solution.py:632
  247.1 11.6 %collective-permute-start.39 = (bf16[512,512]{1,0:T(8,128)(2,1)S(1)}, bf16[512,512]{1,0:T(8,128)(2,1)S(1)}, u32[]{:S(2)}, u32[]{:S(2)}) collective-permute-start(bf16[512,512]{1,0:T(8,128)(2,1)S(1)} %get-tuple-element.298), channel_id=1, source_target_pairs={{1,0},{2,1},{3,2},{5,4},{6,5},{7,6},{9,8},{10,9},{11,10},{13,12},{... | collective-permute-start | bytes 1572872 | tf_op jit(solution)/shard_map/ppermute | solution.py:596
  259.9 29.3 %collective-permute-start.41 = (bf16[3,640,256]{2,1,0:T(8,128)(2,1)S(1)}, bf16[3,640,256]{2,1,0:T(8,128)(2,1)}, u32[]{:S(2)}, u32[]{:S(2)}) collective-permute-start(bf16[3,640,256]{2,1,0:T(8,128)(2,1)S(1)} %get-tuple-element.302), channel_id=1, source_target_pairs={{0,2},{1,3},{2,0},{3,1},{4,6},{5,7},{6,4},{7,5},{8,10},{9,11},{10,... | collective-permute-start | bytes 2949128 | tf_op jit(solution)/shard_map/ppermute | solution.py:628
  289.2 23.7 %collective-permute-start.42 = (bf16[2,2,3,640,256]{4,3,2,1,0:T(8,128)(2,1)}, bf16[2,2,3,640,256]{4,3,2,1,0:T(8,128)(2,1)}, u32[]{:S(2)}, u32[]{:S(2)}) collective-permute-start(bf16[2,2,3,640,256]{4,3,2,1,0:T(8,128)(2,1)} %get-tuple-element.333), channel_id=1, source_target_pairs={{0,1},{1,0},{2,3},{3,2},{4,5},{5,4},{6,7},{7,6},{8,9},{9,8},{10,11... | collective-permute-start | bytes 11796488 | tf_op jit(solution)/shard_map/ppermute | solution.py:632
  289.6 23.3 %collective-permute-start.43 = (bf16[3,640,256]{2,1,0:T(8,128)(2,1)}, bf16[3,640,256]{2,1,0:T(8,128)(2,1)S(1)}, u32[]{:S(2)}, u32[]{:S(2)}) collective-permute-start(bf16[3,640,256]{2,1,0:T(8,128)(2,1)} %get-tuple-element.334), channel_id=1, source_target_pairs={{0,2},{1,3},{2,0},{3,1},{4,6},{5,7},{6,4},{7,5},{8,10},{9,11},{10,... | collective-permute-start | bytes 2949128 | tf_op jit(solution)/shard_map/ppermute | solution.py:628
  312.9 16.4 %collective-permute-start.44 = (bf16[512,512]{1,0:T(8,128)(2,1)S(1)}, bf16[512,512]{1,0:T(8,128)(2,1)S(1)}, u32[]{:S(2)}, u32[]{:S(2)}) collective-permute-start(bf16[512,512]{1,0:T(8,128)(2,1)S(1)} %get-tuple-element.339), channel_id=1, source_target_pairs={{1,0},{2,1},{3,2},{5,4},{6,5},{7,6},{9,8},{10,9},{11,10},{13,12},{... | collective-permute-start | bytes 1572872 | tf_op jit(solution)/shard_map/ppermute | solution.py:596
  316.0 19.3 %collective-permute-start.49 = (bf16[640,512]{1,0:T(8,128)(2,1)}, bf16[640,512]{1,0:T(8,128)(2,1)}, u32[]{:S(2)}, u32[]{:S(2)}) collective-permute-start(bf16[640,512]{1,0:T(8,128)(2,1)} %get-tuple-element.359), channel_id=1, source_target_pairs={{0,2},{1,3},{2,0},{3,1},{4,6},{5,7},{6,4},{7,5},{8,10},{9,11},{10,... | collective-permute-start | bytes 1966088 | tf_op jit(solution)/shard_map/ppermute | solution.py:628
  317.3 19.9 %collective-permute-start.48 = (bf16[2,640,512]{2,1,0:T(8,128)(2,1)}, bf16[2,640,512]{2,1,0:T(8,128)(2,1)}, u32[]{:S(2)}, u32[]{:S(2)}) collective-permute-start(bf16[2,640,512]{2,1,0:T(8,128)(2,1)} %get-tuple-element.357), channel_id=1, source_target_pairs={{0,1},{1,0},{2,3},{3,2},{4,5},{5,4},{6,7},{7,6},{8,9},{9,8},{10,11... | collective-permute-start | bytes 3932168 | tf_op jit(solution)/shard_map/ppermute | solution.py:632
  317.7 6.5 %collective-permute-start.47 = (bf16[1,352,512]{2,1,0:T(8,128)(2,1)S(1)}, bf16[1,352,512]{2,1,0:T(8,128)(2,1)S(1)}, u32[]{:S(2)}, u32[]{:S(2)}) collective-permute-start(bf16[1,352,512]{2,1,0:T(8,128)(2,1)S(1)} %bitcast.226), channel_id=1, source_target_pairs={{0,1},{1,0},{2,3},{3,2},{4,5},{5,4},{6,7},{7,6},{8,9},{9,8},{10,11... | collective-permute-start | bytes 1081352 | tf_op jit(solution)/shard_map/ppermute | solution.py:632
  322.8 31.4 %collective-permute-start.45 = (bf16[3,640,256]{2,1,0:T(8,128)(2,1)}, bf16[3,640,256]{2,1,0:T(8,128)(2,1)}, u32[]{:S(2)}, u32[]{:S(2)}) collective-permute-start(bf16[3,640,256]{2,1,0:T(8,128)(2,1)} %get-tuple-element.390), channel_id=1, source_target_pairs={{0,2},{1,3},{2,0},{3,1},{4,6},{5,7},{6,4},{7,5},{8,10},{9,11},{10,... | collective-permute-start | bytes 2949128 | tf_op jit(solution)/shard_map/ppermute | solution.py:628
  335.0 19.2 %collective-permute-start.50 = (bf16[512,640]{1,0:T(8,128)(2,1)S(1)}, bf16[512,640]{1,0:T(8,128)(2,1)S(1)}, u32[]{:S(2)}, u32[]{:S(2)}) collective-permute-start(bf16[512,640]{1,0:T(8,128)(2,1)S(1)} %broadcast_select_fusion.3), channel_id=1, source_target_pairs={{0,16},{16,0},{1,17},{17,1},{2,18},{18,2},{3,19},{19,3},{4,20},{20... | collective-permute-start | bytes 1966088 | tf_op jit(solution)/shard_map/ppermute | solution.py:636
  356.8 17.6 %collective-permute-start.52 = (bf16[3,640,256]{2,1,0:T(8,128)(2,1)S(1)}, bf16[3,640,256]{2,1,0:T(8,128)(2,1)S(1)}, u32[]{:S(2)}, u32[]{:S(2)}) collective-permute-start(bf16[3,640,256]{2,1,0:T(8,128)(2,1)S(1)} %broadcast_select_fusion.2), channel_id=1, source_target_pairs={{0,16},{16,0},{1,17},{17,1},{2,18},{18,2},{3,19},{19,3},{4,20},{20... | collective-permute-start | bytes 2949128 | tf_op jit(solution)/shard_map/ppermute | solution.py:636
  357.1 20.0 %collective-permute-start.51 = (bf16[3,640,256]{2,1,0:T(8,128)(2,1)S(1)}, bf16[3,640,256]{2,1,0:T(8,128)(2,1)S(1)}, u32[]{:S(2)}, u32[]{:S(2)}) collective-permute-start(bf16[3,640,256]{2,1,0:T(8,128)(2,1)S(1)} %copy-done.48), channel_id=1, source_target_pairs={{0,2},{1,3},{2,0},{3,1},{4,6},{5,7},{6,4},{7,5},{8,10},{9,11},{10,... | collective-permute-start | bytes 2949128 | tf_op jit(solution)/shard_map/ppermute | solution.py:628
  377.1 30.1 %collective-permute-start.53 = (bf16[1344,512]{1,0:T(8,128)(2,1)}, bf16[1344,512]{1,0:T(8,128)(2,1)}, u32[]{:S(2)}, u32[]{:S(2)}) collective-permute-start(bf16[1344,512]{1,0:T(8,128)(2,1)} %pad_maximum_fusion), channel_id=1, source_target_pairs={{0,2},{1,3},{2,0},{3,1},{4,6},{5,7},{6,4},{7,5},{8,10},{9,11},{10,... | collective-permute-start | bytes 4128776 | tf_op jit(solution)/shard_map/ppermute | solution.py:628
  381.1 24.4 %collective-permute-start.57 = (bf16[3,640,256]{2,1,0:T(8,128)(2,1)}, bf16[3,640,256]{2,1,0:T(8,128)(2,1)}, u32[]{:S(2)}, u32[]{:S(2)}) collective-permute-start(bf16[3,640,256]{2,1,0:T(8,128)(2,1)} %broadcast_select_fusion.1), channel_id=1, source_target_pairs={{0,16},{16,0},{1,17},{17,1},{2,18},{18,2},{3,19},{19,3},{4,20},{20... | collective-permute-start | bytes 2949128 | tf_op jit(solution)/shard_map/ppermute | solution.py:636
  382.9 7.2 %collective-permute-start.54 = (bf16[480,256]{1,0:T(8,128)(2,1)S(1)}, bf16[480,256]{1,0:T(8,128)(2,1)S(1)}, u32[]{:S(2)}, u32[]{:S(2)}) collective-permute-start(bf16[480,256]{1,0:T(8,128)(2,1)S(1)} %bitcast.241), channel_id=1, source_target_pairs={{0,4},{4,8},{8,12},{12,0},{1,5},{5,9},{9,13},{13,1},{2,6},{6,10},{... | collective-permute-start | bytes 737288 | tf_op jit(solution)/shard_map/ppermute | solution.py:665
  386.9 18.4 %collective-permute-start.55 = (bf16[480,256]{1,0:T(8,128)(2,1)S(1)}, bf16[480,256]{1,0:T(8,128)(2,1)S(1)}, u32[]{:S(2)}, u32[]{:S(2)}) collective-permute-start(bf16[480,256]{1,0:T(8,128)(2,1)S(1)} %bitcast.240), channel_id=1, source_target_pairs={{0,8},{4,12},{8,0},{12,4},{1,9},{5,13},{9,1},{13,5},{2,10},{6,14},... | collective-permute-start | bytes 737288 | tf_op jit(solution)/shard_map/ppermute | solution.py:665
  386.9 18.4 %collective-permute-start.56 = (bf16[480,256]{1,0:T(8,128)(2,1)S(1)}, bf16[480,256]{1,0:T(8,128)(2,1)S(1)}, u32[]{:S(2)}, u32[]{:S(2)}) collective-permute-start(bf16[480,256]{1,0:T(8,128)(2,1)S(1)} %bitcast.238), channel_id=1, source_target_pairs={{0,12},{4,0},{8,4},{12,8},{1,13},{5,1},{9,5},{13,9},{2,14},{6,2},{... | collective-permute-start | bytes 737288 | tf_op jit(solution)/shard_map/ppermute | solution.py:665
  410.0 28.1 %collective-permute-start.61 = (bf16[992,512]{1,0:T(8,128)(2,1)S(1)}, bf16[992,512]{1,0:T(8,128)(2,1)S(1)}, u32[]{:S(2)}, u32[]{:S(2)}) collective-permute-start(bf16[992,512]{1,0:T(8,128)(2,1)S(1)} %broadcast_select_fusion), channel_id=1, source_target_pairs={{0,16},{16,0},{1,17},{17,1},{2,18},{18,2},{3,19},{19,3},{4,20},{20... | collective-permute-start | bytes 3047432 | tf_op jit(solution)/shard_map/ppermute | solution.py:636
  413.0 8.3 %collective-permute-start.58 = (bf16[480,256]{1,0:T(8,128)(2,1)S(1)}, bf16[480,256]{1,0:T(8,128)(2,1)S(1)}, u32[]{:S(2)}, u32[]{:S(2)}) collective-permute-start(bf16[480,256]{1,0:T(8,128)(2,1)S(1)} %bitcast.239), channel_id=1, source_target_pairs={{0,4},{4,8},{8,12},{12,0},{1,5},{5,9},{9,13},{13,1},{2,6},{6,10},{... | collective-permute-start | bytes 737288 | tf_op jit(solution)/shard_map/ppermute | solution.py:665
  414.9 23.0 %collective-permute-start.59 = (bf16[480,256]{1,0:T(8,128)(2,1)S(1)}, bf16[480,256]{1,0:T(8,128)(2,1)S(1)}, u32[]{:S(2)}, u32[]{:S(2)}) collective-permute-start(bf16[480,256]{1,0:T(8,128)(2,1)S(1)} %bitcast.237), channel_id=1, source_target_pairs={{0,8},{4,12},{8,0},{12,4},{1,9},{5,13},{9,1},{13,5},{2,10},{6,14},... | collective-permute-start | bytes 737288 | tf_op jit(solution)/shard_map/ppermute | solution.py:665
  418.0 19.9 %collective-permute-start.60 = (bf16[480,256]{1,0:T(8,128)(2,1)S(1)}, bf16[480,256]{1,0:T(8,128)(2,1)S(1)}, u32[]{:S(2)}, u32[]{:S(2)}) collective-permute-start(bf16[480,256]{1,0:T(8,128)(2,1)S(1)} %bitcast.236), channel_id=1, source_target_pairs={{0,12},{4,0},{8,4},{12,8},{1,13},{5,1},{9,5},{13,9},{2,14},{6,2},{... | collective-permute-start | bytes 737288 | tf_op jit(solution)/shard_map/ppermute | solution.py:665
  440.2 5.9 %collective-permute-start.62 = (bf16[496,256]{1,0:T(8,128)(2,1)S(1)}, bf16[496,256]{1,0:T(8,128)(2,1)S(1)}, u32[]{:S(2)}, u32[]{:S(2)}) collective-permute-start(bf16[496,256]{1,0:T(8,128)(2,1)S(1)} %pad_maximum_fusion.4), channel_id=1, source_target_pairs={{0,4},{4,8},{8,12},{12,0},{1,5},{5,9},{9,13},{13,1},{2,6},{6,10},{... | collective-permute-start | bytes 761864 | tf_op jit(solution)/shard_map/ppermute | solution.py:665
  440.3 23.6 %collective-permute-start.63 = (bf16[496,256]{1,0:T(8,128)(2,1)S(1)}, bf16[496,256]{1,0:T(8,128)(2,1)S(1)}, u32[]{:S(2)}, u32[]{:S(2)}) collective-permute-start(bf16[496,256]{1,0:T(8,128)(2,1)S(1)} %pad_maximum_fusion.5), channel_id=1, source_target_pairs={{0,8},{4,12},{8,0},{12,4},{1,9},{5,13},{9,1},{13,5},{2,10},{6,14},... | collective-permute-start | bytes 761864 | tf_op jit(solution)/shard_map/ppermute | solution.py:665
  442.1 21.8 %collective-permute-start.64 = (bf16[496,256]{1,0:T(8,128)(2,1)S(1)}, bf16[496,256]{1,0:T(8,128)(2,1)S(1)}, u32[]{:S(2)}, u32[]{:S(2)}) collective-permute-start(bf16[496,256]{1,0:T(8,128)(2,1)S(1)} %pad_maximum_fusion.6), channel_id=1, source_target_pairs={{0,12},{4,0},{8,4},{12,8},{1,13},{5,1},{9,5},{13,9},{2,14},{6,2},{... | collective-permute-start | bytes 761864 | tf_op jit(solution)/shard_map/ppermute | solution.py:665
  (59 other events, 638.7 us)
where the time goes:
time: 475 us; the launch traced here: 469 us
  waiting for transfers between devices  170 us (36%)
  Pallas kernels  143 us (30%)
  starting transfers between devices  79.4 us (17%)
  other arithmetic  49.7 us (10%)
  local copies, waits for them, and re-layouts  25.1 us (5%)
    pallas_call x16, Pallas kernels, run(): pl.pallas_call(kernel, grid=grid, in_specs=[spec(a.shape) for a, spec in...  143 us
    ppermute x12, waiting for transfers between devices, rows_over_dp(): lax.ppermute(part, 'dp', [(i, (i + shift) % count) for i in range(count)])  57.2 us
    ppermute x9, waiting for transfers between devices, summed_over_dp(): lax.ppermute(share(me + shift), 'dp', [(i, (i + shift) % count) for i in...  50.6 us
    convert_element_type x11, other arithmetic, add(): return (left.astype(F32) + right.astype(F32)).astype(BF16)  24.9 us
    ppermute x12, starting transfers between devices, rows_over_dp(): lax.ppermute(part, 'dp', [(i, (i + shift) % count) for i in range(count)])  19.7 us
    ppermute x11, waiting for transfers between devices, across_tensor(): return lax.ppermute(part, 'tensor', tensor_pairs(2))  19.5 us
    ppermute x9, waiting for transfers between devices, across_section(): return lax.ppermute(part, 'section', [(0, 1), (1, 0)])  18 us
    ppermute x21, starting transfers between devices, beside_tensor(): return lax.ppermute(part, 'tensor', tensor_pairs(1))  16.8 us
  transfers between devices with their start and end apart: 66, of which 28 were waited for; matrix products, arithmetic and copies ran while one was open for 11% of the time, Pallas kernels for 25%

commit v1 on v0

--- a/solution.py
+++ b/solution.py
@@ -431,6 +431,10 @@
     return pl.BlockSpec(memory_space=pltpu.HBM)
 
 
+def resident(shape):
+    return pl.BlockSpec(memory_space=pltpu.VMEM)
+
+
 def scalars(shape):
     return pl.BlockSpec(memory_space=pltpu.SMEM)
 
@@ -618,7 +622,7 @@
     place = lax.axis_index("dp").astype(jnp.int32).reshape(1)
     return run(
         functools.partial(assemble_kernel, cuts), (),
-        [(place, scalars)] + [(piece, anywhere) for piece in pieces],
+        [(place, scalars)] + [(piece, resident) for piece in pieces],
         [(lead + (count * rows, columns), part.dtype, anywhere) for _, rows in cuts],
         [pltpu.SemaphoreType.DMA((count, len(cuts)))],
     )
@@ -754,15 +758,21 @@
     places = jnp.arange(length, dtype=jnp.int32)
     before = jnp.concatenate([own_segments[:1] - 1, own_segments[:-1]])
     starts = lax.cummax(jnp.where(own_segments != before, places, 0), axis=0)
-    positions = lax.dynamic_slice_in_dim(places - starts, place * rows, rows, 0)
     inverse = jnp.exp(-jnp.log(10000.0) * jnp.arange(HALF, dtype=F32) / HALF)
-    angle = positions.astype(F32)[:, None] * inverse[None, :]
+
+    def tables(block):
+        positions = lax.dynamic_slice_in_dim(places - starts, block * rows, rows, 0)
+        angle = positions.astype(F32)[:, None] * inverse[None, :]
+        return jnp.cos(angle), jnp.sin(angle)
+
+    tables_before = tables(jnp.maximum(place - 1, 0))
     here = lax.dynamic_slice_in_dim(own_segments, place * rows, rows, 0)
     padded = jnp.concatenate([jnp.full((rows,), -1, jnp.int32), own_segments])
     prior = lax.dynamic_slice_in_dim(padded, place * rows, rows, 0)
-    common = (jnp.cos(angle), jnp.sin(angle), here[:, None], here[None, :], prior[None, :])
+    common = (*tables(place), here[:, None], here[None, :], prior[None, :])
 
     x0 = lax.dynamic_index_in_dim(section_input, section, 0, keepdims=False)
+    x_before = halo_on(x0)
     grad = lax.dynamic_index_in_dim(cotangent, section, 0, keepdims=False)
     count = lax.axis_size("dp")
 
@@ -780,20 +790,21 @@
 
     whole_cut = ((0, local),)
     gathered0 = rows_over_dp(shared_l[0], cuts)
-    feed_in, qo_mine, kvw0, rows0, x0 = after((feeds[0], *gathered0, x0))
+    feed_in, qo_mine, kvw0, rows0, x0, x_before = after((feeds[0], *gathered0, x0, x_before))
     qo_across = across_tensor(qo_mine)
     feed_a = rows_over_dp(feed_in, whole_cut)[0]
     small0 = small_of((qo_mine, kvw0, rows0))
-    feed_a, feed_in, qo_across, small0 = after((feed_a, feeds[1], qo_across, small0))
+    other_a, mine_a = across_section(feed_a), across_tensor(feed_a)
+    feed_in, qo_across, small0 = after((feeds[1], qo_across, small0), feed_a)
     keys0 = forward_keys(x0, small0, common)
-    other_a, mine_a = across_section(feed_a), across_tensor(feed_a)
+    prev0 = forward_keys(x_before, small0, tables_before)[2]
     feed_b = rows_over_dp(feed_in, whole_cut)[0]
-    prev0 = halo_on(keys0[2])
-    other_a, mine_a, feed_b = after((other_a, mine_a, feed_b))
+    other_a, mine_a, feed_b, qo_mine, qo_across, keys0, prev0 = after(
+        (other_a, mine_a, feed_b, qo_mine, qo_across, keys0, prev0)
+    )
     qo0 = [beside_tensor(qo_mine), beside_tensor(qo_across), qo_mine, qo_across]
     other_b, mine_b = across_section(feed_b), across_tensor(feed_b)
     keys0 = (*keys0, prev0)
-    qo0, keys0 = after((qo0, keys0))
     beside_a = [beside_tensor(part) for part in (feed_a, mine_a, other_a)]
     attended0 = forward_attend(x0, keys0, small0, choices[0], qo0, common)
     other_a, other_b, mine_b, beside_a, attended0, shared1 = after(
@@ -835,7 +846,7 @@
     next1 = halo_back(at1[3])
     qo1_core = beside_tensor(at1[0])
     sums1 = [kept_sums(ff1_core, ff1[1], half) for half in range(2)]
-    next1, qo1_core, sums1 = after((next1, qo1_core, sums1))
+    next1, sums1 = after((next1, sums1))
     across1a = across_tensor(sums1[0][0])
     kv1, grad1, grad1_low, gain1, key1 = backward_keys(
         x1, at1[2], next1, keys1, small1, at1[4], ff1[2], common

time: 475 us -> 473 us (level)
  starting transfers between devices: 79.4 us -> 71 us
    ppermute x9, waiting for transfers between devices: 18 us -> 24 us  [across_section(): return lax.ppermute(part, 'section', [(0, 1), (1, 0)])]
    unnamed x119 -> x143, local copies, waits for them, and re-layouts: 13 us -> 18 us
    pallas_call x16 -> x17, Pallas kernels: 143 us -> 142 us  [run(): pl.pallas_call(kernel, grid=grid, in_specs=[spec(a.shape) for a, spec in...]
  transfers between devices with their start and end apart: 66 -> 66, of which waited for: 28 -> 27; matrix products, arithmetic and copies ran while one was open for 11% -> 10% of each run, Pallas kernels for 25% -> 26%
where the time goes in v1:
time: 473 us; the launch traced here: 464 us
  waiting for transfers between devices  172 us (36%)
  Pallas kernels  142 us (30%)
  starting transfers between devices  71 us (15%)
  other arithmetic  51.1 us (11%)
  local copies, waits for them, and re-layouts  26 us (5%)
    pallas_call x17, Pallas kernels, run(): pl.pallas_call(kernel, grid=grid, in_specs=[spec(a.shape) for a, spec in...  142 us
    ppermute x12, waiting for transfers between devices, rows_over_dp(): lax.ppermute(part, 'dp', [(i, (i + shift) % count) for i in range(count)])  60.9 us
    ppermute x9, waiting for transfers between devices, summed_over_dp(): lax.ppermute(share(me + shift), 'dp', [(i, (i + shift) % count) for i in...  48.1 us
    convert_element_type x11, other arithmetic, add(): return (left.astype(F32) + right.astype(F32)).astype(BF16)  26.9 us
    ppermute x9, waiting for transfers between devices, across_section(): return lax.ppermute(part, 'section', [(0, 1), (1, 0)])  24 us
    ppermute x12, starting transfers between devices, rows_over_dp(): lax.ppermute(part, 'dp', [(i, (i + shift) % count) for i in range(count)])  21.5 us
    ppermute x11, waiting for transfers between devices, across_tensor(): return lax.ppermute(part, 'tensor', tensor_pairs(2))  18.1 us
    unnamed x143, local copies, waits for them, and re-layouts  18 us
  transfers between devices with their start and end apart: 66, of which 27 were waited for; matrix products, arithmetic and copies ran while one was open for 10% of the time, Pallas kernels for 26%

profile of v1, /device:TPU:27, one launch (start us, length us, event | category | flops | bytes accessed | tf_op | source)
XLA Modules:
  0.0 464.1 jit_solution(11498696879354709284)
XLA Ops:
  3.7 4.0 collective-permute-start.4
  12.4 4.6 collective-permute-done.1.refs_1_
  17.0 16.7 %collective-permute-done.2.refs_2_ = bf16[256,512]{1,0:T(8,128)(2,1)S(1)} collective-permute-done((bf16[256,512]{1,0:T(8,128)(2,1)S(1)}, bf16[256,512]{1,0:T(8,128)(2,1)S(1)}, u32[]{:S(2)}, u32[]{:S(2)}) %collective-permute-start.2) | collective-permute-done | bytes 262176 | tf_op jit(solution)/shard_map/ppermute | solution.py:619
  36.6 3.1 collective-permute-start.6
  39.7 1.4 collective-permute-start.7
  41.1 1.9 multiply_sine_fusion
  43.0 1.4 collective-permute-start.11
  46.0 15.3 %collective-permute-done.6.refs_2_ = bf16[3,160,256]{2,1,0:T(8,128)(2,1)S(1)} collective-permute-done((bf16[3,160,256]{2,1,0:T(8,128)(2,1)S(1)}, bf16[3,160,256]{2,1,0:T(8,128)(2,1)S(1)}, u32[]{:S(2)}, u32[]{:S(2)}) %collective-permute-start.6) | collective-permute-done | bytes 245792 | tf_op jit(solution)/shard_map/ppermute | solution.py:619
  61.3 1.4 shard_map.204.refs_4_
  65.7 1.4 collective-permute-start.14
  67.1 2.5 shard_map.207
  72.1 14.6 %collective-permute-done.13.refs_2_ = bf16[3,160,256]{2,1,0:T(8,128)(2,1)S(1)} collective-permute-done((bf16[3,160,256]{2,1,0:T(8,128)(2,1)S(1)}, bf16[3,160,256]{2,1,0:T(8,128)(2,1)S(1)}, u32[]{:S(2)}, u32[]{:S(2)}) %collective-permute-start.13) | collective-permute-done | bytes 245792 | tf_op jit(solution)/shard_map/ppermute | solution.py:619
  90.1 1.7 collective-permute-start.20
  98.4 11.0 %shard_map.208 = (f32[4,512,256]{2,1,0:T(8,128)}, bf16[4,512,256]{2,1,0:T(8,128)(2,1)}, bf16[4,512,256]{2,1,0:T(8,128)(2,1)}, f32[4,512,1]{2,1,0:T(8,128)}, f32[...) custom-call(s32[1]{0:T(128)} %bitcast.choice, ...), custom_call_target="tpu_custom_call" | custom-call | flops 16142000128 | bytes 1 | tf_op jit(solution)/shard_map/pallas_call | solution.py:464
  110.2 7.4 %collective-permute-done.15.refs_13_ = bf16[3,640,256]{2,1,0:T(8,128)(2,1)} collective-permute-done((bf16[3,640,256]{2,1,0:T(8,128)(2,1)}, bf16[3,640,256]{2,1,0:T(8,128)(2,1)}, u32[]{:S(2)}, u32[]{:S(2)}) %collective-permute-start.15) | collective-permute-done | bytes 983072 | tf_op jit(solution)/shard_map/ppermute | solution.py:640
  120.4 1.7 collective-permute-start.25
  122.0 12.1 %collective-permute-start.26 = (bf16[256,512]{1,0:T(8,128)(2,1)S(1)}, bf16[256,512]{1,0:T(8,128)(2,1)S(1)}, u32[]{:S(2)}, u32[]{:S(2)}) collective-permute-start(bf16[256,512]{1,0:T(8,128)(2,1)S(1)} %get-tuple-element.236.refs_0_), channel_id=1, source_target_pairs={{0,12},{4,0},{8,4},{12,8},{1,13},{5,1},{9,5},{13,9},{2,14},{6,2},{... | collective-permute-start | bytes 786440 | tf_op jit(solution)/shard_map/ppermute | solution.py:619
  134.2 9.6 %collective-permute-done.25.refs_2_ = bf16[256,512]{1,0:T(8,128)(2,1)S(1)} collective-permute-done((bf16[256,512]{1,0:T(8,128)(2,1)S(1)}, bf16[256,512]{1,0:T(8,128)(2,1)S(1)}, u32[]{:S(2)}, u32[]{:S(2)}) %collective-permute-start.25) | collective-permute-done | bytes 262176 | tf_op jit(solution)/shard_map/ppermute | solution.py:619
  145.0 2.4 collective-permute-start.32
  151.8 1.4 collective-permute-done.29.refs_9_
  153.2 1.4 collective-permute-done.30.refs_10_
  154.7 1.4 collective-permute-done.31.refs_11_
  158.5 11.8 %shard_map.210 = (bf16[4,512,512]{2,1,0:T(8,128)(2,1)}, bf16[4,512,512]{2,1,0:T(8,128)(2,1)}, f32[512,640]{1,0:T(8,128)}, f32[512,640]{1,0:T(8,128)}, bf16[512,640]{1,0:T(8,128)(2,1)S(1)}) custom-call(s32[1]{0:T(128)} %bitcast.choice, bf16[512,640]{1,0:T(8,128)(2,1)S(1)} %copy-done.29, f32[512,640]{1,0:T(8,128)} %get-tuple-element.231.middle, ...), custom_call_target="tpu_custom_call" | custom-call | flops 13836000256 | bytes 1 | tf_op jit(solution)/shard_map/pallas_call | solution.py:464
  173.5 2.5 collective-permute-start.34
  177.2 4.9 %collective-permute-done.34.prev = bf16[512,512]{1,0:T(8,128)(2,1)S(1)} collective-permute-done((bf16[512,512]{1,0:T(8,128)(2,1)S(1)}, bf16[512,512]{1,0:T(8,128)(2,1)S(1)}, u32[]{:S(2)}, u32[]{:S(2)}) %collective-permute-start.34) | collective-permute-done | bytes 524320 | tf_op jit(solution)/shard_map/ppermute | solution.py:500
  183.2 11.0 %shard_map.212 = (f32[4,512,256]{2,1,0:T(8,128)}, bf16[4,512,256]{2,1,0:T(8,128)(2,1)}, bf16[4,512,256]{2,1,0:T(8,128)(2,1)}, f32[4,512,1]{2,1,0:T(8,128)}, f32[...) custom-call(s32[1]{0:T(128)} %bitcast.27.choice, bf16[512,640]{1,0:T(8,128)(2,1)S(1)} %get-tuple-element.262.x, ...), custom_call_target="tpu_custom_call" | custom-call | flops 16142000128 | bytes 1 | tf_op jit(solution)/shard_map/pallas_call | solution.py:464
  194.3 11.7 %shard_map.213 = (bf16[4,512,512]{2,1,0:T(8,128)(2,1)}, bf16[4,512,512]{2,1,0:T(8,128)(2,1)}, f32[512,640]{1,0:T(8,128)}, f32[512,640]{1,0:T(8,128)}, bf16[512,640]{1,0:T(8,128)(2,1)S(1)}) custom-call(s32[1]{0:T(128)} %bitcast.27.choice, bf16[512,640]{1,0:T(8,128)(2,1)S(1)} %get-tuple-element.269.normed_two, f32[512,640]{1,0:T(8,128)} %get-tuple-element.270.middle, ...), custom_call_target="tpu_custom_call" | custom-call | flops 13836000256 | bytes 1 | tf_op jit(solution)/shard_map/pallas_call | solution.py:464
  206.1 1.4 collective-permute-start.37
  207.5 22.7 %shard_map.214 = (bf16[2,2,3,640,256]{4,3,2,1,0:T(8,128)(2,1)}, bf16[2,2,3,640,256]{4,3,2,1,0:T(8,128)(2,1)}, f32[512,640]{1,0:T(8,128)}, bf16[512,640]{1,0:T(8,128)(2,1)S(1)}, f32[4,640]{1,0:T(4,128)S(1)}) custom-call(s32[1]{0:T(128)} %bitcast.27.choice, bf16[512,640]{1,0:T(8,128)(2,1)S(1)} %dynamic-slice_bitcast_fusion.grad, ...), custom_call_target="tpu_custom_call" | custom-call | flops 28824999936 | bytes 1 | tf_op jit(solution)/shard_map/pallas_call | solution.py:464
  230.4 16.1 %shard_map.215 = (bf16[2,640,512]{2,1,0:T(8,128)(2,1)}, bf16[2,640,512]{2,1,0:T(8,128)(2,1)}, f32[512,512]{1,0:T(8,128)}, bf16[512,512]{1,0:T(8,128)(2,1)S(1)}, ...) custom-call(s32[1]{0:T(128)} %bitcast.27.choice, bf16[512,640]{1,0:T(8,128)(2,1)S(1)} %get-tuple-element.283.grad_branch, ...), custom_call_target="tpu_custom_call" | custom-call | flops 19601000448 | bytes 1 | tf_op jit(solution)/shard_map/pallas_call | solution.py:464
  246.6 2.2 collective-permute-start.39
  248.9 4.4 fusion.9
  253.2 4.8 %collective-permute-done.39.kv_next = bf16[512,512]{1,0:T(8,128)(2,1)S(1)} collective-permute-done((bf16[512,512]{1,0:T(8,128)(2,1)S(1)}, bf16[512,512]{1,0:T(8,128)(2,1)S(1)}, u32[]{:S(2)}, u32[]{:S(2)}) %collective-permute-start.39) | collective-permute-done | bytes 524320 | tf_op jit(solution)/shard_map/ppermute | solution.py:600
  258.1 5.1 %shard_map.216 = (bf16[640,512]{1,0:T(8,128)(2,1)S(1)}, f32[512,640]{1,0:T(8,128)}, bf16[512,640]{1,0:T(8,128)(2,1)S(1)}, f32[1,640]{1,0:T(1,128)S(1)}, f32[1,256]{1,0:T(1,128)S(1)}) custom-call(f32[512,512]{1,0:T(8,128)} %get-tuple-element.299.kv_own, bf16[512,512]{1,0:T(8,128)(2,1)S(1)} %collective-permute-done.39.kv_next, ...), custom_call_target="tpu_custom_call" | custom-call | flops 5765000192 | bytes 1 | tf_op jit(solution)/shard_map/pallas_call | solution.py:464
  263.2 23.3 %shard_map.217 = (bf16[2,2,3,640,256]{4,3,2,1,0:T(8,128)(2,1)}, bf16[2,2,3,640,256]{4,3,2,1,0:T(8,128)(2,1)}, f32[512,640]{1,0:T(8,128)}, bf16[512,640]{1,0:T(8,128)(2,1)S(1)}, f32[4,640]{1,0:T(4,128)S(1)}) custom-call(s32[1]{0:T(128)} %bitcast.choice, bf16[512,640]{1,0:T(8,128)(2,1)S(1)} %get-tuple-element.304.grad, ...), custom_call_target="tpu_custom_call" | custom-call | flops 28824999936 | bytes 1 | tf_op jit(solution)/shard_map/pallas_call | solution.py:464
  292.3 15.9 %shard_map.218 = (bf16[2,640,512]{2,1,0:T(8,128)(2,1)}, bf16[2,640,512]{2,1,0:T(8,128)(2,1)}, f32[512,512]{1,0:T(8,128)}, bf16[512,512]{1,0:T(8,128)(2,1)S(1)}, ...) custom-call(s32[1]{0:T(128)} %bitcast.choice, bf16[512,640]{1,0:T(8,128)(2,1)S(1)} %copy-done.32, ...), custom_call_target="tpu_custom_call" | custom-call | flops 19601000448 | bytes 1 | tf_op jit(solution)/shard_map/pallas_call | solution.py:464
  308.2 2.8 fusion.19
  311.0 2.5 add_convert_fusion.7
  313.6 2.6 collective-permute-start.44
  317.9 4.8 %fusion.13 = (bf16[3,640,256]{2,1,0:T(8,128)(2,1)}, bf16[3,640,256]{2,1,0:T(8,128)(2,1)}, bf16[3,640,256]{2,1,0:T(8,128)(2,1)}, bf16[3,640,256]{2,1,0:T(8,128)(2,1)}) fusion(bf16[2,2,3,640,256]{4,3,2,1,0:T(8,128)(2,1)} %collective-permute-done.42, bf16[2,2,3,640,256]{4,3,2,1,0:T(8,128)(2,1)S(1)} %copy-done.40), kind=kLoop, calls=%fused_computation.44 | loop fusion | flops 7864320 | bytes 11796480 | tf_op jit(solution)/shard_map/convert_element_type | solution.py:648
  325.4 3.9 collective-permute-done.44.kv_next
  329.3 5.1 %shard_map.219 = (bf16[640,512]{1,0:T(8,128)(2,1)S(1)}, f32[512,640]{1,0:T(8,128)}, bf16[512,640]{1,0:T(8,128)(2,1)S(1)}, f32[1,640]{1,0:T(1,128)S(1)}, f32[1,256]{1,0:T(1,128)S(1)}) custom-call(f32[512,512]{1,0:T(8,128)} %get-tuple-element.334.kv_own, bf16[512,512]{1,0:T(8,128)(2,1)S(1)} %collective-permute-done.44.kv_next, f32[512,256]{1,0:T(8,128)S(1)} %copy-done.22, ...), custom_call_target="tpu_custom_call" | custom-call | flops 5765000192 | bytes 1 | tf_op jit(solution)/shard_map/pallas_call | solution.py:464
  337.2 2.6 fusion.21
  339.8 14.6 %collective-permute-done.45 = bf16[3,640,256]{2,1,0:T(8,128)(2,1)} collective-permute-done((bf16[3,640,256]{2,1,0:T(8,128)(2,1)}, bf16[3,640,256]{2,1,0:T(8,128)(2,1)}, u32[]{:S(2)}, u32[]{:S(2)}) %collective-permute-start.45) | collective-permute-done | bytes 983072 | tf_op jit(solution)/shard_map/ppermute | solution.py:632
  355.3 1.7 broadcast_select_fusion.2
  358.4 16.3 %collective-permute-done.52 = bf16[3,640,256]{2,1,0:T(8,128)(2,1)S(1)} collective-permute-done((bf16[3,640,256]{2,1,0:T(8,128)(2,1)S(1)}, bf16[3,640,256]{2,1,0:T(8,128)(2,1)S(1)}, u32[]{:S(2)}, u32[]{:S(2)}) %collective-permute-start.52) | collective-permute-done | bytes 983072 | tf_op jit(solution)/shard_map/ppermute | solution.py:640
  374.7 2.7 add_convert_fusion.4
  378.9 1.5 constant_dynamic-slice_fusion.8
  382.0 1.6 fusion.2
  383.7 2.5 collective-permute-done.54
  386.2 13.6 %collective-permute-done.55 = bf16[480,256]{1,0:T(8,128)(2,1)S(1)} collective-permute-done((bf16[480,256]{1,0:T(8,128)(2,1)S(1)}, bf16[480,256]{1,0:T(8,128)(2,1)S(1)}, u32[]{:S(2)}, u32[]{:S(2)}) %collective-permute-start.55) | collective-permute-done | bytes 245792 | tf_op jit(solution)/shard_map/ppermute | solution.py:669
  400.0 1.8 add_convert_fusion.2
  401.8 2.3 collective-permute-done.53
  405.3 1.6 broadcast_select_fusion
  406.9 2.2 collective-permute-start.61
  409.1 1.7 maximum_bitcast_fusion
  413.1 1.7 maximum_bitcast_fusion.1
  414.7 2.5 collective-permute-done.58
  417.3 12.6 %collective-permute-done.59 = bf16[480,256]{1,0:T(8,128)(2,1)S(1)} collective-permute-done((bf16[480,256]{1,0:T(8,128)(2,1)S(1)}, bf16[480,256]{1,0:T(8,128)(2,1)S(1)}, u32[]{:S(2)}, u32[]{:S(2)}) %collective-permute-start.59) | collective-permute-done | bytes 245792 | tf_op jit(solution)/shard_map/ppermute | solution.py:669
  430.0 1.8 add_convert_fusion
  432.9 4.4 collective-permute-start.63
  437.4 1.5 collective-permute-start.64
  441.4 16.9 %collective-permute-done.63 = bf16[496,256]{1,0:T(8,128)(2,1)S(1)} collective-permute-done((bf16[496,256]{1,0:T(8,128)(2,1)S(1)}, bf16[496,256]{1,0:T(8,128)(2,1)S(1)}, u32[]{:S(2)}, u32[]{:S(2)}) %collective-permute-start.63) | collective-permute-done | bytes 253984 | tf_op jit(solution)/shard_map/ppermute | solution.py:669
  458.4 2.5 collective-permute-start.65
  (343 shorter events, 73.1 us)
Async XLA Ops:
  3.3 7.2 %collective-permute-start = (bf16[256,512]{1,0:T(8,128)(2,1)S(1)}, bf16[256,512]{1,0:T(8,128)(2,1)S(1)}, u32[]{:S(2)}, u32[]{:S(2)}) collective-permute-start(bf16[256,512]{1,0:T(8,128)(2,1)S(1)} %fusion.31), channel_id=1, source_target_pairs={{0,16},{16,0},{1,17},{17,1},{2,18},{18,2},{3,19},{19,3},{4,20},{20... | collective-permute-start | bytes 786440 | tf_op jit(solution)/shard_map/ppermute | solution.py:640
  3.7 32.8 %collective-permute-start.4 = (bf16[512,640]{1,0:T(8,128)(2,1)S(1)}, bf16[512,640]{1,0:T(8,128)(2,1)}, u32[]{:S(2)}, u32[]{:S(2)}) collective-permute-start(bf16[512,640]{1,0:T(8,128)(2,1)S(1)} %dynamic-slice_bitcast_fusion.1.x), channel_id=1, source_target_pairs={{0,1},{1,2},{2,3},{4,5},{5,6},{6,7},{8,9},{9,10},{10,11},{12,13},{... | collective-permute-start | bytes 1966088 | tf_op jit(solution)/shard_map/ppermute | solution.py:500
  10.7 6.3 %collective-permute-start.1 = (bf16[256,512]{1,0:T(8,128)(2,1)S(1)}, bf16[256,512]{1,0:T(8,128)(2,1)S(1)}, u32[]{:S(2)}, u32[]{:S(2)}) collective-permute-start(bf16[256,512]{1,0:T(8,128)(2,1)S(1)} %get-tuple-element.428.refs_0_), channel_id=1, source_target_pairs={{0,4},{4,8},{8,12},{12,0},{1,5},{5,9},{9,13},{13,1},{2,6},{6,10},{... | collective-permute-start | bytes 786440 | tf_op jit(solution)/shard_map/ppermute | solution.py:619
  10.7 23.0 %collective-permute-start.2 = (bf16[256,512]{1,0:T(8,128)(2,1)S(1)}, bf16[256,512]{1,0:T(8,128)(2,1)S(1)}, u32[]{:S(2)}, u32[]{:S(2)}) collective-permute-start(bf16[256,512]{1,0:T(8,128)(2,1)S(1)} %get-tuple-element.428.refs_0_), channel_id=1, source_target_pairs={{0,8},{4,12},{8,0},{12,4},{1,9},{5,13},{9,1},{13,5},{2,10},{6,14},... | collective-permute-start | bytes 786440 | tf_op jit(solution)/shard_map/ppermute | solution.py:619
  12.1 21.6 %collective-permute-start.3 = (bf16[256,512]{1,0:T(8,128)(2,1)S(1)}, bf16[256,512]{1,0:T(8,128)(2,1)S(1)}, u32[]{:S(2)}, u32[]{:S(2)}) collective-permute-start(bf16[256,512]{1,0:T(8,128)(2,1)S(1)} %get-tuple-element.428.refs_0_), channel_id=1, source_target_pairs={{0,12},{4,0},{8,4},{12,8},{1,13},{5,1},{9,5},{13,9},{2,14},{6,2},{... | collective-permute-start | bytes 786440 | tf_op jit(solution)/shard_map/ppermute | solution.py:619
  36.5 9.4 %collective-permute-start.5 = (bf16[3,160,256]{2,1,0:T(8,128)(2,1)S(1)}, bf16[3,160,256]{2,1,0:T(8,128)(2,1)S(1)}, u32[]{:S(2)}, u32[]{:S(2)}) collective-permute-start(bf16[3,160,256]{2,1,0:T(8,128)(2,1)S(1)} %pad_maximum_fusion.7.refs_0_), channel_id=1, source_target_pairs={{0,4},{4,8},{8,12},{12,0},{1,5},{5,9},{9,13},{13,1},{2,6},{6,10},{... | collective-permute-start | bytes 737288 | tf_op jit(solution)/shard_map/ppermute | solution.py:619
  36.6 24.7 %collective-permute-start.6 = (bf16[3,160,256]{2,1,0:T(8,128)(2,1)S(1)}, bf16[3,160,256]{2,1,0:T(8,128)(2,1)S(1)}, u32[]{:S(2)}, u32[]{:S(2)}) collective-permute-start(bf16[3,160,256]{2,1,0:T(8,128)(2,1)S(1)} %pad_maximum_fusion.7.refs_0_), channel_id=1, source_target_pairs={{0,8},{4,12},{8,0},{12,4},{1,9},{5,13},{9,1},{13,5},{2,10},{6,14},... | collective-permute-start | bytes 737288 | tf_op jit(solution)/shard_map/ppermute | solution.py:619
  39.7 21.6 %collective-permute-start.7 = (bf16[3,160,256]{2,1,0:T(8,128)(2,1)S(1)}, bf16[3,160,256]{2,1,0:T(8,128)(2,1)}, u32[]{:S(2)}, u32[]{:S(2)}) collective-permute-start(bf16[3,160,256]{2,1,0:T(8,128)(2,1)S(1)} %pad_maximum_fusion.7.refs_0_), channel_id=1, source_target_pairs={{0,12},{4,0},{8,4},{12,8},{1,13},{5,1},{9,5},{13,9},{2,14},{6,2},{... | collective-permute-start | bytes 737288 | tf_op jit(solution)/shard_map/ppermute | solution.py:619
  43.0 21.4 %collective-permute-start.11 = (bf16[320,512]{1,0:T(8,128)(2,1)S(1)}, bf16[320,512]{1,0:T(8,128)(2,1)}, u32[]{:S(2)}, u32[]{:S(2)}) collective-permute-start(bf16[320,512]{1,0:T(8,128)(2,1)S(1)} %get-tuple-element.202), channel_id=1, source_target_pairs={{0,1},{1,0},{2,3},{3,2},{4,5},{5,4},{6,7},{7,6},{8,9},{9,8},{10,11... | collective-permute-start | bytes 983048 | tf_op jit(solution)/shard_map/ppermute | solution.py:636
  44.4 21.1 %collective-permute-start.10 = (bf16[640,512]{1,0:T(8,128)(2,1)}, bf16[640,512]{1,0:T(8,128)(2,1)}, u32[]{:S(2)}, u32[]{:S(2)}) collective-permute-start(bf16[640,512]{1,0:T(8,128)(2,1)} %get-tuple-element.221.qo_c), channel_id=1, source_target_pairs={{0,2},{1,3},{2,0},{3,1},{4,6},{5,7},{6,4},{7,5},{8,10},{9,11},{10,... | collective-permute-start | bytes 1966088 | tf_op jit(solution)/shard_map/ppermute | solution.py:632
  62.7 25.4 %collective-permute-start.8 = (bf16[3,640,256]{2,1,0:T(8,128)(2,1)S(1)}, bf16[3,640,256]{2,1,0:T(8,128)(2,1)S(1)}, u32[]{:S(2)}, u32[]{:S(2)}) collective-permute-start(bf16[3,640,256]{2,1,0:T(8,128)(2,1)S(1)} %shard_map.204.refs_4_), channel_id=1, source_target_pairs={{0,16},{16,0},{1,17},{17,1},{2,18},{18,2},{3,19},{19,3},{4,20},{20... | collective-permute-start | bytes 2949128 | tf_op jit(solution)/shard_map/ppermute | solution.py:640
  63.7 24.4 %collective-permute-start.9 = (bf16[3,640,256]{2,1,0:T(8,128)(2,1)S(1)}, bf16[3,640,256]{2,1,0:T(8,128)(2,1)S(1)}, u32[]{:S(2)}, u32[]{:S(2)}) collective-permute-start(bf16[3,640,256]{2,1,0:T(8,128)(2,1)S(1)} %shard_map.204.refs_4_), channel_id=1, source_target_pairs={{0,2},{1,3},{2,0},{3,1},{4,6},{5,7},{6,4},{7,5},{8,10},{9,11},{10,... | collective-permute-start | bytes 2949128 | tf_op jit(solution)/shard_map/ppermute | solution.py:632
  65.5 6.6 %collective-permute-start.12 = (bf16[3,160,256]{2,1,0:T(8,128)(2,1)S(1)}, bf16[3,160,256]{2,1,0:T(8,128)(2,1)S(1)}, u32[]{:S(2)}, u32[]{:S(2)}) collective-permute-start(bf16[3,160,256]{2,1,0:T(8,128)(2,1)S(1)} %pad_maximum_fusion.8.refs_0_), channel_id=1, source_target_pairs={{0,4},{4,8},{8,12},{12,0},{1,5},{5,9},{9,13},{13,1},{2,6},{6,10},{... | collective-permute-start | bytes 737288 | tf_op jit(solution)/shard_map/ppermute | solution.py:619
  65.6 21.1 %collective-permute-start.13 = (bf16[3,160,256]{2,1,0:T(8,128)(2,1)S(1)}, bf16[3,160,256]{2,1,0:T(8,128)(2,1)S(1)}, u32[]{:S(2)}, u32[]{:S(2)}) collective-permute-start(bf16[3,160,256]{2,1,0:T(8,128)(2,1)S(1)} %pad_maximum_fusion.8.refs_0_), channel_id=1, source_target_pairs={{0,8},{4,12},{8,0},{12,4},{1,9},{5,13},{9,1},{13,5},{2,10},{6,14},... | collective-permute-start | bytes 737288 | tf_op jit(solution)/shard_map/ppermute | solution.py:619
  65.7 21.0 %collective-permute-start.14 = (bf16[3,160,256]{2,1,0:T(8,128)(2,1)S(1)}, bf16[3,160,256]{2,1,0:T(8,128)(2,1)S(1)}, u32[]{:S(2)}, u32[]{:S(2)}) collective-permute-start(bf16[3,160,256]{2,1,0:T(8,128)(2,1)S(1)} %pad_maximum_fusion.8.refs_0_), channel_id=1, source_target_pairs={{0,12},{4,0},{8,4},{12,8},{1,13},{5,1},{9,5},{13,9},{2,14},{6,2},{... | collective-permute-start | bytes 737288 | tf_op jit(solution)/shard_map/ppermute | solution.py:619
  90.1 5.5 %collective-permute-start.20 = (bf16[640,512]{1,0:T(8,128)(2,1)}, bf16[640,512]{1,0:T(8,128)(2,1)}, u32[]{:S(2)}, u32[]{:S(2)}) collective-permute-start(bf16[640,512]{1,0:T(8,128)(2,1)} %get-tuple-element.221.qo_c), channel_id=1, source_target_pairs={{0,1},{1,0},{2,3},{3,2},{4,5},{5,4},{6,7},{7,6},{8,9},{9,8},{10,11... | collective-permute-start | bytes 1966088 | tf_op jit(solution)/shard_map/ppermute | solution.py:636
  91.7 4.5 collective-permute-start.21
  93.5 16.7 %collective-permute-start.17 = (bf16[3,640,256]{2,1,0:T(8,128)(2,1)S(1)}, bf16[3,640,256]{2,1,0:T(8,128)(2,1)S(1)}, u32[]{:S(2)}, u32[]{:S(2)}) collective-permute-start(bf16[3,640,256]{2,1,0:T(8,128)(2,1)S(1)} %copy-done.7), channel_id=1, source_target_pairs={{0,1},{1,0},{2,3},{3,2},{4,5},{5,4},{6,7},{7,6},{8,9},{9,8},{10,11... | collective-permute-start | bytes 2949128 | tf_op jit(solution)/shard_map/ppermute | solution.py:636
  94.0 23.6 %collective-permute-start.15 = (bf16[3,640,256]{2,1,0:T(8,128)(2,1)}, bf16[3,640,256]{2,1,0:T(8,128)(2,1)}, u32[]{:S(2)}, u32[]{:S(2)}) collective-permute-start(bf16[3,640,256]{2,1,0:T(8,128)(2,1)} %copy-done.8), channel_id=1, source_target_pairs={{0,16},{16,0},{1,17},{17,1},{2,18},{18,2},{3,19},{19,3},{4,20},{20... | collective-permute-start | bytes 2949128 | tf_op jit(solution)/shard_map/ppermute | solution.py:640
  95.2 23.3 %collective-permute-start.16 = (bf16[3,640,256]{2,1,0:T(8,128)(2,1)}, bf16[3,640,256]{2,1,0:T(8,128)(2,1)}, u32[]{:S(2)}, u32[]{:S(2)}) collective-permute-start(bf16[3,640,256]{2,1,0:T(8,128)(2,1)} %copy-done.8), channel_id=1, source_target_pairs={{0,2},{1,3},{2,0},{3,1},{4,6},{5,7},{6,4},{7,5},{8,10},{9,11},{10,... | collective-permute-start | bytes 2949128 | tf_op jit(solution)/shard_map/ppermute | solution.py:632
  95.6 23.0 %collective-permute-start.18 = (bf16[3,640,256]{2,1,0:T(8,128)(2,1)}, bf16[3,640,256]{2,1,0:T(8,128)(2,1)S(1)}, u32[]{:S(2)}, u32[]{:S(2)}) collective-permute-start(bf16[3,640,256]{2,1,0:T(8,128)(2,1)} %copy-done.66), channel_id=1, source_target_pairs={{0,1},{1,0},{2,3},{3,2},{4,5},{5,4},{6,7},{7,6},{8,9},{9,8},{10,11... | collective-permute-start | bytes 2949128 | tf_op jit(solution)/shard_map/ppermute | solution.py:636
  96.2 22.4 %collective-permute-start.19 = (bf16[3,640,256]{2,1,0:T(8,128)(2,1)}, bf16[3,640,256]{2,1,0:T(8,128)(2,1)S(1)}, u32[]{:S(2)}, u32[]{:S(2)}) collective-permute-start(bf16[3,640,256]{2,1,0:T(8,128)(2,1)} %copy-done.64), channel_id=1, source_target_pairs={{0,1},{1,0},{2,3},{3,2},{4,5},{5,4},{6,7},{7,6},{8,9},{9,8},{10,11... | collective-permute-start | bytes 2949128 | tf_op jit(solution)/shard_map/ppermute | solution.py:636
  118.6 26.4 %collective-permute-start.22 = (bf16[3,640,256]{2,1,0:T(8,128)(2,1)S(1)}, bf16[3,640,256]{2,1,0:T(8,128)(2,1)}, u32[]{:S(2)}, u32[]{:S(2)}) collective-permute-start(bf16[3,640,256]{2,1,0:T(8,128)(2,1)S(1)} %copy-done.65), channel_id=1, source_target_pairs={{0,2},{1,3},{2,0},{3,1},{4,6},{5,7},{6,4},{7,5},{8,10},{9,11},{10,... | collective-permute-start | bytes 2949128 | tf_op jit(solution)/shard_map/ppermute | solution.py:632
  119.2 25.8 %collective-permute-start.23 = (bf16[3,640,256]{2,1,0:T(8,128)(2,1)}, bf16[3,640,256]{2,1,0:T(8,128)(2,1)}, u32[]{:S(2)}, u32[]{:S(2)}) collective-permute-start(bf16[3,640,256]{2,1,0:T(8,128)(2,1)} %collective-permute-done.16.refs_7_), channel_id=1, source_target_pairs={{0,16},{16,0},{1,17},{17,1},{2,18},{18,2},{3,19},{19,3},{4,20},{20... | collective-permute-start | bytes 2949128 | tf_op jit(solution)/shard_map/ppermute | solution.py:640
  120.4 13.8 %collective-permute-start.24 = (bf16[256,512]{1,0:T(8,128)(2,1)S(1)}, bf16[256,512]{1,0:T(8,128)(2,1)S(1)}, u32[]{:S(2)}, u32[]{:S(2)}) collective-permute-start(bf16[256,512]{1,0:T(8,128)(2,1)S(1)} %get-tuple-element.236.refs_0_), channel_id=1, source_target_pairs={{0,4},{4,8},{8,12},{12,0},{1,5},{5,9},{9,13},{13,1},{2,6},{6,10},{... | collective-permute-start | bytes 786440 | tf_op jit(solution)/shard_map/ppermute | solution.py:619
  120.4 23.4 %collective-permute-start.25 = (bf16[256,512]{1,0:T(8,128)(2,1)S(1)}, bf16[256,512]{1,0:T(8,128)(2,1)S(1)}, u32[]{:S(2)}, u32[]{:S(2)}) collective-permute-start(bf16[256,512]{1,0:T(8,128)(2,1)S(1)} %get-tuple-element.236.refs_0_), channel_id=1, source_target_pairs={{0,8},{4,12},{8,0},{12,4},{1,9},{5,13},{9,1},{13,5},{2,10},{6,14},... | collective-permute-start | bytes 786440 | tf_op jit(solution)/shard_map/ppermute | solution.py:619
  122.0 21.7 %collective-permute-start.26 = (bf16[256,512]{1,0:T(8,128)(2,1)S(1)}, bf16[256,512]{1,0:T(8,128)(2,1)S(1)}, u32[]{:S(2)}, u32[]{:S(2)}) collective-permute-start(bf16[256,512]{1,0:T(8,128)(2,1)S(1)} %get-tuple-element.236.refs_0_), channel_id=1, source_target_pairs={{0,12},{4,0},{8,4},{12,8},{1,13},{5,1},{9,5},{13,9},{2,14},{6,2},{... | collective-permute-start | bytes 786440 | tf_op jit(solution)/shard_map/ppermute | solution.py:619
  145.0 3.7 collective-permute-start.32
  147.5 4.3 collective-permute-start.28
  147.9 5.3 %collective-permute-start.29 = (bf16[3,640,256]{2,1,0:T(8,128)(2,1)}, bf16[3,640,256]{2,1,0:T(8,128)(2,1)}, u32[]{:S(2)}, u32[]{:S(2)}) collective-permute-start(bf16[3,640,256]{2,1,0:T(8,128)(2,1)} %collective-permute-done.15.refs_13_), channel_id=1, source_target_pairs={{0,1},{1,0},{2,3},{3,2},{4,5},{5,4},{6,7},{7,6},{8,9},{9,8},{10,11... | collective-permute-start | bytes 2949128 | tf_op jit(solution)/shard_map/ppermute | solution.py:636
  148.0 6.6 %collective-permute-start.30 = (bf16[3,640,256]{2,1,0:T(8,128)(2,1)}, bf16[3,640,256]{2,1,0:T(8,128)(2,1)}, u32[]{:S(2)}, u32[]{:S(2)}) collective-permute-start(bf16[3,640,256]{2,1,0:T(8,128)(2,1)} %collective-permute-done.22.refs_14_), channel_id=1, source_target_pairs={{0,1},{1,0},{2,3},{3,2},{4,5},{5,4},{6,7},{7,6},{8,9},{9,8},{10,11... | collective-permute-start | bytes 2949128 | tf_op jit(solution)/shard_map/ppermute | solution.py:636
  148.7 7.4 %collective-permute-start.31 = (bf16[3,640,256]{2,1,0:T(8,128)(2,1)}, bf16[3,640,256]{2,1,0:T(8,128)(2,1)}, u32[]{:S(2)}, u32[]{:S(2)}) collective-permute-start(bf16[3,640,256]{2,1,0:T(8,128)(2,1)} %collective-permute-done.23.refs_15_), channel_id=1, source_target_pairs={{0,1},{1,0},{2,3},{3,2},{4,5},{5,4},{6,7},{7,6},{8,9},{9,8},{10,11... | collective-permute-start | bytes 2949128 | tf_op jit(solution)/shard_map/ppermute | solution.py:636
  156.1 16.3 %collective-permute-start.33 = (bf16[640,512]{1,0:T(8,128)(2,1)}, bf16[640,512]{1,0:T(8,128)(2,1)}, u32[]{:S(2)}, u32[]{:S(2)}) collective-permute-start(bf16[640,512]{1,0:T(8,128)(2,1)} %get-tuple-element.267.qo_c), channel_id=1, source_target_pairs={{0,2},{1,3},{2,0},{3,1},{4,6},{5,7},{6,4},{7,5},{8,10},{9,11},{10,... | collective-permute-start | bytes 1966088 | tf_op jit(solution)/shard_map/ppermute | solution.py:632
  156.8 20.4 %collective-permute-start.35 = (bf16[640,512]{1,0:T(8,128)(2,1)}, bf16[640,512]{1,0:T(8,128)(2,1)}, u32[]{:S(2)}, u32[]{:S(2)}) collective-permute-start(bf16[640,512]{1,0:T(8,128)(2,1)} %get-tuple-element.267.qo_c), channel_id=1, source_target_pairs={{0,1},{1,0},{2,3},{3,2},{4,5},{5,4},{6,7},{7,6},{8,9},{9,8},{10,11... | collective-permute-start | bytes 1966088 | tf_op jit(solution)/shard_map/ppermute | solution.py:636
  172.3 9.8 %collective-permute-start.36 = (bf16[640,512]{1,0:T(8,128)(2,1)}, bf16[640,512]{1,0:T(8,128)(2,1)}, u32[]{:S(2)}, u32[]{:S(2)}) collective-permute-start(bf16[640,512]{1,0:T(8,128)(2,1)} %collective-permute-done.33.qo_d), channel_id=1, source_target_pairs={{0,1},{1,0},{2,3},{3,2},{4,5},{5,4},{6,7},{7,6},{8,9},{9,8},{10,11... | collective-permute-start | bytes 1966088 | tf_op jit(solution)/shard_map/ppermute | solution.py:636
  173.5 8.6 %collective-permute-start.34 = (bf16[512,512]{1,0:T(8,128)(2,1)S(1)}, bf16[512,512]{1,0:T(8,128)(2,1)S(1)}, u32[]{:S(2)}, u32[]{:S(2)}) collective-permute-start(bf16[512,512]{1,0:T(8,128)(2,1)S(1)} %get-tuple-element.260.own), channel_id=1, source_target_pairs={{0,1},{1,2},{2,3},{4,5},{5,6},{6,7},{8,9},{9,10},{10,11},{12,13},{... | collective-permute-start | bytes 1572872 | tf_op jit(solution)/shard_map/ppermute | solution.py:500
  206.1 24.2 %collective-permute-start.37 = (bf16[512,640]{1,0:T(8,128)(2,1)S(1)}, bf16[512,640]{1,0:T(8,128)(2,1)S(1)}, u32[]{:S(2)}, u32[]{:S(2)}) collective-permute-start(bf16[512,640]{1,0:T(8,128)(2,1)S(1)} %broadcast_select_fusion.4), channel_id=1, source_target_pairs={{0,16},{16,0},{1,17},{17,1},{2,18},{18,2},{3,19},{19,3},{4,20},{20... | collective-permute-start | bytes 1966088 | tf_op jit(solution)/shard_map/ppermute | solution.py:640
  230.3 16.3 %collective-permute-start.38 = (bf16[2,2,3,640,256]{4,3,2,1,0:T(8,128)(2,1)}, bf16[2,2,3,640,256]{4,3,2,1,0:T(8,128)(2,1)}, u32[]{:S(2)}, u32[]{:S(2)}) collective-permute-start(bf16[2,2,3,640,256]{4,3,2,1,0:T(8,128)(2,1)} %get-tuple-element.294), channel_id=1, source_target_pairs={{0,1},{1,0},{2,3},{3,2},{4,5},{5,4},{6,7},{7,6},{8,9},{9,8},{10,11... | collective-permute-start | bytes 11796488 | tf_op jit(solution)/shard_map/ppermute | solution.py:636
  246.6 11.5 %collective-permute-start.39 = (bf16[512,512]{1,0:T(8,128)(2,1)S(1)}, bf16[512,512]{1,0:T(8,128)(2,1)S(1)}, u32[]{:S(2)}, u32[]{:S(2)}) collective-permute-start(bf16[512,512]{1,0:T(8,128)(2,1)S(1)} %get-tuple-element.295), channel_id=1, source_target_pairs={{1,0},{2,1},{3,2},{5,4},{6,5},{7,6},{9,8},{10,9},{11,10},{13,12},{... | collective-permute-start | bytes 1572872 | tf_op jit(solution)/shard_map/ppermute | solution.py:600
  248.8 38.6 %collective-permute-start.41 = (bf16[2,640,512]{2,1,0:T(8,128)(2,1)}, bf16[2,640,512]{2,1,0:T(8,128)(2,1)}, u32[]{:S(2)}, u32[]{:S(2)}) collective-permute-start(bf16[2,640,512]{2,1,0:T(8,128)(2,1)} %get-tuple-element.317), channel_id=1, source_target_pairs={{0,1},{1,0},{2,3},{3,2},{4,5},{5,4},{6,7},{7,6},{8,9},{9,8},{10,11... | collective-permute-start | bytes 3932168 | tf_op jit(solution)/shard_map/ppermute | solution.py:636
  258.1 29.3 %collective-permute-start.40 = (bf16[3,640,256]{2,1,0:T(8,128)(2,1)S(1)}, bf16[3,640,256]{2,1,0:T(8,128)(2,1)}, u32[]{:S(2)}, u32[]{:S(2)}) collective-permute-start(bf16[3,640,256]{2,1,0:T(8,128)(2,1)S(1)} %get-tuple-element.298), channel_id=1, source_target_pairs={{0,2},{1,3},{2,0},{3,1},{4,6},{5,7},{6,4},{7,5},{8,10},{9,11},{10,... | collective-permute-start | bytes 2949128 | tf_op jit(solution)/shard_map/ppermute | solution.py:632
  287.3 26.2 %collective-permute-start.42 = (bf16[2,2,3,640,256]{4,3,2,1,0:T(8,128)(2,1)}, bf16[2,2,3,640,256]{4,3,2,1,0:T(8,128)(2,1)}, u32[]{:S(2)}, u32[]{:S(2)}) collective-permute-start(bf16[2,2,3,640,256]{4,3,2,1,0:T(8,128)(2,1)} %get-tuple-element.329), channel_id=1, source_target_pairs={{0,1},{1,0},{2,3},{3,2},{4,5},{5,4},{6,7},{7,6},{8,9},{9,8},{10,11... | collective-permute-start | bytes 11796488 | tf_op jit(solution)/shard_map/ppermute | solution.py:636
  287.8 25.8 %collective-permute-start.43 = (bf16[3,640,256]{2,1,0:T(8,128)(2,1)}, bf16[3,640,256]{2,1,0:T(8,128)(2,1)S(1)}, u32[]{:S(2)}, u32[]{:S(2)}) collective-permute-start(bf16[3,640,256]{2,1,0:T(8,128)(2,1)} %get-tuple-element.330), channel_id=1, source_target_pairs={{0,2},{1,3},{2,0},{3,1},{4,6},{5,7},{6,4},{7,5},{8,10},{9,11},{10,... | collective-permute-start | bytes 2949128 | tf_op jit(solution)/shard_map/ppermute | solution.py:632
  313.6 15.7 %collective-permute-start.44 = (bf16[512,512]{1,0:T(8,128)(2,1)S(1)}, bf16[512,512]{1,0:T(8,128)(2,1)S(1)}, u32[]{:S(2)}, u32[]{:S(2)}) collective-permute-start(bf16[512,512]{1,0:T(8,128)(2,1)S(1)} %get-tuple-element.335), channel_id=1, source_target_pairs={{1,0},{2,1},{3,2},{5,4},{6,5},{7,6},{9,8},{10,9},{11,10},{13,12},{... | collective-permute-start | bytes 1572872 | tf_op jit(solution)/shard_map/ppermute | solution.py:600
  316.2 18.9 %collective-permute-start.49 = (bf16[640,512]{1,0:T(8,128)(2,1)}, bf16[640,512]{1,0:T(8,128)(2,1)}, u32[]{:S(2)}, u32[]{:S(2)}) collective-permute-start(bf16[640,512]{1,0:T(8,128)(2,1)} %get-tuple-element.355), channel_id=1, source_target_pairs={{0,2},{1,3},{2,0},{3,1},{4,6},{5,7},{6,4},{7,5},{8,10},{9,11},{10,... | collective-permute-start | bytes 1966088 | tf_op jit(solution)/shard_map/ppermute | solution.py:632
  316.4 20.8 %collective-permute-start.48 = (bf16[2,640,512]{2,1,0:T(8,128)(2,1)}, bf16[2,640,512]{2,1,0:T(8,128)(2,1)}, u32[]{:S(2)}, u32[]{:S(2)}) collective-permute-start(bf16[2,640,512]{2,1,0:T(8,128)(2,1)} %get-tuple-element.353), channel_id=1, source_target_pairs={{0,1},{1,0},{2,3},{3,2},{4,5},{5,4},{6,7},{7,6},{8,9},{9,8},{10,11... | collective-permute-start | bytes 3932168 | tf_op jit(solution)/shard_map/ppermute | solution.py:636
  317.9 6.7 %collective-permute-start.47 = (bf16[1,352,512]{2,1,0:T(8,128)(2,1)S(1)}, bf16[1,352,512]{2,1,0:T(8,128)(2,1)S(1)}, u32[]{:S(2)}, u32[]{:S(2)}) collective-permute-start(bf16[1,352,512]{2,1,0:T(8,128)(2,1)S(1)} %bitcast.227), channel_id=1, source_target_pairs={{0,1},{1,0},{2,3},{3,2},{4,5},{5,4},{6,7},{7,6},{8,9},{9,8},{10,11... | collective-permute-start | bytes 1081352 | tf_op jit(solution)/shard_map/ppermute | solution.py:636
  322.7 31.6 %collective-permute-start.45 = (bf16[3,640,256]{2,1,0:T(8,128)(2,1)}, bf16[3,640,256]{2,1,0:T(8,128)(2,1)}, u32[]{:S(2)}, u32[]{:S(2)}) collective-permute-start(bf16[3,640,256]{2,1,0:T(8,128)(2,1)} %get-tuple-element.386), channel_id=1, source_target_pairs={{0,2},{1,3},{2,0},{3,1},{4,6},{5,7},{6,4},{7,5},{8,10},{9,11},{10,... | collective-permute-start | bytes 2949128 | tf_op jit(solution)/shard_map/ppermute | solution.py:632
  335.0 19.4 %collective-permute-start.50 = (bf16[512,640]{1,0:T(8,128)(2,1)S(1)}, bf16[512,640]{1,0:T(8,128)(2,1)S(1)}, u32[]{:S(2)}, u32[]{:S(2)}) collective-permute-start(bf16[512,640]{1,0:T(8,128)(2,1)S(1)} %broadcast_select_fusion.3), channel_id=1, source_target_pairs={{0,16},{16,0},{1,17},{17,1},{2,18},{18,2},{3,19},{19,3},{4,20},{20... | collective-permute-start | bytes 1966088 | tf_op jit(solution)/shard_map/ppermute | solution.py:640
  357.0 17.7 %collective-permute-start.52 = (bf16[3,640,256]{2,1,0:T(8,128)(2,1)S(1)}, bf16[3,640,256]{2,1,0:T(8,128)(2,1)S(1)}, u32[]{:S(2)}, u32[]{:S(2)}) collective-permute-start(bf16[3,640,256]{2,1,0:T(8,128)(2,1)S(1)} %broadcast_select_fusion.2), channel_id=1, source_target_pairs={{0,16},{16,0},{1,17},{17,1},{2,18},{18,2},{3,19},{19,3},{4,20},{20... | collective-permute-start | bytes 2949128 | tf_op jit(solution)/shard_map/ppermute | solution.py:640
  357.2 20.2 %collective-permute-start.51 = (bf16[3,640,256]{2,1,0:T(8,128)(2,1)S(1)}, bf16[3,640,256]{2,1,0:T(8,128)(2,1)S(1)}, u32[]{:S(2)}, u32[]{:S(2)}) collective-permute-start(bf16[3,640,256]{2,1,0:T(8,128)(2,1)S(1)} %copy-done.52), channel_id=1, source_target_pairs={{0,2},{1,3},{2,0},{3,1},{4,6},{5,7},{6,4},{7,5},{8,10},{9,11},{10,... | collective-permute-start | bytes 2949128 | tf_op jit(solution)/shard_map/ppermute | solution.py:632
  377.4 26.8 %collective-permute-start.53 = (bf16[1344,512]{1,0:T(8,128)(2,1)}, bf16[1344,512]{1,0:T(8,128)(2,1)}, u32[]{:S(2)}, u32[]{:S(2)}) collective-permute-start(bf16[1344,512]{1,0:T(8,128)(2,1)} %pad_maximum_fusion), channel_id=1, source_target_pairs={{0,2},{1,3},{2,0},{3,1},{4,6},{5,7},{6,4},{7,5},{8,10},{9,11},{10,... | collective-permute-start | bytes 4128776 | tf_op jit(solution)/shard_map/ppermute | solution.py:632
  378.8 21.2 %collective-permute-start.57 = (bf16[3,640,256]{2,1,0:T(8,128)(2,1)}, bf16[3,640,256]{2,1,0:T(8,128)(2,1)}, u32[]{:S(2)}, u32[]{:S(2)}) collective-permute-start(bf16[3,640,256]{2,1,0:T(8,128)(2,1)} %broadcast_select_fusion.1), channel_id=1, source_target_pairs={{0,16},{16,0},{1,17},{17,1},{2,18},{18,2},{3,19},{19,3},{4,20},{20... | collective-permute-start | bytes 2949128 | tf_op jit(solution)/shard_map/ppermute | solution.py:640
  380.4 5.8 %collective-permute-start.54 = (bf16[480,256]{1,0:T(8,128)(2,1)S(1)}, bf16[480,256]{1,0:T(8,128)(2,1)S(1)}, u32[]{:S(2)}, u32[]{:S(2)}) collective-permute-start(bf16[480,256]{1,0:T(8,128)(2,1)S(1)} %bitcast.242), channel_id=1, source_target_pairs={{0,4},{4,8},{8,12},{12,0},{1,5},{5,9},{9,13},{13,1},{2,6},{6,10},{... | collective-permute-start | bytes 737288 | tf_op jit(solution)/shard_map/ppermute | solution.py:669
  381.4 18.4 %collective-permute-start.55 = (bf16[480,256]{1,0:T(8,128)(2,1)S(1)}, bf16[480,256]{1,0:T(8,128)(2,1)S(1)}, u32[]{:S(2)}, u32[]{:S(2)}) collective-permute-start(bf16[480,256]{1,0:T(8,128)(2,1)S(1)} %bitcast.241), channel_id=1, source_target_pairs={{0,8},{4,12},{8,0},{12,4},{1,9},{5,13},{9,1},{13,5},{2,10},{6,14},... | collective-permute-start | bytes 737288 | tf_op jit(solution)/shard_map/ppermute | solution.py:669
  381.4 18.4 %collective-permute-start.56 = (bf16[480,256]{1,0:T(8,128)(2,1)S(1)}, bf16[480,256]{1,0:T(8,128)(2,1)S(1)}, u32[]{:S(2)}, u32[]{:S(2)}) collective-permute-start(bf16[480,256]{1,0:T(8,128)(2,1)S(1)} %bitcast.239), channel_id=1, source_target_pairs={{0,12},{4,0},{8,4},{12,8},{1,13},{5,1},{9,5},{13,9},{2,14},{6,2},{... | collective-permute-start | bytes 737288 | tf_op jit(solution)/shard_map/ppermute | solution.py:669
  406.9 23.1 %collective-permute-start.61 = (bf16[992,512]{1,0:T(8,128)(2,1)S(1)}, bf16[992,512]{1,0:T(8,128)(2,1)S(1)}, u32[]{:S(2)}, u32[]{:S(2)}) collective-permute-start(bf16[992,512]{1,0:T(8,128)(2,1)S(1)} %broadcast_select_fusion), channel_id=1, source_target_pairs={{0,16},{16,0},{1,17},{17,1},{2,18},{18,2},{3,19},{19,3},{4,20},{20... | collective-permute-start | bytes 3047432 | tf_op jit(solution)/shard_map/ppermute | solution.py:640
  410.8 6.5 %collective-permute-start.58 = (bf16[480,256]{1,0:T(8,128)(2,1)S(1)}, bf16[480,256]{1,0:T(8,128)(2,1)S(1)}, u32[]{:S(2)}, u32[]{:S(2)}) collective-permute-start(bf16[480,256]{1,0:T(8,128)(2,1)S(1)} %bitcast.240), channel_id=1, source_target_pairs={{0,4},{4,8},{8,12},{12,0},{1,5},{5,9},{9,13},{13,1},{2,6},{6,10},{... | collective-permute-start | bytes 737288 | tf_op jit(solution)/shard_map/ppermute | solution.py:669
  411.8 18.0 %collective-permute-start.59 = (bf16[480,256]{1,0:T(8,128)(2,1)S(1)}, bf16[480,256]{1,0:T(8,128)(2,1)S(1)}, u32[]{:S(2)}, u32[]{:S(2)}) collective-permute-start(bf16[480,256]{1,0:T(8,128)(2,1)S(1)} %bitcast.238), channel_id=1, source_target_pairs={{0,8},{4,12},{8,0},{12,4},{1,9},{5,13},{9,1},{13,5},{2,10},{6,14},... | collective-permute-start | bytes 737288 | tf_op jit(solution)/shard_map/ppermute | solution.py:669
  411.8 18.0 %collective-permute-start.60 = (bf16[480,256]{1,0:T(8,128)(2,1)S(1)}, bf16[480,256]{1,0:T(8,128)(2,1)S(1)}, u32[]{:S(2)}, u32[]{:S(2)}) collective-permute-start(bf16[480,256]{1,0:T(8,128)(2,1)S(1)} %bitcast.237), channel_id=1, source_target_pairs={{0,12},{4,0},{8,4},{12,8},{1,13},{5,1},{9,5},{13,9},{2,14},{6,2},{... | collective-permute-start | bytes 737288 | tf_op jit(solution)/shard_map/ppermute | solution.py:669
  432.1 9.3 %collective-permute-start.62 = (bf16[496,256]{1,0:T(8,128)(2,1)S(1)}, bf16[496,256]{1,0:T(8,128)(2,1)S(1)}, u32[]{:S(2)}, u32[]{:S(2)}) collective-permute-start(bf16[496,256]{1,0:T(8,128)(2,1)S(1)} %pad_maximum_fusion.4), channel_id=1, source_target_pairs={{0,4},{4,8},{8,12},{12,0},{1,5},{5,9},{9,13},{13,1},{2,6},{6,10},{... | collective-permute-start | bytes 761864 | tf_op jit(solution)/shard_map/ppermute | solution.py:669
  432.9 25.3 %collective-permute-start.63 = (bf16[496,256]{1,0:T(8,128)(2,1)S(1)}, bf16[496,256]{1,0:T(8,128)(2,1)S(1)}, u32[]{:S(2)}, u32[]{:S(2)}) collective-permute-start(bf16[496,256]{1,0:T(8,128)(2,1)S(1)} %pad_maximum_fusion.5), channel_id=1, source_target_pairs={{0,8},{4,12},{8,0},{12,4},{1,9},{5,13},{9,1},{13,5},{2,10},{6,14},... | collective-permute-start | bytes 761864 | tf_op jit(solution)/shard_map/ppermute | solution.py:669
  437.4 20.8 %collective-permute-start.64 = (bf16[496,256]{1,0:T(8,128)(2,1)S(1)}, bf16[496,256]{1,0:T(8,128)(2,1)S(1)}, u32[]{:S(2)}, u32[]{:S(2)}) collective-permute-start(bf16[496,256]{1,0:T(8,128)(2,1)S(1)} %pad_maximum_fusion.6), channel_id=1, source_target_pairs={{0,12},{4,0},{8,4},{12,8},{1,13},{5,1},{9,5},{13,9},{2,14},{6,2},{... | collective-permute-start | bytes 761864 | tf_op jit(solution)/shard_map/ppermute | solution.py:669
  458.4 3.5 collective-permute-start.65
  (71 other events, 723.9 us)

commit v2 on v1

--- a/solution.py
+++ b/solution.py
@@ -858,12 +858,12 @@
     at0 = backward_attend(ff0[3], keys0, attended0, small0, choices[0], qo0, common)
     pair1 = kept_sums(qo1_core, at1[1])
     at0, ff0_core, across1b, pair1, kv1 = after((at0, ff0_core, across1b, pair1, kv1))
-    pair1_across = across_tensor(pair1[0])
     rest1 = core_half(packed(kv1, gain1, key1, ff1, at1))[0]
     next0 = halo_back(at0[3])
     qo0_core = beside_tensor(at0[0])
-    sums0 = [kept_sums(ff0_core, ff0[1], half) for half in range(2)]
+    sums0 = [kept_sums(ff0_core, ff0[1], 0), kept_sums(after(ff0_core, next0), ff0[1], 1)]
     across0a = across_tensor(sums0[0][0])
+    pair1_across = across_tensor(after(pair1[0], sums0[0]))
     kv0, grad0, grad0_low, gain0, key0 = backward_keys(
         x0, at0[2], next0, keys0, small0, at0[4], ff0[2], common
     )
@@ -872,8 +872,8 @@
     rest0 = core_half(packed(kv0, gain0, key0, ff0, at0))[0]
     full1 = [add(sums1[0][1], across1a), add(sums1[1][1], across1b)]
     pair1 = add(pair1[1], pair1_across)
-    across0a, rest0, rest1, pair0, pair1, sums0, full1, grad_got = after(
-        (across0a, rest0, rest1, pair0, pair1, sums0, full1, grad_got)
+    across0a, rest0, rest1, pair0, sums0, full1, grad_got = after(
+        (across0a, rest0, rest1, pair0, sums0, full1, grad_got)
     )
 
     def swapped(zero, one):

time: 473 us -> 490 us (1.036)
  waiting for transfers between devices: 172 us -> 199 us
  other arithmetic: 51.1 us -> 45.1 us
    ppermute x9, waiting for transfers between devices: 24 us -> 40.1 us  [across_section(): return lax.ppermute(part, 'section', [(0, 1), (1, 0)])]
    ppermute x11, waiting for transfers between devices: 18.1 us -> 33.6 us  [across_tensor(): return lax.ppermute(part, 'tensor', tensor_pairs(2))]
    ppermute x9, waiting for transfers between devices: 48.1 us -> 42 us  [summed_over_dp(): lax.ppermute(share(me + shift), 'dp', [(i, (i + shift) % count) for i in...]
    unnamed x143 -> x147, local copies, waits for them, and re-layouts: 18 us -> 17.4 us
  transfers between devices with their start and end apart: 66 -> 66, of which waited for: 27 -> 29; matrix products, arithmetic and copies ran while one was open for 10% -> 9% of each run, Pallas kernels for 26% -> 25%
where the time goes in v2:
time: 490 us; the launch traced here: 481 us
  waiting for transfers between devices  199 us (41%)
  Pallas kernels  142 us (29%)
  starting transfers between devices  68.1 us (14%)
  other arithmetic  45.1 us (9%)
  local copies, waits for them, and re-layouts  24.9 us (5%)
    pallas_call x17, Pallas kernels, run(): pl.pallas_call(kernel, grid=grid, in_specs=[spec(a.shape) for a, spec in...  142 us
    ppermute x12, waiting for transfers between devices, rows_over_dp(): lax.ppermute(part, 'dp', [(i, (i + shift) % count) for i in range(count)])  60.9 us
    ppermute x9, waiting for transfers between devices, summed_over_dp(): lax.ppermute(share(me + shift), 'dp', [(i, (i + shift) % count) for i in...  42 us
    ppermute x9, waiting for transfers between devices, across_section(): return lax.ppermute(part, 'section', [(0, 1), (1, 0)])  40.1 us
    ppermute x11, waiting for transfers between devices, across_tensor(): return lax.ppermute(part, 'tensor', tensor_pairs(2))  33.6 us
    convert_element_type x11, other arithmetic, add(): return (left.astype(F32) + right.astype(F32)).astype(BF16)  23.2 us
    ppermute x12, starting transfers between devices, rows_over_dp(): lax.ppermute(part, 'dp', [(i, (i + shift) % count) for i in range(count)])  21.5 us
    unnamed x147, local copies, waits for them, and re-layouts  17.4 us
  transfers between devices with their start and end apart: 66, of which 29 were waited for; matrix products, arithmetic and copies ran while one was open for 9% of the time, Pallas kernels for 25%

profile of v2, /device:TPU:27, one launch (start us, length us, event | category | flops | bytes accessed | tf_op | source)
XLA Modules:
  0.0 480.6 jit_solution(15462639347005162121)
XLA Ops:
  3.7 4.0 collective-permute-start.4
  12.4 4.6 collective-permute-done.1.refs_1_
  17.0 16.7 %collective-permute-done.2.refs_2_ = bf16[256,512]{1,0:T(8,128)(2,1)S(1)} collective-permute-done((bf16[256,512]{1,0:T(8,128)(2,1)S(1)}, bf16[256,512]{1,0:T(8,128)(2,1)S(1)}, u32[]{:S(2)}, u32[]{:S(2)}) %collective-permute-start.2) | collective-permute-done | bytes 262176 | tf_op jit(solution)/shard_map/ppermute | solution.py:619
  36.6 3.1 collective-permute-start.6
  39.7 1.4 collective-permute-start.7
  41.1 1.9 multiply_sine_fusion
  43.0 1.4 collective-permute-start.11
  44.4 1.4 collective-permute-start.10
  46.0 15.3 %collective-permute-done.6.refs_2_ = bf16[3,160,256]{2,1,0:T(8,128)(2,1)S(1)} collective-permute-done((bf16[3,160,256]{2,1,0:T(8,128)(2,1)S(1)}, bf16[3,160,256]{2,1,0:T(8,128)(2,1)S(1)}, u32[]{:S(2)}, u32[]{:S(2)}) %collective-permute-start.6) | collective-permute-done | bytes 245792 | tf_op jit(solution)/shard_map/ppermute | solution.py:619
  61.3 1.4 shard_map.204.refs_4_
  65.7 1.4 collective-permute-start.14
  67.1 2.5 shard_map.207
  72.1 14.6 %collective-permute-done.13.refs_2_ = bf16[3,160,256]{2,1,0:T(8,128)(2,1)S(1)} collective-permute-done((bf16[3,160,256]{2,1,0:T(8,128)(2,1)S(1)}, bf16[3,160,256]{2,1,0:T(8,128)(2,1)S(1)}, u32[]{:S(2)}, u32[]{:S(2)}) %collective-permute-start.13) | collective-permute-done | bytes 245792 | tf_op jit(solution)/shard_map/ppermute | solution.py:619
  90.1 1.7 collective-permute-start.20
  98.4 11.0 %shard_map.208 = (f32[4,512,256]{2,1,0:T(8,128)}, bf16[4,512,256]{2,1,0:T(8,128)(2,1)}, bf16[4,512,256]{2,1,0:T(8,128)(2,1)}, f32[4,512,1]{2,1,0:T(8,128)}, f32[...) custom-call(s32[1]{0:T(128)} %bitcast.choice, ...), custom_call_target="tpu_custom_call" | custom-call | flops 16142000128 | bytes 1 | tf_op jit(solution)/shard_map/pallas_call | solution.py:464
  110.3 7.4 %collective-permute-done.15.refs_13_ = bf16[3,640,256]{2,1,0:T(8,128)(2,1)} collective-permute-done((bf16[3,640,256]{2,1,0:T(8,128)(2,1)}, bf16[3,640,256]{2,1,0:T(8,128)(2,1)}, u32[]{:S(2)}, u32[]{:S(2)}) %collective-permute-start.15) | collective-permute-done | bytes 983072 | tf_op jit(solution)/shard_map/ppermute | solution.py:640
  120.4 1.7 collective-permute-start.25
  122.1 12.1 %collective-permute-start.26 = (bf16[256,512]{1,0:T(8,128)(2,1)S(1)}, bf16[256,512]{1,0:T(8,128)(2,1)S(1)}, u32[]{:S(2)}, u32[]{:S(2)}) collective-permute-start(bf16[256,512]{1,0:T(8,128)(2,1)S(1)} %get-tuple-element.237.refs_0_), channel_id=1, source_target_pairs={{0,12},{4,0},{8,4},{12,8},{1,13},{5,1},{9,5},{13,9},{2,14},{6,2},{... | collective-permute-start | bytes 786440 | tf_op jit(solution)/shard_map/ppermute | solution.py:619
  134.2 9.6 %collective-permute-done.25.refs_2_ = bf16[256,512]{1,0:T(8,128)(2,1)S(1)} collective-permute-done((bf16[256,512]{1,0:T(8,128)(2,1)S(1)}, bf16[256,512]{1,0:T(8,128)(2,1)S(1)}, u32[]{:S(2)}, u32[]{:S(2)}) %collective-permute-start.25) | collective-permute-done | bytes 262176 | tf_op jit(solution)/shard_map/ppermute | solution.py:619
  145.0 2.4 collective-permute-start.32
  151.9 1.4 collective-permute-done.29.refs_9_
  153.3 1.4 collective-permute-done.30.refs_10_
  154.7 1.4 collective-permute-done.31.refs_11_
  158.6 11.8 %shard_map.210 = (bf16[4,512,512]{2,1,0:T(8,128)(2,1)}, bf16[4,512,512]{2,1,0:T(8,128)(2,1)}, f32[512,640]{1,0:T(8,128)}, f32[512,640]{1,0:T(8,128)}, bf16[512,640]{1,0:T(8,128)(2,1)S(1)}) custom-call(s32[1]{0:T(128)} %bitcast.choice, bf16[512,640]{1,0:T(8,128)(2,1)S(1)} %copy-done.29, f32[512,640]{1,0:T(8,128)} %get-tuple-element.232.middle, ...), custom_call_target="tpu_custom_call" | custom-call | flops 13836000256 | bytes 1 | tf_op jit(solution)/shard_map/pallas_call | solution.py:464
  173.6 2.5 collective-permute-start.34
  177.3 4.9 %collective-permute-done.34.prev = bf16[512,512]{1,0:T(8,128)(2,1)S(1)} collective-permute-done((bf16[512,512]{1,0:T(8,128)(2,1)S(1)}, bf16[512,512]{1,0:T(8,128)(2,1)S(1)}, u32[]{:S(2)}, u32[]{:S(2)}) %collective-permute-start.34) | collective-permute-done | bytes 524320 | tf_op jit(solution)/shard_map/ppermute | solution.py:500
  183.3 11.0 %shard_map.212 = (f32[4,512,256]{2,1,0:T(8,128)}, bf16[4,512,256]{2,1,0:T(8,128)(2,1)}, bf16[4,512,256]{2,1,0:T(8,128)(2,1)}, f32[4,512,1]{2,1,0:T(8,128)}, f32[...) custom-call(s32[1]{0:T(128)} %bitcast.27.choice, bf16[512,640]{1,0:T(8,128)(2,1)S(1)} %get-tuple-element.263.x, ...), custom_call_target="tpu_custom_call" | custom-call | flops 16142000128 | bytes 1 | tf_op jit(solution)/shard_map/pallas_call | solution.py:464
  194.3 11.7 %shard_map.213 = (bf16[4,512,512]{2,1,0:T(8,128)(2,1)}, bf16[4,512,512]{2,1,0:T(8,128)(2,1)}, f32[512,640]{1,0:T(8,128)}, f32[512,640]{1,0:T(8,128)}, bf16[512,640]{1,0:T(8,128)(2,1)S(1)}) custom-call(s32[1]{0:T(128)} %bitcast.27.choice, bf16[512,640]{1,0:T(8,128)(2,1)S(1)} %get-tuple-element.270.normed_two, f32[512,640]{1,0:T(8,128)} %get-tuple-element.271.middle, ...), custom_call_target="tpu_custom_call" | custom-call | flops 13836000256 | bytes 1 | tf_op jit(solution)/shard_map/pallas_call | solution.py:464
  206.1 1.4 collective-permute-start.37
  207.5 22.7 %shard_map.214 = (bf16[2,2,3,640,256]{4,3,2,1,0:T(8,128)(2,1)}, bf16[2,2,3,640,256]{4,3,2,1,0:T(8,128)(2,1)}, f32[512,640]{1,0:T(8,128)}, bf16[512,640]{1,0:T(8,128)(2,1)S(1)}, f32[4,640]{1,0:T(4,128)S(1)}) custom-call(s32[1]{0:T(128)} %bitcast.27.choice, bf16[512,640]{1,0:T(8,128)(2,1)S(1)} %dynamic-slice_bitcast_fusion.grad, ...), custom_call_target="tpu_custom_call" | custom-call | flops 28824999936 | bytes 1 | tf_op jit(solution)/shard_map/pallas_call | solution.py:464
  230.3 16.2 %shard_map.215 = (bf16[2,640,512]{2,1,0:T(8,128)(2,1)}, bf16[2,640,512]{2,1,0:T(8,128)(2,1)}, f32[512,512]{1,0:T(8,128)}, bf16[512,512]{1,0:T(8,128)(2,1)S(1)}, ...) custom-call(s32[1]{0:T(128)} %bitcast.27.choice, bf16[512,640]{1,0:T(8,128)(2,1)S(1)} %get-tuple-element.284.grad_branch, ...), custom_call_target="tpu_custom_call" | custom-call | flops 19601000448 | bytes 1 | tf_op jit(solution)/shard_map/pallas_call | solution.py:464
  246.5 2.2 collective-permute-start.39
  248.8 4.4 fusion.9
  253.2 4.9 %collective-permute-done.39.kv_next = bf16[512,512]{1,0:T(8,128)(2,1)S(1)} collective-permute-done((bf16[512,512]{1,0:T(8,128)(2,1)S(1)}, bf16[512,512]{1,0:T(8,128)(2,1)S(1)}, u32[]{:S(2)}, u32[]{:S(2)}) %collective-permute-start.39) | collective-permute-done | bytes 524320 | tf_op jit(solution)/shard_map/ppermute | solution.py:600
  258.1 5.1 %shard_map.216 = (bf16[640,512]{1,0:T(8,128)(2,1)S(1)}, f32[512,640]{1,0:T(8,128)}, bf16[512,640]{1,0:T(8,128)(2,1)S(1)}, f32[1,640]{1,0:T(1,128)S(1)}, f32[1,256]{1,0:T(1,128)S(1)}) custom-call(f32[512,512]{1,0:T(8,128)} %get-tuple-element.300.kv_own, bf16[512,512]{1,0:T(8,128)(2,1)S(1)} %collective-permute-done.39.kv_next, ...), custom_call_target="tpu_custom_call" | custom-call | flops 5765000192 | bytes 1 | tf_op jit(solution)/shard_map/pallas_call | solution.py:464
  263.1 23.3 %shard_map.217 = (bf16[2,2,3,640,256]{4,3,2,1,0:T(8,128)(2,1)}, bf16[2,2,3,640,256]{4,3,2,1,0:T(8,128)(2,1)}, f32[512,640]{1,0:T(8,128)}, bf16[512,640]{1,0:T(8,128)(2,1)S(1)}, f32[4,640]{1,0:T(4,128)S(1)}) custom-call(s32[1]{0:T(128)} %bitcast.choice, bf16[512,640]{1,0:T(8,128)(2,1)S(1)} %get-tuple-element.305.grad, ...), custom_call_target="tpu_custom_call" | custom-call | flops 28824999936 | bytes 1 | tf_op jit(solution)/shard_map/pallas_call | solution.py:464
  292.3 15.9 %shard_map.218 = (bf16[2,640,512]{2,1,0:T(8,128)(2,1)}, bf16[2,640,512]{2,1,0:T(8,128)(2,1)}, f32[512,512]{1,0:T(8,128)}, bf16[512,512]{1,0:T(8,128)(2,1)S(1)}, ...) custom-call(s32[1]{0:T(128)} %bitcast.choice, bf16[512,640]{1,0:T(8,128)(2,1)S(1)} %copy-done.32, ...), custom_call_target="tpu_custom_call" | custom-call | flops 19601000448 | bytes 1 | tf_op jit(solution)/shard_map/pallas_call | solution.py:464
  308.2 2.8 fusion.19
  311.0 2.4 add_convert_fusion.7
  313.5 2.8 collective-permute-start.44
  319.1 5.0 %collective-permute-done.44.kv_next = bf16[512,512]{1,0:T(8,128)(2,1)S(1)} collective-permute-done((bf16[512,512]{1,0:T(8,128)(2,1)S(1)}, bf16[512,512]{1,0:T(8,128)(2,1)S(1)}, u32[]{:S(2)}, u32[]{:S(2)}) %collective-permute-start.44) | collective-permute-done | bytes 524320 | tf_op jit(solution)/shard_map/ppermute | solution.py:600
  324.1 5.0 %shard_map.219 = (bf16[640,512]{1,0:T(8,128)(2,1)S(1)}, f32[512,640]{1,0:T(8,128)}, bf16[512,640]{1,0:T(8,128)(2,1)S(1)}, f32[1,640]{1,0:T(1,128)S(1)}, f32[1,256]{1,0:T(1,128)S(1)}) custom-call(f32[512,512]{1,0:T(8,128)} %get-tuple-element.335.kv_own, bf16[512,512]{1,0:T(8,128)(2,1)S(1)} %collective-permute-done.44.kv_next, f32[512,256]{1,0:T(8,128)S(1)} %copy-done.22, ...), custom_call_target="tpu_custom_call" | custom-call | flops 5765000192 | bytes 1 | tf_op jit(solution)/shard_map/pallas_call | solution.py:464
  329.6 5.2 %fusion.13 = (bf16[3,640,256]{2,1,0:T(8,128)(2,1)S(1)}, bf16[3,640,256]{2,1,0:T(8,128)(2,1)}, bf16[3,640,256]{2,1,0:T(8,128)(2,1)S(1)}, bf16[3,640,256]{2,1,0:T(8,128)(2,1)S(1)}) fusion(bf16[2,2,3,640,256]{4,3,2,1,0:T(8,128)(2,1)} %collective-permute-done.42, bf16[2,2,3,640,256]{4,3,2,1,0:T(8,128)(2,1)} %get-tuple-element.341), kind=kLoop, calls=%fused_computation.44 | loop fusion | flops 7864320 | bytes 11796480 | tf_op jit(solution)/shard_map/convert_element_type | solution.py:648
  337.3 2.9 fusion.21
  340.1 10.7 %collective-permute-done.49 = bf16[512,640]{1,0:T(8,128)(2,1)S(1)} collective-permute-done((bf16[512,640]{1,0:T(8,128)(2,1)S(1)}, bf16[512,640]{1,0:T(8,128)(2,1)S(1)}, u32[]{:S(2)}, u32[]{:S(2)}) %collective-permute-start.49) | collective-permute-done | bytes 655392 | tf_op jit(solution)/shard_map/ppermute | solution.py:640
  350.8 6.9 %collective-permute-done.45 = bf16[3,640,256]{2,1,0:T(8,128)(2,1)S(1)} collective-permute-done((bf16[3,640,256]{2,1,0:T(8,128)(2,1)S(1)}, bf16[3,640,256]{2,1,0:T(8,128)(2,1)S(1)}, u32[]{:S(2)}, u32[]{:S(2)}) %collective-permute-start.45) | collective-permute-done | bytes 983072 | tf_op jit(solution)/shard_map/ppermute | solution.py:632
  357.7 1.4 broadcast_select_fusion.2
  361.8 19.4 %collective-permute-done.51 = bf16[3,640,256]{2,1,0:T(8,128)(2,1)} collective-permute-done((bf16[3,640,256]{2,1,0:T(8,128)(2,1)}, bf16[3,640,256]{2,1,0:T(8,128)(2,1)}, u32[]{:S(2)}, u32[]{:S(2)}) %collective-permute-start.51) | collective-permute-done | bytes 983072 | tf_op jit(solution)/shard_map/ppermute | solution.py:640
  381.3 1.8 add_convert_fusion.4
  383.1 1.7 broadcast_select_fusion.1
  386.9 8.1 %collective-permute-done.60 = bf16[640,512]{1,0:T(8,128)(2,1)S(1)} collective-permute-done((bf16[640,512]{1,0:T(8,128)(2,1)}, bf16[640,512]{1,0:T(8,128)(2,1)S(1)}, u32[]{:S(2)}, u32[]{:S(2)}) %collective-permute-start.60) | collective-permute-done | bytes 655392 | tf_op jit(solution)/shard_map/ppermute | solution.py:632
  395.2 7.6 %collective-permute-done.54 = bf16[480,256]{1,0:T(8,128)(2,1)S(1)} collective-permute-done((bf16[480,256]{1,0:T(8,128)(2,1)S(1)}, bf16[480,256]{1,0:T(8,128)(2,1)S(1)}, u32[]{:S(2)}, u32[]{:S(2)}) %collective-permute-start.54) | collective-permute-done | bytes 245792 | tf_op jit(solution)/shard_map/ppermute | solution.py:669
  403.0 2.3 collective-permute-done.56
  405.3 1.7 add_convert_fusion.2
  407.1 17.5 %collective-permute-done.52 = bf16[1344,512]{1,0:T(8,128)(2,1)S(1)} collective-permute-done((bf16[1344,512]{1,0:T(8,128)(2,1)S(1)}, bf16[1344,512]{1,0:T(8,128)(2,1)S(1)}, u32[]{:S(2)}, u32[]{:S(2)}) %collective-permute-start.52) | collective-permute-done | bytes 1376288 | tf_op jit(solution)/shard_map/ppermute | solution.py:632
  425.1 1.4 collective-permute-start.61
  426.5 1.7 maximum_bitcast_fusion
  430.1 1.7 maximum_bitcast_fusion.1
  431.8 2.2 collective-permute-done.57
  434.0 14.6 %collective-permute-done.58 = bf16[480,256]{1,0:T(8,128)(2,1)S(1)} collective-permute-done((bf16[480,256]{1,0:T(8,128)(2,1)S(1)}, bf16[480,256]{1,0:T(8,128)(2,1)S(1)}, u32[]{:S(2)}, u32[]{:S(2)}) %collective-permute-start.58) | collective-permute-done | bytes 245792 | tf_op jit(solution)/shard_map/ppermute | solution.py:669
  449.8 4.1 collective-permute-start.63
  453.9 1.5 collective-permute-start.64
  457.9 17.6 %collective-permute-done.63 = bf16[496,256]{1,0:T(8,128)(2,1)S(1)} collective-permute-done((bf16[496,256]{1,0:T(8,128)(2,1)S(1)}, bf16[496,256]{1,0:T(8,128)(2,1)S(1)}, u32[]{:S(2)}, u32[]{:S(2)}) %collective-permute-start.63) | collective-permute-done | bytes 253984 | tf_op jit(solution)/shard_map/ppermute | solution.py:669
  475.6 1.8 collective-permute-start.65
  (347 shorter events, 68.9 us)
Async XLA Ops:
  3.3 7.2 %collective-permute-start = (bf16[256,512]{1,0:T(8,128)(2,1)S(1)}, bf16[256,512]{1,0:T(8,128)(2,1)S(1)}, u32[]{:S(2)}, u32[]{:S(2)}) collective-permute-start(bf16[256,512]{1,0:T(8,128)(2,1)S(1)} %fusion.31), channel_id=1, source_target_pairs={{0,16},{16,0},{1,17},{17,1},{2,18},{18,2},{3,19},{19,3},{4,20},{20... | collective-permute-start | bytes 786440 | tf_op jit(solution)/shard_map/ppermute | solution.py:640
  3.7 32.8 %collective-permute-start.4 = (bf16[512,640]{1,0:T(8,128)(2,1)S(1)}, bf16[512,640]{1,0:T(8,128)(2,1)}, u32[]{:S(2)}, u32[]{:S(2)}) collective-permute-start(bf16[512,640]{1,0:T(8,128)(2,1)S(1)} %dynamic-slice_bitcast_fusion.1.x), channel_id=1, source_target_pairs={{0,1},{1,2},{2,3},{4,5},{5,6},{6,7},{8,9},{9,10},{10,11},{12,13},{... | collective-permute-start | bytes 1966088 | tf_op jit(solution)/shard_map/ppermute | solution.py:500
  10.7 6.3 %collective-permute-start.1 = (bf16[256,512]{1,0:T(8,128)(2,1)S(1)}, bf16[256,512]{1,0:T(8,128)(2,1)S(1)}, u32[]{:S(2)}, u32[]{:S(2)}) collective-permute-start(bf16[256,512]{1,0:T(8,128)(2,1)S(1)} %get-tuple-element.432.refs_0_), channel_id=1, source_target_pairs={{0,4},{4,8},{8,12},{12,0},{1,5},{5,9},{9,13},{13,1},{2,6},{6,10},{... | collective-permute-start | bytes 786440 | tf_op jit(solution)/shard_map/ppermute | solution.py:619
  10.7 23.0 %collective-permute-start.2 = (bf16[256,512]{1,0:T(8,128)(2,1)S(1)}, bf16[256,512]{1,0:T(8,128)(2,1)S(1)}, u32[]{:S(2)}, u32[]{:S(2)}) collective-permute-start(bf16[256,512]{1,0:T(8,128)(2,1)S(1)} %get-tuple-element.432.refs_0_), channel_id=1, source_target_pairs={{0,8},{4,12},{8,0},{12,4},{1,9},{5,13},{9,1},{13,5},{2,10},{6,14},... | collective-permute-start | bytes 786440 | tf_op jit(solution)/shard_map/ppermute | solution.py:619
  12.1 21.6 %collective-permute-start.3 = (bf16[256,512]{1,0:T(8,128)(2,1)S(1)}, bf16[256,512]{1,0:T(8,128)(2,1)S(1)}, u32[]{:S(2)}, u32[]{:S(2)}) collective-permute-start(bf16[256,512]{1,0:T(8,128)(2,1)S(1)} %get-tuple-element.432.refs_0_), channel_id=1, source_target_pairs={{0,12},{4,0},{8,4},{12,8},{1,13},{5,1},{9,5},{13,9},{2,14},{6,2},{... | collective-permute-start | bytes 786440 | tf_op jit(solution)/shard_map/ppermute | solution.py:619
  36.5 9.5 %collective-permute-start.5 = (bf16[3,160,256]{2,1,0:T(8,128)(2,1)S(1)}, bf16[3,160,256]{2,1,0:T(8,128)(2,1)S(1)}, u32[]{:S(2)}, u32[]{:S(2)}) collective-permute-start(bf16[3,160,256]{2,1,0:T(8,128)(2,1)S(1)} %pad_maximum_fusion.7.refs_0_), channel_id=1, source_target_pairs={{0,4},{4,8},{8,12},{12,0},{1,5},{5,9},{9,13},{13,1},{2,6},{6,10},{... | collective-permute-start | bytes 737288 | tf_op jit(solution)/shard_map/ppermute | solution.py:619
  36.6 24.7 %collective-permute-start.6 = (bf16[3,160,256]{2,1,0:T(8,128)(2,1)S(1)}, bf16[3,160,256]{2,1,0:T(8,128)(2,1)S(1)}, u32[]{:S(2)}, u32[]{:S(2)}) collective-permute-start(bf16[3,160,256]{2,1,0:T(8,128)(2,1)S(1)} %pad_maximum_fusion.7.refs_0_), channel_id=1, source_target_pairs={{0,8},{4,12},{8,0},{12,4},{1,9},{5,13},{9,1},{13,5},{2,10},{6,14},... | collective-permute-start | bytes 737288 | tf_op jit(solution)/shard_map/ppermute | solution.py:619
  39.7 21.6 %collective-permute-start.7 = (bf16[3,160,256]{2,1,0:T(8,128)(2,1)S(1)}, bf16[3,160,256]{2,1,0:T(8,128)(2,1)}, u32[]{:S(2)}, u32[]{:S(2)}) collective-permute-start(bf16[3,160,256]{2,1,0:T(8,128)(2,1)S(1)} %pad_maximum_fusion.7.refs_0_), channel_id=1, source_target_pairs={{0,12},{4,0},{8,4},{12,8},{1,13},{5,1},{9,5},{13,9},{2,14},{6,2},{... | collective-permute-start | bytes 737288 | tf_op jit(solution)/shard_map/ppermute | solution.py:619
  43.0 21.4 %collective-permute-start.11 = (bf16[320,512]{1,0:T(8,128)(2,1)S(1)}, bf16[320,512]{1,0:T(8,128)(2,1)}, u32[]{:S(2)}, u32[]{:S(2)}) collective-permute-start(bf16[320,512]{1,0:T(8,128)(2,1)S(1)} %get-tuple-element.203), channel_id=1, source_target_pairs={{0,1},{1,0},{2,3},{3,2},{4,5},{5,4},{6,7},{7,6},{8,9},{9,8},{10,11... | collective-permute-start | bytes 983048 | tf_op jit(solution)/shard_map/ppermute | solution.py:636
  44.4 21.1 %collective-permute-start.10 = (bf16[640,512]{1,0:T(8,128)(2,1)}, bf16[640,512]{1,0:T(8,128)(2,1)}, u32[]{:S(2)}, u32[]{:S(2)}) collective-permute-start(bf16[640,512]{1,0:T(8,128)(2,1)} %get-tuple-element.222.qo_c), channel_id=1, source_target_pairs={{0,2},{1,3},{2,0},{3,1},{4,6},{5,7},{6,4},{7,5},{8,10},{9,11},{10,... | collective-permute-start | bytes 1966088 | tf_op jit(solution)/shard_map/ppermute | solution.py:632
  62.7 25.4 %collective-permute-start.8 = (bf16[3,640,256]{2,1,0:T(8,128)(2,1)S(1)}, bf16[3,640,256]{2,1,0:T(8,128)(2,1)S(1)}, u32[]{:S(2)}, u32[]{:S(2)}) collective-permute-start(bf16[3,640,256]{2,1,0:T(8,128)(2,1)S(1)} %shard_map.204.refs_4_), channel_id=1, source_target_pairs={{0,16},{16,0},{1,17},{17,1},{2,18},{18,2},{3,19},{19,3},{4,20},{20... | collective-permute-start | bytes 2949128 | tf_op jit(solution)/shard_map/ppermute | solution.py:640
  63.8 24.4 %collective-permute-start.9 = (bf16[3,640,256]{2,1,0:T(8,128)(2,1)S(1)}, bf16[3,640,256]{2,1,0:T(8,128)(2,1)S(1)}, u32[]{:S(2)}, u32[]{:S(2)}) collective-permute-start(bf16[3,640,256]{2,1,0:T(8,128)(2,1)S(1)} %shard_map.204.refs_4_), channel_id=1, source_target_pairs={{0,2},{1,3},{2,0},{3,1},{4,6},{5,7},{6,4},{7,5},{8,10},{9,11},{10,... | collective-permute-start | bytes 2949128 | tf_op jit(solution)/shard_map/ppermute | solution.py:632
  65.5 6.6 %collective-permute-start.12 = (bf16[3,160,256]{2,1,0:T(8,128)(2,1)S(1)}, bf16[3,160,256]{2,1,0:T(8,128)(2,1)S(1)}, u32[]{:S(2)}, u32[]{:S(2)}) collective-permute-start(bf16[3,160,256]{2,1,0:T(8,128)(2,1)S(1)} %pad_maximum_fusion.8.refs_0_), channel_id=1, source_target_pairs={{0,4},{4,8},{8,12},{12,0},{1,5},{5,9},{9,13},{13,1},{2,6},{6,10},{... | collective-permute-start | bytes 737288 | tf_op jit(solution)/shard_map/ppermute | solution.py:619
  65.6 21.1 %collective-permute-start.13 = (bf16[3,160,256]{2,1,0:T(8,128)(2,1)S(1)}, bf16[3,160,256]{2,1,0:T(8,128)(2,1)S(1)}, u32[]{:S(2)}, u32[]{:S(2)}) collective-permute-start(bf16[3,160,256]{2,1,0:T(8,128)(2,1)S(1)} %pad_maximum_fusion.8.refs_0_), channel_id=1, source_target_pairs={{0,8},{4,12},{8,0},{12,4},{1,9},{5,13},{9,1},{13,5},{2,10},{6,14},... | collective-permute-start | bytes 737288 | tf_op jit(solution)/shard_map/ppermute | solution.py:619
  65.7 21.0 %collective-permute-start.14 = (bf16[3,160,256]{2,1,0:T(8,128)(2,1)S(1)}, bf16[3,160,256]{2,1,0:T(8,128)(2,1)S(1)}, u32[]{:S(2)}, u32[]{:S(2)}) collective-permute-start(bf16[3,160,256]{2,1,0:T(8,128)(2,1)S(1)} %pad_maximum_fusion.8.refs_0_), channel_id=1, source_target_pairs={{0,12},{4,0},{8,4},{12,8},{1,13},{5,1},{9,5},{13,9},{2,14},{6,2},{... | collective-permute-start | bytes 737288 | tf_op jit(solution)/shard_map/ppermute | solution.py:619
  90.1 5.5 %collective-permute-start.20 = (bf16[640,512]{1,0:T(8,128)(2,1)}, bf16[640,512]{1,0:T(8,128)(2,1)}, u32[]{:S(2)}, u32[]{:S(2)}) collective-permute-start(bf16[640,512]{1,0:T(8,128)(2,1)} %get-tuple-element.222.qo_c), channel_id=1, source_target_pairs={{0,1},{1,0},{2,3},{3,2},{4,5},{5,4},{6,7},{7,6},{8,9},{9,8},{10,11... | collective-permute-start | bytes 1966088 | tf_op jit(solution)/shard_map/ppermute | solution.py:636
  91.8 4.5 collective-permute-start.21
  93.5 16.7 %collective-permute-start.17 = (bf16[3,640,256]{2,1,0:T(8,128)(2,1)S(1)}, bf16[3,640,256]{2,1,0:T(8,128)(2,1)S(1)}, u32[]{:S(2)}, u32[]{:S(2)}) collective-permute-start(bf16[3,640,256]{2,1,0:T(8,128)(2,1)S(1)} %copy-done.7), channel_id=1, source_target_pairs={{0,1},{1,0},{2,3},{3,2},{4,5},{5,4},{6,7},{7,6},{8,9},{9,8},{10,11... | collective-permute-start | bytes 2949128 | tf_op jit(solution)/shard_map/ppermute | solution.py:636
  94.0 23.6 %collective-permute-start.15 = (bf16[3,640,256]{2,1,0:T(8,128)(2,1)}, bf16[3,640,256]{2,1,0:T(8,128)(2,1)}, u32[]{:S(2)}, u32[]{:S(2)}) collective-permute-start(bf16[3,640,256]{2,1,0:T(8,128)(2,1)} %copy-done.8), channel_id=1, source_target_pairs={{0,16},{16,0},{1,17},{17,1},{2,18},{18,2},{3,19},{19,3},{4,20},{20... | collective-permute-start | bytes 2949128 | tf_op jit(solution)/shard_map/ppermute | solution.py:640
  95.3 23.3 %collective-permute-start.16 = (bf16[3,640,256]{2,1,0:T(8,128)(2,1)}, bf16[3,640,256]{2,1,0:T(8,128)(2,1)}, u32[]{:S(2)}, u32[]{:S(2)}) collective-permute-start(bf16[3,640,256]{2,1,0:T(8,128)(2,1)} %copy-done.8), channel_id=1, source_target_pairs={{0,2},{1,3},{2,0},{3,1},{4,6},{5,7},{6,4},{7,5},{8,10},{9,11},{10,... | collective-permute-start | bytes 2949128 | tf_op jit(solution)/shard_map/ppermute | solution.py:632
  95.6 23.0 %collective-permute-start.18 = (bf16[3,640,256]{2,1,0:T(8,128)(2,1)}, bf16[3,640,256]{2,1,0:T(8,128)(2,1)S(1)}, u32[]{:S(2)}, u32[]{:S(2)}) collective-permute-start(bf16[3,640,256]{2,1,0:T(8,128)(2,1)} %copy-done.68), channel_id=1, source_target_pairs={{0,1},{1,0},{2,3},{3,2},{4,5},{5,4},{6,7},{7,6},{8,9},{9,8},{10,11... | collective-permute-start | bytes 2949128 | tf_op jit(solution)/shard_map/ppermute | solution.py:636
  96.2 22.4 %collective-permute-start.19 = (bf16[3,640,256]{2,1,0:T(8,128)(2,1)}, bf16[3,640,256]{2,1,0:T(8,128)(2,1)S(1)}, u32[]{:S(2)}, u32[]{:S(2)}) collective-permute-start(bf16[3,640,256]{2,1,0:T(8,128)(2,1)} %copy-done.66), channel_id=1, source_target_pairs={{0,1},{1,0},{2,3},{3,2},{4,5},{5,4},{6,7},{7,6},{8,9},{9,8},{10,11... | collective-permute-start | bytes 2949128 | tf_op jit(solution)/shard_map/ppermute | solution.py:636
  118.6 26.4 %collective-permute-start.22 = (bf16[3,640,256]{2,1,0:T(8,128)(2,1)S(1)}, bf16[3,640,256]{2,1,0:T(8,128)(2,1)}, u32[]{:S(2)}, u32[]{:S(2)}) collective-permute-start(bf16[3,640,256]{2,1,0:T(8,128)(2,1)S(1)} %copy-done.67), channel_id=1, source_target_pairs={{0,2},{1,3},{2,0},{3,1},{4,6},{5,7},{6,4},{7,5},{8,10},{9,11},{10,... | collective-permute-start | bytes 2949128 | tf_op jit(solution)/shard_map/ppermute | solution.py:632
  119.3 25.8 %collective-permute-start.23 = (bf16[3,640,256]{2,1,0:T(8,128)(2,1)}, bf16[3,640,256]{2,1,0:T(8,128)(2,1)}, u32[]{:S(2)}, u32[]{:S(2)}) collective-permute-start(bf16[3,640,256]{2,1,0:T(8,128)(2,1)} %collective-permute-done.16.refs_7_), channel_id=1, source_target_pairs={{0,16},{16,0},{1,17},{17,1},{2,18},{18,2},{3,19},{19,3},{4,20},{20... | collective-permute-start | bytes 2949128 | tf_op jit(solution)/shard_map/ppermute | solution.py:640
  120.4 13.8 %collective-permute-start.24 = (bf16[256,512]{1,0:T(8,128)(2,1)S(1)}, bf16[256,512]{1,0:T(8,128)(2,1)S(1)}, u32[]{:S(2)}, u32[]{:S(2)}) collective-permute-start(bf16[256,512]{1,0:T(8,128)(2,1)S(1)} %get-tuple-element.237.refs_0_), channel_id=1, source_target_pairs={{0,4},{4,8},{8,12},{12,0},{1,5},{5,9},{9,13},{13,1},{2,6},{6,10},{... | collective-permute-start | bytes 786440 | tf_op jit(solution)/shard_map/ppermute | solution.py:619
  120.4 23.4 %collective-permute-start.25 = (bf16[256,512]{1,0:T(8,128)(2,1)S(1)}, bf16[256,512]{1,0:T(8,128)(2,1)S(1)}, u32[]{:S(2)}, u32[]{:S(2)}) collective-permute-start(bf16[256,512]{1,0:T(8,128)(2,1)S(1)} %get-tuple-element.237.refs_0_), channel_id=1, source_target_pairs={{0,8},{4,12},{8,0},{12,4},{1,9},{5,13},{9,1},{13,5},{2,10},{6,14},... | collective-permute-start | bytes 786440 | tf_op jit(solution)/shard_map/ppermute | solution.py:619
  122.1 21.7 %collective-permute-start.26 = (bf16[256,512]{1,0:T(8,128)(2,1)S(1)}, bf16[256,512]{1,0:T(8,128)(2,1)S(1)}, u32[]{:S(2)}, u32[]{:S(2)}) collective-permute-start(bf16[256,512]{1,0:T(8,128)(2,1)S(1)} %get-tuple-element.237.refs_0_), channel_id=1, source_target_pairs={{0,12},{4,0},{8,4},{12,8},{1,13},{5,1},{9,5},{13,9},{2,14},{6,2},{... | collective-permute-start | bytes 786440 | tf_op jit(solution)/shard_map/ppermute | solution.py:619
  145.0 3.7 collective-permute-start.32
  147.6 4.3 collective-permute-start.28
  148.0 5.3 %collective-permute-start.29 = (bf16[3,640,256]{2,1,0:T(8,128)(2,1)}, bf16[3,640,256]{2,1,0:T(8,128)(2,1)}, u32[]{:S(2)}, u32[]{:S(2)}) collective-permute-start(bf16[3,640,256]{2,1,0:T(8,128)(2,1)} %collective-permute-done.15.refs_13_), channel_id=1, source_target_pairs={{0,1},{1,0},{2,3},{3,2},{4,5},{5,4},{6,7},{7,6},{8,9},{9,8},{10,11... | collective-permute-start | bytes 2949128 | tf_op jit(solution)/shard_map/ppermute | solution.py:636
  148.1 6.6 %collective-permute-start.30 = (bf16[3,640,256]{2,1,0:T(8,128)(2,1)}, bf16[3,640,256]{2,1,0:T(8,128)(2,1)}, u32[]{:S(2)}, u32[]{:S(2)}) collective-permute-start(bf16[3,640,256]{2,1,0:T(8,128)(2,1)} %collective-permute-done.22.refs_14_), channel_id=1, source_target_pairs={{0,1},{1,0},{2,3},{3,2},{4,5},{5,4},{6,7},{7,6},{8,9},{9,8},{10,11... | collective-permute-start | bytes 2949128 | tf_op jit(solution)/shard_map/ppermute | solution.py:636
  148.7 7.4 %collective-permute-start.31 = (bf16[3,640,256]{2,1,0:T(8,128)(2,1)}, bf16[3,640,256]{2,1,0:T(8,128)(2,1)}, u32[]{:S(2)}, u32[]{:S(2)}) collective-permute-start(bf16[3,640,256]{2,1,0:T(8,128)(2,1)} %collective-permute-done.23.refs_15_), channel_id=1, source_target_pairs={{0,1},{1,0},{2,3},{3,2},{4,5},{5,4},{6,7},{7,6},{8,9},{9,8},{10,11... | collective-permute-start | bytes 2949128 | tf_op jit(solution)/shard_map/ppermute | solution.py:636
  156.1 16.3 %collective-permute-start.33 = (bf16[640,512]{1,0:T(8,128)(2,1)}, bf16[640,512]{1,0:T(8,128)(2,1)}, u32[]{:S(2)}, u32[]{:S(2)}) collective-permute-start(bf16[640,512]{1,0:T(8,128)(2,1)} %get-tuple-element.268.qo_c), channel_id=1, source_target_pairs={{0,2},{1,3},{2,0},{3,1},{4,6},{5,7},{6,4},{7,5},{8,10},{9,11},{10,... | collective-permute-start | bytes 1966088 | tf_op jit(solution)/shard_map/ppermute | solution.py:632
  156.8 20.4 %collective-permute-start.35 = (bf16[640,512]{1,0:T(8,128)(2,1)}, bf16[640,512]{1,0:T(8,128)(2,1)}, u32[]{:S(2)}, u32[]{:S(2)}) collective-permute-start(bf16[640,512]{1,0:T(8,128)(2,1)} %get-tuple-element.268.qo_c), channel_id=1, source_target_pairs={{0,1},{1,0},{2,3},{3,2},{4,5},{5,4},{6,7},{7,6},{8,9},{9,8},{10,11... | collective-permute-start | bytes 1966088 | tf_op jit(solution)/shard_map/ppermute | solution.py:636
  172.4 9.8 %collective-permute-start.36 = (bf16[640,512]{1,0:T(8,128)(2,1)}, bf16[640,512]{1,0:T(8,128)(2,1)}, u32[]{:S(2)}, u32[]{:S(2)}) collective-permute-start(bf16[640,512]{1,0:T(8,128)(2,1)} %collective-permute-done.33.qo_d), channel_id=1, source_target_pairs={{0,1},{1,0},{2,3},{3,2},{4,5},{5,4},{6,7},{7,6},{8,9},{9,8},{10,11... | collective-permute-start | bytes 1966088 | tf_op jit(solution)/shard_map/ppermute | solution.py:636
  173.6 8.6 %collective-permute-start.34 = (bf16[512,512]{1,0:T(8,128)(2,1)S(1)}, bf16[512,512]{1,0:T(8,128)(2,1)S(1)}, u32[]{:S(2)}, u32[]{:S(2)}) collective-permute-start(bf16[512,512]{1,0:T(8,128)(2,1)S(1)} %get-tuple-element.261.own), channel_id=1, source_target_pairs={{0,1},{1,2},{2,3},{4,5},{5,6},{6,7},{8,9},{9,10},{10,11},{12,13},{... | collective-permute-start | bytes 1572872 | tf_op jit(solution)/shard_map/ppermute | solution.py:500
  206.1 24.1 %collective-permute-start.37 = (bf16[512,640]{1,0:T(8,128)(2,1)S(1)}, bf16[512,640]{1,0:T(8,128)(2,1)S(1)}, u32[]{:S(2)}, u32[]{:S(2)}) collective-permute-start(bf16[512,640]{1,0:T(8,128)(2,1)S(1)} %broadcast_select_fusion.4), channel_id=1, source_target_pairs={{0,16},{16,0},{1,17},{17,1},{2,18},{18,2},{3,19},{19,3},{4,20},{20... | collective-permute-start | bytes 1966088 | tf_op jit(solution)/shard_map/ppermute | solution.py:640
  230.2 16.3 %collective-permute-start.38 = (bf16[2,2,3,640,256]{4,3,2,1,0:T(8,128)(2,1)}, bf16[2,2,3,640,256]{4,3,2,1,0:T(8,128)(2,1)}, u32[]{:S(2)}, u32[]{:S(2)}) collective-permute-start(bf16[2,2,3,640,256]{4,3,2,1,0:T(8,128)(2,1)} %get-tuple-element.295), channel_id=1, source_target_pairs={{0,1},{1,0},{2,3},{3,2},{4,5},{5,4},{6,7},{7,6},{8,9},{9,8},{10,11... | collective-permute-start | bytes 11796488 | tf_op jit(solution)/shard_map/ppermute | solution.py:636
  246.5 11.5 %collective-permute-start.39 = (bf16[512,512]{1,0:T(8,128)(2,1)S(1)}, bf16[512,512]{1,0:T(8,128)(2,1)S(1)}, u32[]{:S(2)}, u32[]{:S(2)}) collective-permute-start(bf16[512,512]{1,0:T(8,128)(2,1)S(1)} %get-tuple-element.296), channel_id=1, source_target_pairs={{1,0},{2,1},{3,2},{5,4},{6,5},{7,6},{9,8},{10,9},{11,10},{13,12},{... | collective-permute-start | bytes 1572872 | tf_op jit(solution)/shard_map/ppermute | solution.py:600
  248.7 38.6 %collective-permute-start.41 = (bf16[2,640,512]{2,1,0:T(8,128)(2,1)}, bf16[2,640,512]{2,1,0:T(8,128)(2,1)}, u32[]{:S(2)}, u32[]{:S(2)}) collective-permute-start(bf16[2,640,512]{2,1,0:T(8,128)(2,1)} %get-tuple-element.318), channel_id=1, source_target_pairs={{0,1},{1,0},{2,3},{3,2},{4,5},{5,4},{6,7},{7,6},{8,9},{9,8},{10,11... | collective-permute-start | bytes 3932168 | tf_op jit(solution)/shard_map/ppermute | solution.py:636
  258.1 29.2 %collective-permute-start.40 = (bf16[3,640,256]{2,1,0:T(8,128)(2,1)S(1)}, bf16[3,640,256]{2,1,0:T(8,128)(2,1)}, u32[]{:S(2)}, u32[]{:S(2)}) collective-permute-start(bf16[3,640,256]{2,1,0:T(8,128)(2,1)S(1)} %get-tuple-element.299), channel_id=1, source_target_pairs={{0,2},{1,3},{2,0},{3,1},{4,6},{5,7},{6,4},{7,5},{8,10},{9,11},{10,... | collective-permute-start | bytes 2949128 | tf_op jit(solution)/shard_map/ppermute | solution.py:632
  287.3 26.2 %collective-permute-start.42 = (bf16[2,2,3,640,256]{4,3,2,1,0:T(8,128)(2,1)}, bf16[2,2,3,640,256]{4,3,2,1,0:T(8,128)(2,1)}, u32[]{:S(2)}, u32[]{:S(2)}) collective-permute-start(bf16[2,2,3,640,256]{4,3,2,1,0:T(8,128)(2,1)} %get-tuple-element.330), channel_id=1, source_target_pairs={{0,1},{1,0},{2,3},{3,2},{4,5},{5,4},{6,7},{7,6},{8,9},{9,8},{10,11... | collective-permute-start | bytes 11796488 | tf_op jit(solution)/shard_map/ppermute | solution.py:636
  287.7 25.7 %collective-permute-start.43 = (bf16[3,640,256]{2,1,0:T(8,128)(2,1)}, bf16[3,640,256]{2,1,0:T(8,128)(2,1)S(1)}, u32[]{:S(2)}, u32[]{:S(2)}) collective-permute-start(bf16[3,640,256]{2,1,0:T(8,128)(2,1)} %get-tuple-element.331), channel_id=1, source_target_pairs={{0,2},{1,3},{2,0},{3,1},{4,6},{5,7},{6,4},{7,5},{8,10},{9,11},{10,... | collective-permute-start | bytes 2949128 | tf_op jit(solution)/shard_map/ppermute | solution.py:632
  313.5 10.6 %collective-permute-start.44 = (bf16[512,512]{1,0:T(8,128)(2,1)S(1)}, bf16[512,512]{1,0:T(8,128)(2,1)S(1)}, u32[]{:S(2)}, u32[]{:S(2)}) collective-permute-start(bf16[512,512]{1,0:T(8,128)(2,1)S(1)} %get-tuple-element.336), channel_id=1, source_target_pairs={{1,0},{2,1},{3,2},{5,4},{6,5},{7,6},{9,8},{10,9},{11,10},{13,12},{... | collective-permute-start | bytes 1572872 | tf_op jit(solution)/shard_map/ppermute | solution.py:600
  316.3 21.0 %collective-permute-start.48 = (bf16[2,640,512]{2,1,0:T(8,128)(2,1)}, bf16[2,640,512]{2,1,0:T(8,128)(2,1)}, u32[]{:S(2)}, u32[]{:S(2)}) collective-permute-start(bf16[2,640,512]{2,1,0:T(8,128)(2,1)} %get-tuple-element.354), channel_id=1, source_target_pairs={{0,1},{1,0},{2,3},{3,2},{4,5},{5,4},{6,7},{7,6},{8,9},{9,8},{10,11... | collective-permute-start | bytes 3932168 | tf_op jit(solution)/shard_map/ppermute | solution.py:636
  317.4 17.7 %collective-permute-start.47 = (bf16[1,352,512]{2,1,0:T(8,128)(2,1)}, bf16[1,352,512]{2,1,0:T(8,128)(2,1)}, u32[]{:S(2)}, u32[]{:S(2)}) collective-permute-start(bf16[1,352,512]{2,1,0:T(8,128)(2,1)} %bitcast.59), channel_id=1, source_target_pairs={{0,1},{1,0},{2,3},{3,2},{4,5},{5,4},{6,7},{7,6},{8,9},{9,8},{10,11... | collective-permute-start | bytes 1081352 | tf_op jit(solution)/shard_map/ppermute | solution.py:636
  329.5 7.6 %collective-permute-start.46 = (bf16[1,352,512]{2,1,0:T(8,128)(2,1)S(1)}, bf16[1,352,512]{2,1,0:T(8,128)(2,1)S(1)}, u32[]{:S(2)}, u32[]{:S(2)}) collective-permute-start(bf16[1,352,512]{2,1,0:T(8,128)(2,1)S(1)} %bitcast.227), channel_id=1, source_target_pairs={{0,1},{1,0},{2,3},{3,2},{4,5},{5,4},{6,7},{7,6},{8,9},{9,8},{10,11... | collective-permute-start | bytes 1081352 | tf_op jit(solution)/shard_map/ppermute | solution.py:636
  334.8 22.8 %collective-permute-start.45 = (bf16[3,640,256]{2,1,0:T(8,128)(2,1)S(1)}, bf16[3,640,256]{2,1,0:T(8,128)(2,1)S(1)}, u32[]{:S(2)}, u32[]{:S(2)}) collective-permute-start(bf16[3,640,256]{2,1,0:T(8,128)(2,1)S(1)} %get-tuple-element.393), channel_id=1, source_target_pairs={{0,2},{1,3},{2,0},{3,1},{4,6},{5,7},{6,4},{7,5},{8,10},{9,11},{10,... | collective-permute-start | bytes 2949128 | tf_op jit(solution)/shard_map/ppermute | solution.py:632
  334.9 15.9 %collective-permute-start.49 = (bf16[512,640]{1,0:T(8,128)(2,1)S(1)}, bf16[512,640]{1,0:T(8,128)(2,1)S(1)}, u32[]{:S(2)}, u32[]{:S(2)}) collective-permute-start(bf16[512,640]{1,0:T(8,128)(2,1)S(1)} %broadcast_select_fusion.3), channel_id=1, source_target_pairs={{0,16},{16,0},{1,17},{17,1},{2,18},{18,2},{3,19},{19,3},{4,20},{20... | collective-permute-start | bytes 1966088 | tf_op jit(solution)/shard_map/ppermute | solution.py:640
  359.0 22.2 %collective-permute-start.51 = (bf16[3,640,256]{2,1,0:T(8,128)(2,1)}, bf16[3,640,256]{2,1,0:T(8,128)(2,1)}, u32[]{:S(2)}, u32[]{:S(2)}) collective-permute-start(bf16[3,640,256]{2,1,0:T(8,128)(2,1)} %broadcast_select_fusion.2), channel_id=1, source_target_pairs={{0,16},{16,0},{1,17},{17,1},{2,18},{18,2},{3,19},{19,3},{4,20},{20... | collective-permute-start | bytes 2949128 | tf_op jit(solution)/shard_map/ppermute | solution.py:640
  359.1 23.9 %collective-permute-start.50 = (bf16[3,640,256]{2,1,0:T(8,128)(2,1)}, bf16[3,640,256]{2,1,0:T(8,128)(2,1)}, u32[]{:S(2)}, u32[]{:S(2)}) collective-permute-start(bf16[3,640,256]{2,1,0:T(8,128)(2,1)} %get-tuple-element.363), channel_id=1, source_target_pairs={{0,2},{1,3},{2,0},{3,1},{4,6},{5,7},{6,4},{7,5},{8,10},{9,11},{10,... | collective-permute-start | bytes 2949128 | tf_op jit(solution)/shard_map/ppermute | solution.py:632
  359.5 35.6 %collective-permute-start.60 = (bf16[640,512]{1,0:T(8,128)(2,1)}, bf16[640,512]{1,0:T(8,128)(2,1)S(1)}, u32[]{:S(2)}, u32[]{:S(2)}) collective-permute-start(bf16[640,512]{1,0:T(8,128)(2,1)} %get-tuple-element.381), channel_id=1, source_target_pairs={{0,2},{1,3},{2,0},{3,1},{4,6},{5,7},{6,4},{7,5},{8,10},{9,11},{10,... | collective-permute-start | bytes 1966088 | tf_op jit(solution)/shard_map/ppermute | solution.py:632
  384.8 20.5 %collective-permute-start.56 = (bf16[3,640,256]{2,1,0:T(8,128)(2,1)S(1)}, bf16[3,640,256]{2,1,0:T(8,128)(2,1)S(1)}, u32[]{:S(2)}, u32[]{:S(2)}) collective-permute-start(bf16[3,640,256]{2,1,0:T(8,128)(2,1)S(1)} %broadcast_select_fusion.1), channel_id=1, source_target_pairs={{0,16},{16,0},{1,17},{17,1},{2,18},{18,2},{3,19},{19,3},{4,20},{20... | collective-permute-start | bytes 2949128 | tf_op jit(solution)/shard_map/ppermute | solution.py:640
  385.0 39.5 %collective-permute-start.52 = (bf16[1344,512]{1,0:T(8,128)(2,1)S(1)}, bf16[1344,512]{1,0:T(8,128)(2,1)S(1)}, u32[]{:S(2)}, u32[]{:S(2)}) collective-permute-start(bf16[1344,512]{1,0:T(8,128)(2,1)S(1)} %pad_maximum_fusion), channel_id=1, source_target_pairs={{0,2},{1,3},{2,0},{3,1},{4,6},{5,7},{6,4},{7,5},{8,10},{9,11},{10,... | collective-permute-start | bytes 4128776 | tf_op jit(solution)/shard_map/ppermute | solution.py:632
  386.0 9.3 %collective-permute-start.53 = (bf16[480,256]{1,0:T(8,128)(2,1)S(1)}, bf16[480,256]{1,0:T(8,128)(2,1)S(1)}, u32[]{:S(2)}, u32[]{:S(2)}) collective-permute-start(bf16[480,256]{1,0:T(8,128)(2,1)S(1)} %bitcast.241), channel_id=1, source_target_pairs={{0,4},{4,8},{8,12},{12,0},{1,5},{5,9},{9,13},{13,1},{2,6},{6,10},{... | collective-permute-start | bytes 737288 | tf_op jit(solution)/shard_map/ppermute | solution.py:669
  386.9 15.9 %collective-permute-start.54 = (bf16[480,256]{1,0:T(8,128)(2,1)S(1)}, bf16[480,256]{1,0:T(8,128)(2,1)S(1)}, u32[]{:S(2)}, u32[]{:S(2)}) collective-permute-start(bf16[480,256]{1,0:T(8,128)(2,1)S(1)} %bitcast.240), channel_id=1, source_target_pairs={{0,8},{4,12},{8,0},{12,4},{1,9},{5,13},{9,1},{13,5},{2,10},{6,14},... | collective-permute-start | bytes 737288 | tf_op jit(solution)/shard_map/ppermute | solution.py:669
  395.0 7.8 %collective-permute-start.55 = (bf16[480,256]{1,0:T(8,128)(2,1)S(1)}, bf16[480,256]{1,0:T(8,128)(2,1)S(1)}, u32[]{:S(2)}, u32[]{:S(2)}) collective-permute-start(bf16[480,256]{1,0:T(8,128)(2,1)S(1)} %bitcast.238), channel_id=1, source_target_pairs={{0,12},{4,0},{8,4},{12,8},{1,13},{5,1},{9,5},{13,9},{2,14},{6,2},{... | collective-permute-start | bytes 737288 | tf_op jit(solution)/shard_map/ppermute | solution.py:669
  425.1 23.7 %collective-permute-start.61 = (bf16[992,512]{1,0:T(8,128)(2,1)S(1)}, bf16[992,512]{1,0:T(8,128)(2,1)S(1)}, u32[]{:S(2)}, u32[]{:S(2)}) collective-permute-start(bf16[992,512]{1,0:T(8,128)(2,1)S(1)} %broadcast_select_fusion), channel_id=1, source_target_pairs={{0,16},{16,0},{1,17},{17,1},{2,18},{18,2},{3,19},{19,3},{4,20},{20... | collective-permute-start | bytes 3047432 | tf_op jit(solution)/shard_map/ppermute | solution.py:640
  428.3 5.7 %collective-permute-start.57 = (bf16[480,256]{1,0:T(8,128)(2,1)S(1)}, bf16[480,256]{1,0:T(8,128)(2,1)S(1)}, u32[]{:S(2)}, u32[]{:S(2)}) collective-permute-start(bf16[480,256]{1,0:T(8,128)(2,1)S(1)} %bitcast.239), channel_id=1, source_target_pairs={{0,4},{4,8},{8,12},{12,0},{1,5},{5,9},{9,13},{13,1},{2,6},{6,10},{... | collective-permute-start | bytes 737288 | tf_op jit(solution)/shard_map/ppermute | solution.py:669
  429.2 19.4 %collective-permute-start.58 = (bf16[480,256]{1,0:T(8,128)(2,1)S(1)}, bf16[480,256]{1,0:T(8,128)(2,1)S(1)}, u32[]{:S(2)}, u32[]{:S(2)}) collective-permute-start(bf16[480,256]{1,0:T(8,128)(2,1)S(1)} %bitcast.237), channel_id=1, source_target_pairs={{0,8},{4,12},{8,0},{12,4},{1,9},{5,13},{9,1},{13,5},{2,10},{6,14},... | collective-permute-start | bytes 737288 | tf_op jit(solution)/shard_map/ppermute | solution.py:669
  429.2 19.4 %collective-permute-start.59 = (bf16[480,256]{1,0:T(8,128)(2,1)S(1)}, bf16[480,256]{1,0:T(8,128)(2,1)S(1)}, u32[]{:S(2)}, u32[]{:S(2)}) collective-permute-start(bf16[480,256]{1,0:T(8,128)(2,1)S(1)} %bitcast.236), channel_id=1, source_target_pairs={{0,12},{4,0},{8,4},{12,8},{1,13},{5,1},{9,5},{13,9},{2,14},{6,2},{... | collective-permute-start | bytes 737288 | tf_op jit(solution)/shard_map/ppermute | solution.py:669
  449.7 8.2 %collective-permute-start.62 = (bf16[496,256]{1,0:T(8,128)(2,1)S(1)}, bf16[496,256]{1,0:T(8,128)(2,1)S(1)}, u32[]{:S(2)}, u32[]{:S(2)}) collective-permute-start(bf16[496,256]{1,0:T(8,128)(2,1)S(1)} %pad_maximum_fusion.4), channel_id=1, source_target_pairs={{0,4},{4,8},{8,12},{12,0},{1,5},{5,9},{9,13},{13,1},{2,6},{6,10},{... | collective-permute-start | bytes 761864 | tf_op jit(solution)/shard_map/ppermute | solution.py:669
  449.8 25.6 %collective-permute-start.63 = (bf16[496,256]{1,0:T(8,128)(2,1)S(1)}, bf16[496,256]{1,0:T(8,128)(2,1)S(1)}, u32[]{:S(2)}, u32[]{:S(2)}) collective-permute-start(bf16[496,256]{1,0:T(8,128)(2,1)S(1)} %pad_maximum_fusion.5), channel_id=1, source_target_pairs={{0,8},{4,12},{8,0},{12,4},{1,9},{5,13},{9,1},{13,5},{2,10},{6,14},... | collective-permute-start | bytes 761864 | tf_op jit(solution)/shard_map/ppermute | solution.py:669
  453.9 21.5 %collective-permute-start.64 = (bf16[496,256]{1,0:T(8,128)(2,1)S(1)}, bf16[496,256]{1,0:T(8,128)(2,1)S(1)}, u32[]{:S(2)}, u32[]{:S(2)}) collective-permute-start(bf16[496,256]{1,0:T(8,128)(2,1)S(1)} %pad_maximum_fusion.6), channel_id=1, source_target_pairs={{0,12},{4,0},{8,4},{12,8},{1,13},{5,1},{9,5},{13,9},{2,14},{6,2},{... | collective-permute-start | bytes 761864 | tf_op jit(solution)/shard_map/ppermute | solution.py:669
  (73 other events, 848.2 us)
